TPU v7x, 32 devices: a whole 2x2x4 slice. The times are simulated.
32 devices in a mesh: order: 8 (over z, x), lat: 4 (over y, core).
Axes of the slice: x: 2, y: 2, z: 4, core: 2. Of those that a mesh axis runs over, the one named last changes fastest.
Arguments:
- position: float32 [16, 2, 64, 2160], P('order', None, None, 'lat'), may hold values from -6 to 6
- residual: float32 [16, 2, 64, 2160], P('order', None, None, 'lat'), as said below
- direction: float32 [16, 2, 64, 2160], P('order', None, None, 'lat'), as said below
- legendre: float32 [16, 2160, 256], P('order', None, 'lat'), may hold values from -0.125 to 0.125
- order_of: int32 [16], replicated, may hold values from 0 to 2025, as said below
- class_idx: int32 [256, 4320], P(('lat', 'order')), may hold values from 0 to 15
- land: int32 [256, 4320], P(('lat', 'order')), may hold values 0 or 1
- class_weight: float32 [16, 2], replicated, may hold values from 0.2 to 5
- damping: float32 [2160], P('lat'), may hold values from 0.05 to 0.5
Outputs:
- new_position: float32 [16, 2, 64, 2160], P('order', None, None, 'lat')
- new_residual: float32 [16, 2, 64, 2160], P('order', None, None, 'lat')
- new_direction: float32 [16, 2, 64, 2160], P('order', None, None, 'lat')
Inputs may be any that keep to these rules, and one draw needn't show every extreme that they name: `order_of`: distinct multiples of 135: each of 0, 135, ..., 135 * (16 - 1) appears exactly once. `residual`: real-valued and not zero. `direction`: real-valued and not zero.
All inputs are finite; a program needn't handle non-finite values. No bound on the sum of `land` on one device may be relied on, other than what follows from the above.
Results may differ from a plain program's by a relative error of at most 0.000058.
Values sent between devices are 32-bit elements; how exact they have to be, the bound alone decides.
No kernel may reach another device: no remote copies, remote signals or barrier semaphores. Data moves between devices by JAX's collectives and lax.ppermute only.
A program may use at most 128 MiB of HBM per device.

v0:
```python
import math

import jax
import jax.numpy as jnp
from jax import lax
from jax.sharding import PartitionSpec as P


def tables(order_of, longitudes):
    longitude = jnp.arange(longitudes, dtype=jnp.int32)
    phases = order_of[:, None] * longitude[None, :] % longitudes
    angles = phases.astype(jnp.float32) * (2.0 * math.pi / longitudes)
    return jnp.stack([jnp.cos(angles), jnp.sin(angles)])


def sample_sums(product):
    return jnp.sum(product, axis=(0, 1, 3))


def shards(
    position, residual, direction, legendre, order_of, class_idx, land, class_weight, damping
):
    highest = lax.Precision.HIGHEST
    m_local = position.shape[0]
    samples = position.shape[2]
    deg_local = position.shape[3]
    band_rows = legendre.shape[2]
    lat_index = lax.axis_index("lat")
    order_index = lax.axis_index("order")
    my_orders = lax.dynamic_slice_in_dim(order_of, order_index * m_local, m_local)
    deg_start = lat_index * deg_local
    own_degrees = deg_start + jnp.arange(deg_local, dtype=jnp.int32)
    own_valid = (own_degrees[None, :] >= my_orders[:, None]).astype(jnp.float32)[:, None, None, :]
    pos_m = position * own_valid
    res_m = residual * own_valid
    dir_m = direction * own_valid
    block_part = lax.all_gather(direction, "lat", axis=3, tiled=True)
    degree_count = block_part.shape[3]
    in_block = jnp.arange(degree_count, dtype=jnp.int32)
    in_triangle = (in_block[None, :] >= my_orders[:, None]).astype(jnp.float32)
    masked = block_part * in_triangle[:, None, None, :]
    synthesis = jnp.einsum("mskd,mdt->mtsk", masked, legendre, precision=highest)
    grid_in = lax.all_to_all(
        synthesis.reshape(m_local, band_rows, 2 * samples),
        "order",
        split_axis=1,
        concat_axis=0,
        tiled=True,
    )
    orders_all = grid_in.shape[0]
    rows_here = grid_in.shape[1]
    grid_in = grid_in.reshape(orders_all, rows_here, 2, samples)
    longitudes = class_idx.shape[1]
    harmonic = tables(order_of, longitudes)
    surface = jnp.einsum("mrsk,sml->rkl", grid_in, harmonic, precision=highest)
    class_count = class_weight.shape[0]
    onehot = (
        class_idx[:, :, None] == jnp.arange(class_count, dtype=jnp.int32)[None, None, :]
    ).astype(jnp.float32)
    by_class = jnp.dot(onehot, class_weight, precision=highest)
    weight_grid = jnp.where(land == 1, by_class[:, :, 1], by_class[:, :, 0])
    weighted = surface * weight_grid[:, None, :]
    spectra = jnp.einsum("rkl,sml->mrsk", weighted, harmonic, precision=highest) * (
        2.0 / longitudes
    )
    returned = lax.all_to_all(
        spectra.reshape(orders_all, rows_here, 2 * samples),
        "order",
        split_axis=0,
        concat_axis=1,
        tiled=True,
    )
    returned = returned.reshape(m_local, band_rows, 2, samples)
    band_part = jnp.einsum("mtsk,mdt->mskd", returned, legendre, precision=highest)
    totals = lax.psum(band_part, "lat")
    summed = lax.dynamic_slice_in_dim(totals, deg_start, deg_local, 3)
    applied = (summed + damping[None, None, None, :] * dir_m) * own_valid
    norm_before, curvature_sum, cross_sum, square_sum = lax.psum(
        (
            sample_sums(res_m * res_m),
            sample_sums(dir_m * applied),
            sample_sums(res_m * applied),
            sample_sums(applied * applied),
        ),
        ("order", "lat"),
    )
    step_flat = norm_before / curvature_sum
    step_size = step_flat[None, None, :, None]
    new_residual = res_m - step_size * applied
    norm_after = norm_before - 2.0 * step_flat * cross_sum + step_flat * step_flat * square_sum
    ratio_new = (norm_after / norm_before)[None, None, :, None]
    new_position = pos_m + step_size * dir_m
    new_direction = new_residual + ratio_new * dir_m
    return (new_position, new_residual, new_direction)


def solution(mesh):
    return jax.shard_map(
        shards,
        mesh=mesh,
        in_specs=(
            P("order", None, None, "lat"),
            P("order", None, None, "lat"),
            P("order", None, None, "lat"),
            P("order", None, "lat"),
            P(),
            P(("lat", "order"), None),
            P(("lat", "order"), None),
            P(),
            P("lat"),
        ),
        out_specs=(
            P("order", None, None, "lat"),
            P("order", None, None, "lat"),
            P("order", None, None, "lat"),
        ),
        check_vma=False,
    )
```

profile of v0, /device:TPU:0, one launch (start us, length us, event | category | flops | bytes accessed | tf_op | source)
XLA Modules:
  0.0 208.7 jit_solution(18183975104363505204)
XLA Ops:
  7.2 0.0 copy-start
  7.2 0.0 copy-start.5
  7.2 0.0 copy-start.6
  7.2 0.0 copy-start.7
  7.2 0.0 all-gather.2.cloned.1.call-start
  7.3 2.4 %copy.19 = f32[2,2,64,540]{2,1,0,3:T(2,128)} copy(f32[2,2,64,540]{3,2,1,0:T(8,128)} %param.11) | data formatting | bytes 1105920 | tf_op args[2]
  9.7 0.0 all-gather.2.cloned.1.call-update
  9.7 0.0 copy-done.5
  9.7 0.1 dynamic_slice.6
  9.8 0.0 copy-done.6
  9.8 0.0 copy-done.7
  9.8 0.7 fusion.5
  10.5 0.1 fusion.16
  10.7 0.2 fusion.33
  10.9 1.2 fusion.25
  12.1 36.3 %all-gather.2.cloned.1.call-done = f32[2,2,64,2160]{2,1,0,3:T(2,128)} async-done(((f32[2,2,64,540]{2,1,0,3:T(2,128)}), f32[2,2,64,2160]{2,1,0,3:T(2,128)}) %all-gather.2.cloned.1.call-update) | async-done | bytes 2211856 | tf_op jit(solution)/shard_map/all_gather | solution.py:37
  48.3 6.4 %broadcast_multiply_fusion = f32[2,2,64,2160]{2,1,0,3:T(2,128)S(1)} fusion(f32[2,2,64,2160]{2,1,0,3:T(2,128)} %all-gather.2.cloned.1.call-done, f32[2,2160]{0,1:T(8,128)S(1)} %fusion.16), kind=kLoop, calls=%fused_computation.8 | loop fusion | flops 552960 | bytes 4440960 | tf_op jit(solution)/shard_map/mul | solution.py:41
  54.8 0.0 copy-done
  54.8 0.0 copy-start.3
  54.8 7.2 %fusion.3 = f32[2,2,64,64]{3,2,1,0:T(8,128)S(1)} fusion(f32[2,2,64,2160]{2,1,0,3:T(2,128)S(1)} %broadcast_multiply_fusion, f32[2,2160,64]{1,2,0:T(8,128)S(1)} %copy-done), kind=kOutput, calls=%fused_computation.4 | convolution fusion | flops 424673280 | bytes 3383296 | tf_op jit(solution)/shard_map/mskd,mdt->mtsk/dot_general | solution.py:42
  61.9 0.7 copy.21
  62.7 5.5 %all-to-all-start = ((f32[2,64,128]{2,0,1:T(2,128)}), f32[2,64,128]{2,0,1:T(2,128)S(1)}, u32[]{:S(2)}, u32[]{:S(2)}) async-start(f32[2,64,128]{2,0,1:T(2,128)} %copy.21), calls=%async_computation | async-start | bytes 131072 | tf_op jit(solution)/shard_map/all_to_all | solution.py:43
  68.2 0.2 all-reduce.3.cloned.1.call-start
  68.4 0.0 copy-done.3
  68.4 6.6 %all-to-all-done = f32[2,64,128]{2,0,1:T(2,128)S(1)} async-done(((f32[2,64,128]{2,0,1:T(2,128)}), f32[2,64,128]{2,0,1:T(2,128)S(1)}, u32[]{:S(2)}, u32[]{:S(2)}) %all-to-all-start) | async-done | bytes 65568 | tf_op jit(solution)/shard_map/all_to_all | solution.py:43
  75.1 0.1 reshape.148
  75.2 7.3 %fusion.18 = f32[8,64,4320,1]{2,1,3,0:T(8,128)S(1)} fusion(f32[1,16,4320]{2,1,0:T(8,128)S(1)} %get-tuple-element.20, f32[1,16,4320]{2,1,0:T(8,128)S(1)} %get-tuple-element.19, f32[16,8,2,64]{3,2,1,0:T(2,128)S(1)} %reshape.148), kind=kOutput, calls=%fused_computation.27 | convolution fusion | flops 849484800 | bytes 9465856 | tf_op jit(solution)/shard_map/mrsk,sml->rkl/dot_general | solution.py:55
  82.6 12.4 %fusion.9 = f32[16,8,2,64]{3,0,1,2:T(8,128)S(1)} fusion(f32[8,64,4320,1]{2,1,3,0:T(8,128)S(1)} %fusion.18, f32[8,4320]{1,0:T(8,128)S(1)} %fusion.27, f32[1,16,4320]{2,1,0:T(8,128)S(1)} %get-tuple-element.20, f32[1,16,4320]{2,1,0:T(8,128)S(1)} %get-tuple-element.19), kind=kOutput, calls=%fused_computation.10 | convolution fusion | flops 851713024 | bytes 9604096 | tf_op jit(solution)/shard_map/rkl,sml->mrsk/dot_general | solution.py:63
  94.9 0.1 copy.26
  95.0 0.1 reshape.149
  95.2 9.3 %all_to_all.30 = f32[16,8,128]{2,1,0:T(8,128)S(1)} all-to-all(f32[16,8,128]{2,1,0:T(8,128)S(1)} %reshape.149), channel_id=1, replica_groups=mesh['order'=8,'lat'=4] {'order'}, dimensions={0} | all-to-all | bytes 131072 | tf_op jit(solution)/shard_map/all_to_all | solution.py:66
  104.5 0.1 reshape.150
  104.6 0.0 copy-start.1
  104.6 0.0 copy-start.2
  104.6 0.0 copy-start.4
  104.6 3.3 %fusion.12 = f32[2,2,64,2160]{3,2,1,0:T(8,128)} fusion(f32[2,2160,64]{1,2,0:T(8,128)S(1)} %copy-done, f32[2,64,2,64]{3,2,1,0:T(2,128)S(1)} %reshape.150), kind=kOutput, calls=%fused_computation.11 | convolution fusion | flops 424673280 | bytes 3383296 | tf_op jit(solution)/shard_map/mtsk,mdt->mskd/dot_general | solution.py:74
  107.9 0.0 all-reduce.3.cloned.1.call-update
  108.0 0.1 compare_convert_fusion
  108.0 50.2 %all-reduce.3.cloned.1.call-done = f32[2,2,64,2160]{3,2,1,0:T(8,128)} async-done(((f32[2,2,64,2160]{3,2,1,0:T(8,128)}), f32[2,2,64,2160]{3,2,1,0:T(8,128)}) %all-reduce.3.cloned.1.call-update) | async-done | bytes 2211856 | tf_op jit(solution)/shard_map/psum | solution.py:75
  158.2 0.0 copy-done.1
  158.2 0.0 copy-done.2
  158.2 0.0 copy-done.4
  158.2 1.6 multiply_reduce_fusion.1
  159.8 39.4 %all-reduce = (f32[64]{0:T(128)S(1)}, f32[64]{0:T(128)S(1)}, f32[64]{0:T(128)S(1)}, f32[64]{0:T(128)S(1)}) all-reduce(f32[64]{0:T(128)S(1)} %get-tuple-element.4, f32[64]{0:T(128)S(1)} %get-tuple-element.5, f32[64]{0:T(128)S(1)} %get-tuple-element.6, f32[64]{0:T(128)S(1)} %get-tuple-element.3), channel_id=1, replica_groups=mesh['order'=8,'lat'=4] {'order','lat'}, use_global_device_ids=true, to_apply=%region_1.2 | all-reduce | flops 256 | bytes 2048 | tf_op jit(solution)/shard_map/psum | solution.py:78
  199.3 2.5 %multiply_add_fusion = (f32[2,2,64,540]{3,2,1,0:T(8,128)}, f32[2,2,64,540]{3,2,1,0:T(8,128)}, f32[2,2,64,540]{3,2,1,0:T(8,128)}) fusion(f32[2,2,64,540]{3,2,1,0:T(8,128)S(1)} %copy-done.1, f32[64]{0:T(128)S(1)} %get-tuple-element.13, f32[2,540]{1,0:T(2,128)S(1)} %compare_convert_fusion, f32[2,2,64,540]{3,2,1,0:T(8,128)S(1)} %get-tuple-element.15, ...), kind=kLoop, calls=%fused_computation.17 | loop fusion | flops 1244160 | bytes 3875552 | tf_op jit(solution)/shard_map/add | solution.py:93
  (6 shorter events, 0.1 us)
Async XLA Ops:
  7.2 47.6 %copy-start = (f32[2,2160,64]{1,2,0:T(8,128)S(1)}, f32[2,2160,64]{1,2,0:T(8,128)}, u32[]{:S(2)}) copy-start(f32[2,2160,64]{1,2,0:T(8,128)} %param.12) | copy-start | bytes 3317764
  7.2 2.5 %copy-start.5 = (s32[16]{0:T(128)S(1)}, s32[16]{0:T(128)}, u32[]{:S(2)}) copy-start(s32[16]{0:T(128)} %param.13) | copy-start | bytes 196
  7.2 2.6 %copy-start.6 = (s32[8,4320]{1,0:T(8,128)S(1)}, s32[8,4320]{1,0:T(8,128)}, u32[]{:S(2)}) copy-start(s32[8,4320]{1,0:T(8,128)} %param.14) | copy-start | bytes 414724
  7.2 2.6 %copy-start.7 = (f32[16,2]{0,1:T(2,128)S(1)}, f32[16,2]{0,1:T(2,128)}, u32[]{:S(2)}) copy-start(f32[16,2]{0,1:T(2,128)} %param.16) | copy-start | bytes 388
  7.2 41.1 %all-gather.2.cloned.1.call-start = ((), (), s32[]{:S(2)}) async-start(), calls=%async_computation.2 | async-start | bytes 5529600 | tf_op jit(solution)/shard_map/all_gather | solution.py:37
  54.8 13.6 %copy-start.3 = (s32[8,4320]{1,0:T(8,128)S(1)}, s32[8,4320]{1,0:T(8,128)}, u32[]{:S(2)}) copy-start(s32[8,4320]{1,0:T(8,128)} %param.15) | copy-start | bytes 414724
  62.7 12.4 %all-to-all-start = ((f32[2,64,128]{2,0,1:T(2,128)}), f32[2,64,128]{2,0,1:T(2,128)S(1)}, u32[]{:S(2)}, u32[]{:S(2)}) async-start(f32[2,64,128]{2,0,1:T(2,128)} %copy.21), calls=%async_computation | async-start | bytes 131072 | tf_op jit(solution)/shard_map/all_to_all | solution.py:43
  68.2 90.0 %all-reduce.3.cloned.1.call-start = ((), (), s32[]{:S(2)}) async-start(), calls=%async_computation.3 | async-start | bytes 4456448 | tf_op jit(solution)/shard_map/psum | solution.py:75
  104.6 53.6 %copy-start.1 = (f32[2,2,64,540]{3,2,1,0:T(8,128)S(1)}, f32[2,2,64,540]{3,2,1,0:T(8,128)}, u32[]{:S(2)}) copy-start(f32[2,2,64,540]{3,2,1,0:T(8,128)} %param.11) | copy-start | bytes 1658884
  104.6 53.6 %copy-start.2 = (f32[2,2,64,540]{3,2,1,0:T(8,128)S(1)}, f32[2,2,64,540]{3,2,1,0:T(8,128)}, u32[]{:S(2)}) copy-start(f32[2,2,64,540]{3,2,1,0:T(8,128)} %param.10) | copy-start | bytes 1658884
  104.6 53.6 %copy-start.4 = (f32[540]{0:T(1024)S(1)}, f32[540]{0:T(1024)}, u32[]{:S(2)}) copy-start(f32[540]{0:T(1024)} %param.17) | copy-start | bytes 6484
Sparse Core Ops, SparseCore 0:
  9.8 38.4 all-gather.1
  108.1 50.0 all-reduce.2
where the time goes:
time: 209 us
  waiting for transfers between devices  93.1 us (45%)
  blocking collectives  48.7 us (23%)
  matrix products  30.9 us (15%)
  between operations  14.2 us (7%)
  other arithmetic  12 us (6%)
  starting transfers between devices  5.77 us (3%)
  local copies, waits for them, and re-layouts  3.97 us (2%)
    psum x1, waiting for transfers between devices, shards(): totals = lax.psum(band_part, 'lat')  50.2 us
    psum x1, blocking collectives, shards(): lax.psum((sample_sums(res_m * res_m), sample_sums(dir_m * applied), sampl...  39.4 us
    all_gather x1, waiting for transfers between devices, shards(): block_part = lax.all_gather(direction, 'lat', axis=3, tiled=True)  36.3 us
    dot_general x1, matrix products, shards(): jnp.einsum('rkl,sml->mrsk', weighted, harmonic, precision=highest)  12.4 us
    all_to_all x1, blocking collectives, shards(): lax.all_to_all(spectra.reshape(orders_all, rows_here, 2 * samples), 'orde...  9.27 us
    dot_general x1, matrix products, shards(): surface = jnp.einsum('mrsk,sml->rkl', grid_in, harmonic, precision=highest)  7.32 us
    dot_general x1, matrix products, shards(): jnp.einsum('mskd,mdt->mtsk', masked, legendre, precision=highest)  7.16 us
    all_to_all x1, waiting for transfers between devices, shards(): lax.all_to_all(synthesis.reshape(m_local, band_rows, 2 * samples), 'order...  6.64 us
  transfers between devices with their start and end apart: 3, of which 3 were waited for; matrix products, arithmetic and copies ran while one was open for 1% of the time, Pallas kernels for 0%

commit v1 on v0

v1 whole, which is shorter than its diff:
```python
import functools
import math

import jax
import jax.numpy as jnp
import numpy as np
from jax import lax
from jax.experimental import pallas as pl
from jax.experimental.pallas import tpu as pltpu
from jax.sharding import Mesh
from jax.sharding import PartitionSpec as P

LANES = 128
HIGHEST = lax.Precision.HIGHEST
VMEM_LIMIT = 48 * 1024 * 1024
WHOLE = pl.BlockSpec(memory_space=pltpu.VMEM)
SCALARS = pl.BlockSpec(memory_space=pltpu.SMEM)
PARAMS = pltpu.CompilerParams(vmem_limit_bytes=VMEM_LIMIT)


def split_bf16(x):
    hi = x.astype(jnp.bfloat16)
    lo = (x - hi.astype(jnp.float32)).astype(jnp.bfloat16)
    return hi, lo


def dot3(a, b, dims):
    (ah, al), (bh, bl) = a, b
    dot = functools.partial(
        lax.dot_general, dimension_numbers=(dims, ((), ())), preferred_element_type=jnp.float32
    )
    return dot(ah, bh) + (dot(ah, bl) + dot(al, bh))


def call(kernel, out_shape, in_specs, flops, moved):
    return pl.pallas_call(
        kernel,
        out_shape=out_shape,
        in_specs=in_specs,
        out_specs=jax.tree.map(lambda _: WHOLE, out_shape),
        compiler_params=PARAMS,
        cost_estimate=pl.CostEstimate(flops=flops, bytes_accessed=moved, transcendentals=0),
    )


def place_direction(geo, scal, *refs):
    parts, (hi_ref, lo_ref) = refs[: geo.inner], refs[geo.inner :]
    m_local, sin_cos, samples, width = parts[0].shape
    window = hi_ref.shape[2]
    rows = sin_cos * samples
    degree = scal[geo.window_start] + lax.broadcasted_iota(jnp.int32, (rows, window), 1)
    for m in range(m_local):
        valid = degree >= scal[geo.orders + m]
        total = None
        for shift, part in enumerate(parts):
            block = part[m].reshape(rows, width)
            block = jnp.concatenate([block, jnp.zeros((rows, window - width), jnp.float32)], axis=1)
            block = pltpu.roll(block, scal[geo.places + shift], 1)
            total = block if total is None else total + block
        total = jnp.where(valid, total, 0.0)
        hi, lo = split_bf16(total)
        hi_ref[m] = hi
        lo_ref[m] = lo


def synthesise_own(leg_ref, hi_ref, lo_ref, out_ref):
    for m in range(leg_ref.shape[0]):
        leg = split_bf16(leg_ref[m])
        out_ref[m] = dot3(leg, (hi_ref[m], lo_ref[m]), ((1,), (1,)))


def synthesise_rest(geo, scal, own_ref, *refs):
    legs, (hi_ref, lo_ref, out_ref) = refs[:-3], refs[-3:]
    rows = out_ref.shape[3]
    for m in range(own_ref.shape[0]):
        for shift in range(geo.outer):
            if shift == 0:
                part = own_ref[m]
            else:
                leg = split_bf16(legs[shift - 1][m])
                part = dot3(leg, (hi_ref[m], lo_ref[m]), ((1,), (1,)))
            a = scal[geo.outer_of + shift]
            for o in range(out_ref.shape[0]):
                out_ref[o, a, m] = part[o * rows : (o + 1) * rows]


def weight_tables(longitudes, period, class_ref, land_ref, value_ref, basis_ref, out_ref):
    classes = class_ref[...]
    on_land = land_ref[...] == 1
    weight = jnp.zeros(classes.shape, jnp.float32)
    for c in range(value_ref.shape[0]):
        value = jnp.where(on_land, value_ref[c, 1], value_ref[c, 0])
        weight = jnp.where(classes == c, value, weight)
    rows = classes.shape[0]
    folded = jnp.zeros((rows, LANES), jnp.float32)
    for start in range(0, longitudes, LANES):
        piece = weight[:, start : min(start + LANES, longitudes)]
        if piece.shape[1] < LANES:
            piece = jnp.concatenate(
                [piece, jnp.zeros((rows, LANES - piece.shape[1]), jnp.float32)], axis=1
            )
        folded = folded + piece
    moments = lax.dot_general(
        folded,
        basis_ref[...],
        (((1,), (0,)), ((), ())),
        precision=HIGHEST,
        preferred_element_type=jnp.float32,
    )
    lane = lax.broadcasted_iota(jnp.int32, (rows, LANES), 1)
    sign = jnp.where(lane < LANES // 2, 1.0, -1.0)
    count = out_ref.shape[1]
    for n in range(count):
        even = jnp.broadcast_to(moments[:, n : n + 1], (rows, LANES))
        odd = jnp.broadcast_to(moments[:, count + n : count + n + 1], (rows, LANES))
        out_ref[0, n] = even
        out_ref[1, n] = sign * even
        out_ref[2, n] = odd
        out_ref[3, n] = sign * odd


def grid_rows(geo, slot, recv_ref, table_ref, out_ref, plain, swapped, done):
    orders = plain.shape[0]
    m_local = recv_ref.shape[1]
    for m in range(orders):
        o, i = divmod(m, m_local)
        total = recv_ref[o * geo.outer, i]
        for a in range(1, geo.outer):
            total = total + recv_ref[o * geo.outer + a, i]
        at = slot[m]
        plain[at] = total
        swapped[at] = pltpu.roll(total, LANES // 2, 1)
    for i in range(orders):
        total = None
        for j in range(orders):
            cos_part = table_ref[0, abs(i - j)] + table_ref[1, i + j]
            if i >= j:
                sin_part = table_ref[2, i + j] - table_ref[3, i - j]
            else:
                sin_part = table_ref[2, i + j] + table_ref[3, j - i]
            term = cos_part * plain[j] + sin_part * swapped[j]
            total = term if total is None else total + term
        done[i] = total
    copies = geo.outer * geo.inner
    for m in range(orders):
        o, i = divmod(m, m_local)
        value = done[slot[m]]
        for c in range(copies):
            out_ref[o * copies + c, i] = value


def split_block(geo, scal, *refs):
    here, (sib_ref, hi_ref, lo_ref) = refs[:-3], refs[-3:]
    width = hi_ref.shape[2]
    start = pl.multiple_of(scal[geo.block_start], LANES)
    for m in range(hi_ref.shape[0]):
        at = 0
        for b in range(geo.inner):
            for a in range(geo.outer):
                if b == 0:
                    block = here[a][m, :, pl.ds(start, width)]
                else:
                    block = sib_ref[b - 1, a, m]
                rows = block.shape[0]
                hi, lo = split_bf16(block)
                hi_ref[m, at : at + rows] = hi
                lo_ref[m, at : at + rows] = lo
                at += rows


def own_mask(geo, scal, m, rows, width):
    degree = scal[geo.own_start] + lax.broadcasted_iota(jnp.int32, (rows, width), 1)
    return degree >= scal[geo.orders + m]


def project(geo, scal, recv_ref, hi_ref, lo_ref, dir_ref, res_ref, damp_ref, app_ref, sums_ref):
    m_local, sin_cos, samples, width = dir_ref.shape
    window = hi_ref.shape[2]
    copies = geo.outer * geo.inner
    order_devices = recv_ref.shape[0] // copies
    damping = damp_ref[...]
    rows = sin_cos * samples
    back = window - scal[geo.block_offset]
    sums = [None] * 4
    for m in range(m_local):
        tiles = []
        for b in range(geo.inner):
            for a in range(geo.outer):
                band = scal[geo.outer_of + a] * geo.inner + scal[geo.inner_of + b]
                for o in range(order_devices):
                    tiles.append(recv_ref[o * copies + band, m])
        spectra = split_bf16(jnp.concatenate(tiles, axis=0))
        summed = dot3(spectra, (hi_ref[m], lo_ref[m]), ((0,), (0,)))
        summed = pltpu.roll(summed, back, 1)[:, :width]
        valid = own_mask(geo, scal, m, samples, width)
        for s in range(sin_cos):
            direction = jnp.where(valid, dir_ref[m, s], 0.0)
            residual = jnp.where(valid, res_ref[m, s], 0.0)
            part = summed[s * samples : (s + 1) * samples]
            applied = jnp.where(valid, part + damping * direction, 0.0)
            app_ref[m, s] = applied
            terms = (
                residual * residual,
                direction * applied,
                residual * applied,
                applied * applied,
            )
            sums = [t if old is None else old + t for old, t in zip(sums, terms)]
    stacked = jnp.concatenate(sums, axis=0)
    totals = jnp.sum(stacked, axis=1, keepdims=True)
    count = totals.shape[0]
    row = lax.broadcasted_iota(jnp.int32, (count, count), 0)
    column = lax.broadcasted_iota(jnp.int32, (count, count), 1)
    line = jnp.sum(jnp.where(row == column, totals, 0.0), axis=0, keepdims=True)
    for device in range(sums_ref.shape[0]):
        sums_ref[device] = line


def update(geo, scal, sums_ref, app_ref, pos_ref, dir_ref, res_ref, pos_out, res_out, dir_out):
    m_local, sin_cos, samples, width = dir_ref.shape
    totals = jnp.sum(sums_ref[...], axis=0)
    before, curvature, cross, square = [
        totals[:, i * samples : (i + 1) * samples] for i in range(4)
    ]
    step_row = before / curvature
    after = before - 2.0 * step_row * cross + step_row * step_row * square
    ratio_row = after / before
    row = lax.broadcasted_iota(jnp.int32, (samples, samples), 0)
    column = lax.broadcasted_iota(jnp.int32, (samples, samples), 1)
    diagonal = row == column
    step = jnp.sum(jnp.where(diagonal, step_row, 0.0), axis=1, keepdims=True)
    ratio = jnp.sum(jnp.where(diagonal, ratio_row, 0.0), axis=1, keepdims=True)
    for m in range(m_local):
        valid = own_mask(geo, scal, m, samples, width)
        for s in range(sin_cos):
            direction = jnp.where(valid, dir_ref[m, s], 0.0)
            residual = jnp.where(valid, res_ref[m, s], 0.0)
            position = jnp.where(valid, pos_ref[m, s], 0.0)
            new_residual = residual - step * app_ref[m, s]
            pos_out[m, s] = position + step * direction
            res_out[m, s] = new_residual
            dir_out[m, s] = new_residual + ratio * direction


class Geometry:
    def __init__(self, outer, inner, degrees, m_local):
        self.outer, self.inner = outer, inner
        bands = outer * inner
        block = degrees // bands
        pair = degrees // outer

        def down(x):
            return x // LANES * LANES

        def up(x):
            return -(-x // LANES) * LANES

        self.window_starts = [down(a * pair) for a in range(outer)]
        self.window = max(up((a + 1) * pair) - s for a, s in enumerate(self.window_starts))
        places = [
            [(a * inner + b) * block - self.window_starts[a] for b in range(inner)]
            for a in range(outer)
        ]
        starts = [[down(p) for p in row] for row in places]
        self.block_window = max(
            up(p + block) - s for prow, srow in zip(places, starts) for p, s in zip(prow, srow)
        )
        self.block_starts = [
            [min(s, self.window - self.block_window) for s in row] for row in starts
        ]
        self.window_start, self.block_start, self.block_offset, self.own_start = 0, 1, 2, 3
        self.places = 4
        self.outer_of = self.places + inner
        self.inner_of = self.outer_of + outer
        self.orders = self.inner_of + inner
        rows = []
        for a in range(outer):
            for b in range(inner):
                row = [
                    self.window_starts[a],
                    self.block_starts[a][b],
                    places[a][b] - self.block_starts[a][b],
                    (a * inner + b) * block,
                ]
                row += [places[a][(b - s) % inner] for s in range(inner)]
                row += [(a - s) % outer for s in range(outer)]
                row += [(b - s) % inner for s in range(inner)]
                rows.append(row)
        self.table = np.array(rows, np.int32)


def pick(index, choices):
    result = choices[-1]
    for i in range(len(choices) - 2, -1, -1):
        result = jnp.where(index == i, choices[i], result)
    return result


def rotate(x, axis, size, shift):
    return lax.ppermute(x, axis, [(i, (i + shift) % size) for i in range(size)])


def plain_grid(geo, grid_in, order_of, class_idx, land, class_weight, period):
    order_devices = grid_in.shape[0] // geo.outer
    m_local, rows, width = grid_in.shape[1:]
    orders = order_devices * m_local
    longitudes = class_idx.shape[1]
    stacked = grid_in.reshape(order_devices, geo.outer, m_local, rows, 2, width // 2)
    stacked = jnp.sum(stacked, axis=1).reshape(orders, rows, 2, width // 2)
    phases = order_of[:, None] * jnp.arange(period, dtype=jnp.int32)[None, :] % longitudes
    angles = phases.astype(jnp.float32) * (2.0 * math.pi / longitudes)
    harmonic = jnp.stack([jnp.cos(angles), jnp.sin(angles)])
    surface = jnp.einsum("mrsk,smp->rkp", stacked, harmonic, precision=HIGHEST)
    onehot = class_idx[:, :, None] == jnp.arange(class_weight.shape[0], dtype=jnp.int32)
    by_class = jnp.dot(onehot.astype(jnp.float32), class_weight, precision=HIGHEST)
    weight = jnp.where(land == 1, by_class[:, :, 1], by_class[:, :, 0])
    folded = jnp.sum(weight.reshape(rows, longitudes // period, period), axis=1)
    weighted = surface * folded[:, None, :]
    spectra = jnp.einsum("rkp,smp->mrsk", weighted, harmonic, precision=HIGHEST)
    spectra = (spectra * (2.0 / longitudes)).reshape(order_devices, 1, m_local, rows, width)
    copies = geo.outer * geo.inner
    spectra = jnp.broadcast_to(spectra, (order_devices, copies, m_local, rows, width))
    return spectra.reshape(order_devices * copies, m_local, rows, width)


def shards(
    outer,
    inner,
    position,
    residual,
    direction,
    legendre,
    order_of,
    class_idx,
    land,
    class_weight,
    damping,
):
    m_local, sin_cos, samples, deg_local = position.shape
    degrees, band_rows = legendre.shape[1:]
    rows_here, longitudes = class_idx.shape
    orders = order_of.shape[0]
    order_devices = orders // m_local
    devices = order_devices * outer * inner
    line = sin_cos * samples
    geo = Geometry(outer, inner, degrees, m_local)
    a = lax.axis_index("outer")
    b = lax.axis_index("inner")
    order_index = lax.axis_index("order")
    my_orders = lax.dynamic_slice_in_dim(order_of, order_index * m_local, m_local)
    where = lax.dynamic_index_in_dim(jnp.asarray(geo.table), a * inner + b, 0, keepdims=False)
    scal = jnp.concatenate([where, my_orders])

    by_row = jnp.transpose(legendre, (0, 2, 1))
    end = max(s + geo.window for s in geo.window_starts)
    by_row = jnp.pad(by_row, ((0, 0), (0, 0), (0, max(0, end - degrees))))
    windows = [by_row[:, :, s : s + geo.window] for s in geo.window_starts]
    received = [
        rotate(pick((a + s) % outer, windows), "outer", outer, s) for s in range(1, outer)
    ]
    siblings = [rotate(direction, "inner", inner, s) for s in range(1, inner)]
    own_window = pick(a, windows)

    pair = jax.ShapeDtypeStruct((m_local, line, geo.window), jnp.bfloat16)
    dir_hi, dir_lo = call(
        functools.partial(place_direction, geo),
        (pair, pair),
        [SCALARS] + [WHOLE] * inner,
        4 * m_local * line * geo.window,
        8 * m_local * line * geo.window,
    )(scal, direction, *siblings)
    own_flops = 6 * m_local * line * geo.window * band_rows
    own_rows = call(
        synthesise_own,
        jax.ShapeDtypeStruct((m_local, band_rows, line), jnp.float32),
        [WHOLE] * 3,
        own_flops,
        4 * m_local * (line + band_rows) * geo.window,
    )(own_window, dir_hi, dir_lo)

    stride = longitudes // (2 * orders)
    period = longitudes // stride if longitudes % stride == 0 else longitudes
    small = orders <= 32 and LANES % period == 0 and line == LANES and longitudes % period == 0
    if small:
        count = 2 * orders
        n = np.arange(count)[None, :]
        p = np.arange(LANES)[:, None]
        angle = 2.0 * math.pi * ((n * p) % period) / period
        basis = np.zeros((LANES, -(-2 * count // LANES) * LANES), np.float32)
        basis[:, :count] = np.cos(angle) / longitudes
        basis[:, count : 2 * count] = np.sin(angle) / longitudes
        tables = call(
            functools.partial(weight_tables, longitudes, period),
            jax.ShapeDtypeStruct((4, count, rows_here, LANES), jnp.float32),
            [WHOLE, WHOLE, SCALARS, WHOLE],
            100 * rows_here * longitudes,
            8 * rows_here * longitudes,
        )(class_idx, land, class_weight, jnp.asarray(basis))

    to_rows = call(
        functools.partial(synthesise_rest, geo),
        jax.ShapeDtypeStruct((order_devices, outer, m_local, rows_here, line), jnp.float32),
        [SCALARS] + [WHOLE] * (outer + 2),
        own_flops * (outer - 1),
        4 * m_local * (line + band_rows) * geo.window,
    )(scal, own_rows, *received, dir_hi, dir_lo)
    grid_in = lax.all_to_all(
        to_rows.reshape(order_devices * outer, m_local, rows_here, line),
        ("order", "outer"),
        split_axis=0,
        concat_axis=0,
        tiled=True,
    )

    def block_of(array, s):
        per_inner = [
            [array[..., t : t + geo.block_window] for t in (geo.block_starts[i][j] for i in range(outer))]
            for j in range(inner)
        ]
        target = (b + s) % inner
        choices = []
        for j in range(inner):
            starts = {geo.block_starts[i][j] for i in range(outer)}
            choices.append(per_inner[j][0] if len(starts) == 1 else pick(a, per_inner[j]))
        return pick(target, choices)

    here = [own_window] + received
    from_inner = [
        rotate(jnp.stack([block_of(x, s) for x in here]), "inner", inner, s)
        for s in range(1, inner)
    ]
    block = jax.ShapeDtypeStruct((m_local, inner * outer * band_rows, geo.block_window), jnp.bfloat16)
    leg_hi, leg_lo = call(
        functools.partial(split_block, geo),
        (block, block),
        [SCALARS] + [WHOLE] * (outer + 1),
        4 * m_local * inner * outer * band_rows * geo.block_window,
        8 * m_local * inner * outer * band_rows * geo.block_window,
    )(scal, *here, jnp.stack(from_inner))

    if small:
        to_orders = pl.pallas_call(
            functools.partial(grid_rows, geo),
            out_shape=jax.ShapeDtypeStruct((devices, m_local, rows_here, line), jnp.float32),
            in_specs=[SCALARS, WHOLE, WHOLE],
            out_specs=WHOLE,
            scratch_shapes=[pltpu.VMEM((orders, rows_here, line), jnp.float32)] * 3,
            compiler_params=PARAMS,
            cost_estimate=pl.CostEstimate(
                flops=6 * orders * orders * rows_here * line,
                bytes_accessed=8 * orders * rows_here * line,
                transcendentals=0,
            ),
        )(order_of // stride, grid_in, tables)
    else:
        to_orders = plain_grid(geo, grid_in, order_of, class_idx, land, class_weight, period)
    spectra = lax.all_to_all(
        to_orders, ("order", "outer", "inner"), split_axis=0, concat_axis=0, tiled=True
    )
    coefficients = jax.ShapeDtypeStruct(position.shape, jnp.float32)
    applied, sums = call(
        functools.partial(project, geo),
        (coefficients, jax.ShapeDtypeStruct((devices, 1, 4 * samples), jnp.float32)),
        [SCALARS] + [WHOLE] * 6,
        6 * m_local * line * geo.block_window * band_rows * outer * inner,
        16 * m_local * line * deg_local,
    )(scal, spectra, leg_hi, leg_lo, direction, residual, damping[None, :])
    sums = lax.all_to_all(
        sums, ("order", "outer", "inner"), split_axis=0, concat_axis=0, tiled=True
    )
    return call(
        functools.partial(update, geo),
        (coefficients,) * 3,
        [SCALARS] + [WHOLE] * 5,
        10 * m_local * line * deg_local,
        28 * m_local * line * deg_local,
    )(scal, sums, applied, position, direction, residual)


def solution(mesh):
    order_devices, bands = mesh.shape["order"], mesh.shape["lat"]
    outer = 2 if bands % 2 == 0 else 1
    inner = bands // outer
    split = Mesh(mesh.devices.reshape(order_devices, outer, inner), ("order", "outer", "inner"))
    lat = ("outer", "inner")
    coefficients = P("order", None, None, lat)
    grid = P(("outer", "inner", "order"), None)
    return jax.shard_map(
        functools.partial(shards, outer, inner),
        mesh=split,
        in_specs=(
            coefficients,
            coefficients,
            coefficients,
            P("order", None, lat),
            P(),
            grid,
            grid,
            P(),
            P(lat),
        ),
        out_specs=(coefficients,) * 3,
        check_vma=False,
    )
```

time: 209 us -> 66.9 us (0.32)
  waiting for transfers between devices: 93.1 us -> 23.7 us
  blocking collectives: 48.7 us -> 9.36 us
  matrix products: 30.9 us -> 0 us
  between operations: 14.2 us -> 0.82 us
  Pallas kernels: 0 us -> 11.7 us
  other arithmetic: 12 us -> 3.45 us
  starting transfers between devices: 5.77 us -> 12.8 us
    psum x1 -> x0, waiting for transfers between devices: 50.2 us -> none  [shards(): totals = lax.psum(band_part, 'lat')]
    psum x1 -> x0, blocking collectives: 39.4 us -> none  [shards(): lax.psum((sample_sums(res_m * res_m), sample_sums(dir_m * applied), sampl...]
    all_gather x1 -> x0, waiting for transfers between devices: 36.3 us -> none  [shards(): block_part = lax.all_gather(direction, 'lat', axis=3, tiled=True)]
    dot_general x5 -> x0, matrix products: 30.9 us -> none  [the longest x1 12.4 us: shards(): jnp.einsum('rkl,sml->mrsk', weighted, harmonic, precision=highest)]
    pallas_call x0 -> x8, Pallas kernels: none -> 11.7 us  [the longest x1 2.1 us: shards(): call(functools.partial(update, geo), (coefficients,) * 3, [SCALARS] + [WH...]
    ppermute x0 -> x3, waiting for transfers between devices: none -> 8.69 us  [rotate(): return lax.ppermute(x, axis, [(i, (i + shift) % size) for i in range(size)])]
    all_to_all x1 -> x2, waiting for transfers between devices: 6.64 us -> 15 us  [the longest x1 8.16 us: shards(): lax.all_to_all(to_orders, ('order', 'outer', 'inner'), split_axis=0, conc...]
    mul x1 -> x0, other arithmetic: 6.42 us -> none  [shards(): masked = block_part * in_triangle[:, None, None, :]]
  transfers between devices with their start and end apart: 3 -> 5, of which waited for: 3 -> 3; matrix products, arithmetic and copies ran while one was open for 1% -> 3% of each run, Pallas kernels for 0% -> 9%
where the time goes in v1:
time: 66.9 us; the launch traced here: 66.5 us
  waiting for transfers between devices  23.7 us (35%)
  starting transfers between devices  12.8 us (19%)
  Pallas kernels  11.7 us (17%)
  blocking collectives  9.36 us (14%)
  local copies, waits for them, and re-layouts  4.74 us (7%)
  other arithmetic  3.45 us (5%)
  between operations  0.82 us (1%)
    all_to_all x1, blocking collectives, shards(): lax.all_to_all(sums, ('order', 'outer', 'inner'), split_axis=0, concat_ax...  9.36 us
    ppermute x3, waiting for transfers between devices, rotate(): return lax.ppermute(x, axis, [(i, (i + shift) % size) for i in range(size)])  8.69 us
    all_to_all x1, waiting for transfers between devices, shards(): lax.all_to_all(to_orders, ('order', 'outer', 'inner'), split_axis=0, conc...  8.16 us
    all_to_all x1, starting transfers between devices, shards(): lax.all_to_all(to_rows.reshape(order_devices * outer, m_local, rows_here,...  7.08 us
    all_to_all x1, waiting for transfers between devices, shards(): lax.all_to_all(to_rows.reshape(order_devices * outer, m_local, rows_here,...  6.84 us
    unnamed x27, local copies, waits for them, and re-layouts  3.97 us
    ppermute x3, starting transfers between devices, rotate(): return lax.ppermute(x, axis, [(i, (i + shift) % size) for i in range(size)])  2.97 us
    all_to_all x1, starting transfers between devices, shards(): lax.all_to_all(to_orders, ('order', 'outer', 'inner'), split_axis=0, conc...  2.72 us
  transfers between devices with their start and end apart: 5, of which 3 were waited for; matrix products, arithmetic and copies ran while one was open for 3% of the time, Pallas kernels for 9%

profile of v1, /device:TPU:0, one launch (start us, length us, event | category | flops | bytes accessed | tf_op | source)
XLA Modules:
  0.0 66.5 jit_solution(10119945930106351291)
XLA Ops:
  0.6 0.0 copy-start
  0.7 0.0 copy-start.11
  0.7 0.0 copy-start.12
  0.7 0.0 copy-start.7
  0.7 0.0 copy-start.8
  0.7 0.0 copy-start.9
  0.7 2.4 %slice_select_fusion = (f32[2,64,1152]{2,1,0:T(8,128)}, f32[2,64,1152]{2,1,0:T(8,128)S(1)}) fusion(f32[2,64,2160]{2,1,0:T(8,128)} %bitcast.10, pred[]{:T(512)S(6)} %eq.15, pred[]{:T(512)S(6)} %eq.14), kind=kLoop, calls=%fused_computation.2 | loop fusion | flops 294912 | bytes 2883586 | tf_op jit(solution)/shard_map/jit(_where)/select_n | solution.py:295
  3.1 3.0 %collective-permute-start.1 = (f32[2,64,1152]{2,1,0:T(8,128)}, f32[2,64,1152]{2,1,0:T(8,128)S(1)}, u32[]{:S(2)}, u32[]{:S(2)}) collective-permute-start(f32[2,64,1152]{2,1,0:T(8,128)} %get-tuple-element.15), channel_id=1, source_target_pairs={{0,2},{2,0},{1,3},{3,1},{4,6},{6,4},{5,7},{7,5},{8,10},{10,8},{9,1... | collective-permute-start | bytes 1769480 | tf_op jit(solution)/shard_map/ppermute | solution.py:300
  6.1 0.0 copy-done
  6.1 0.0 collective-permute-start
  6.1 0.0 copy-done.11
  6.1 0.1 copy.14.value_ref
  6.2 0.0 copy-done.12
  6.2 0.1 dynamic_slice.8
  6.3 0.0 copy-done.7
  6.3 0.0 copy-done.8
  6.3 0.0 copy-done.9
  6.3 1.4 %shard_map.133.table_ref = f32[4,32,8,128]{3,2,1,0:T(8,128)S(1)} custom-call(s32[8,4320]{1,0:T(8,128)S(1)} %copy-done.7, s32[8,4320]{1,0:T(8,128)S(1)} %copy-done.8, f32[16,2]{1,0:T(8,128)S(1)} %copy.14.value_ref, f32[128,128]{1,0:T(8,128)S(1)} %copy-done.9), custom_call_target="tpu_custom_call" | custom-call | flops 3456000 | bytes 276480 | tf_op jit(solution)/shard_map/pallas_call | solution.py:392
  7.6 0.7 %dynamic-slice_bitcast_fusion = s32[10]{0:T(128)S(1)} fusion(s32[4,10]{1,0:T(4,128)} %constant.55.clone, s32[]{:T(128)S(6)} %select_n.51), kind=kLoop, calls=%fused_computation.10 | loop fusion | bytes 84 | tf_op jit(solution)/shard_map/jit(dynamic_index_in_dim)/squeeze | solution.py:351
  8.3 0.1 pad_add_fusion.scal
  8.4 0.0 collective-permute-done.refs_1_
  8.4 1.7 %shard_map.130 = (bf16[2,128,1152]{2,1,0:T(8,128)(2,1)S(1)}, bf16[2,128,1152]{2,1,0:T(8,128)(2,1)S(1)}) custom-call(s32[12]{0:T(128)S(1)} %pad_add_fusion.scal, f32[2,2,64,540]{3,2,1,0:T(8,128)S(1)} %copy-done, f32[2,2,64,540]{3,2,1,0:T(8,128)S(1)} %collective-permute-done.refs_1_), custom_call_target="tpu_custom_call" | custom-call | flops 1179648 | bytes 2359296 | tf_op jit(solution)/shard_map/pallas_call | solution.py:365
  10.2 0.8 %shard_map.131.own_ref = f32[2,64,128]{2,1,0:T(8,128)S(1)} custom-call(f32[2,64,1152]{2,1,0:T(8,128)S(1)} %get-tuple-element.16.leg_ref.refs_0_, bf16[2,128,1152]{2,1,0:T(8,128)(2,1)S(1)} %get-tuple-element.9.hi_ref.refs_1_, bf16[2,128,1152]{2,1,0:T(8,128)(2,1)S(1)} %get-tuple-element.10.lo_ref.refs_2_), custom_call_target="tpu_custom_call" | custom-call | flops 113246208 | bytes 1769472 | tf_op jit(solution)/shard_map/pallas_call | solution.py:373
  10.9 8.7 %collective-permute-done.1.refs_0_.refs_1_ = f32[2,64,1152]{2,1,0:T(8,128)S(1)} collective-permute-done((f32[2,64,1152]{2,1,0:T(8,128)}, f32[2,64,1152]{2,1,0:T(8,128)S(1)}, u32[]{:S(2)}, u32[]{:S(2)}) %collective-permute-start.1) | collective-permute-done | bytes 589856 | tf_op jit(solution)/shard_map/ppermute | solution.py:300
  19.6 2.0 %shard_map.132 = f32[8,2,2,8,128]{4,3,2,1,0:T(8,128)} custom-call(s32[12]{0:T(128)S(1)} %pad_add_fusion.scal, f32[2,64,128]{2,1,0:T(8,128)S(1)} %shard_map.131.own_ref, f32[2,64,1152]{2,1,0:T(8,128)S(1)} %collective-permute-done.1.refs_0_.refs_1_, bf16[2,128,1152]{2,1,0:T(8,128)(2,1)S(1)} %get-tuple-element.9.hi_ref.refs_1_, ...), custom_call_target="tpu_custom_call" | custom-call | flops 113246208 | bytes 1769472 | tf_op jit(solution)/shard_map/pallas_call | solution.py:400
  21.6 7.1 %all-to-all-start = ((f32[16,2,8,128]{3,2,1,0:T(8,128)}), f32[16,2,8,128]{3,2,1,0:T(8,128)S(1)}, u32[]{:S(2)}, u32[]{:S(2)}) async-start(f32[16,2,8,128]{3,2,1,0:T(8,128)} %bitcast.2), calls=%async_computation | async-start | bytes 262144 | tf_op jit(solution)/shard_map/all_to_all | solution.py:407
  28.7 0.0 copy-start.10
  28.8 0.9 %pad_maximum_fusion = f32[2,2,64,640]{3,2,1,0:T(8,128)} fusion(f32[1,2,64,640]{3,2,1,0:T(8,128)S(1)} %fusion, f32[1,2,64,640]{3,2,1,0:T(8,128)S(1)} %fusion.1), kind=kLoop, calls=%fused_computation.1 | loop fusion | flops 163840 | bytes 1310720 | tf_op jit(solution)/shard_map/stack | solution.py:429
  29.6 0.0 collective-permute-start.2
  29.7 6.8 %all-to-all-done.recv_ref = f32[16,2,8,128]{3,2,1,0:T(8,128)S(1)} async-done(((f32[16,2,8,128]{3,2,1,0:T(8,128)}), f32[16,2,8,128]{3,2,1,0:T(8,128)S(1)}, u32[]{:S(2)}, u32[]{:S(2)}) %all-to-all-start) | async-done | bytes 131104 | tf_op jit(solution)/shard_map/all_to_all | solution.py:407
  36.5 1.5 %shard_map.134 = f32[32,2,8,128]{3,2,1,0:T(8,128)} custom-call(s32[16]{0:T(128)S(1)} %and_select_fusion.slot, f32[16,2,8,128]{3,2,1,0:T(8,128)S(1)} %all-to-all-done.recv_ref, f32[4,32,8,128]{3,2,1,0:T(8,128)S(1)} %shard_map.133.table_ref), custom_call_target="tpu_custom_call" | custom-call | flops 1572864 | bytes 131072 | tf_op jit(solution)/shard_map/pallas_call | solution.py:442
  38.0 0.0 copy-start.1
  38.0 2.7 %all-to-all-start.1 = ((f32[32,2,8,128]{3,2,1,0:T(8,128)}), f32[32,2,8,128]{3,2,1,0:T(8,128)S(1)}, u32[]{:S(2)}, u32[]{:S(2)}) async-start(f32[32,2,8,128]{3,2,1,0:T(8,128)} %shard_map.134), calls=%async_computation.1 | async-start | bytes 524288 | tf_op jit(solution)/shard_map/all_to_all | solution.py:457
  40.8 0.0 copy-done.10
  40.8 0.0 collective-permute-done.2
  40.8 0.7 %shard_map.135 = (bf16[2,256,640]{2,1,0:T(8,128)(2,1)S(1)}, bf16[2,256,640]{2,1,0:T(8,128)(2,1)S(1)}) custom-call(s32[12]{0:T(128)S(1)} %pad_add_fusion.scal, f32[2,64,1152]{2,1,0:T(8,128)S(1)} %get-tuple-element.16.leg_ref.refs_0_, f32[2,64,1152]{2,1,0:T(8,128)S(1)} %collective-permute-done.1.refs_0_.refs_1_, f32[1,2,2,64,640]{4,3,2,1,0:T(8,128)S(1)} %bitcast.9), custom_call_target="tpu_custom_call" | custom-call | flops 1310720 | bytes 2621440 | tf_op jit(solution)/shard_map/pallas_call | solution.py:433
  41.5 0.0 copy-start.3
  41.5 0.8 %copy-done.3 = bf16[2,256,640]{2,1,0:T(8,128)(2,1)} copy-done((bf16[2,256,640]{2,1,0:T(8,128)(2,1)}, bf16[2,256,640]{2,1,0:T(8,128)(2,1)S(1)}, u32[]{:S(2)}) %copy-start.3) | copy-done | bytes 655384
  42.4 0.0 copy-start.5
  42.4 0.8 %copy-done.5 = bf16[2,256,640]{2,1,0:T(8,128)(2,1)} copy-done((bf16[2,256,640]{2,1,0:T(8,128)(2,1)}, bf16[2,256,640]{2,1,0:T(8,128)(2,1)S(1)}, u32[]{:S(2)}) %copy-start.5) | copy-done | bytes 655384
  43.2 8.2 %all-to-all-done.1.recv_ref = f32[32,2,8,128]{3,2,1,0:T(8,128)S(1)} async-done(((f32[32,2,8,128]{3,2,1,0:T(8,128)}), f32[32,2,8,128]{3,2,1,0:T(8,128)S(1)}, u32[]{:S(2)}, u32[]{:S(2)}) %all-to-all-start.1) | async-done | bytes 262176 | tf_op jit(solution)/shard_map/all_to_all | solution.py:457
  51.4 0.0 copy-done.1
  51.4 0.0 copy-start.4
  51.4 1.1 %copy-done.4 = bf16[2,256,640]{2,1,0:T(8,128)(2,1)S(1)} copy-done((bf16[2,256,640]{2,1,0:T(8,128)(2,1)S(1)}, bf16[2,256,640]{2,1,0:T(8,128)(2,1)}, u32[]{:S(2)}) %copy-start.4) | copy-done | bytes 655384
  52.5 0.0 copy-start.6
  52.5 1.1 %copy-done.6 = bf16[2,256,640]{2,1,0:T(8,128)(2,1)S(1)} copy-done((bf16[2,256,640]{2,1,0:T(8,128)(2,1)S(1)}, bf16[2,256,640]{2,1,0:T(8,128)(2,1)}, u32[]{:S(2)}) %copy-start.6) | copy-done | bytes 655384
  53.5 0.0 copy-start.2
  53.5 1.5 %shard_map.136 = (f32[2,2,64,540]{3,2,1,0:T(8,128)S(1)}, f32[32,1,256]{2,1,0:T(1,128)S(1)}) custom-call(s32[12]{0:T(128)S(1)} %pad_add_fusion.scal, f32[32,2,8,128]{3,2,1,0:T(8,128)S(1)} %all-to-all-done.1.recv_ref, bf16[2,256,640]{2,1,0:T(8,128)(2,1)S(1)} %copy-done.4, bf16[2,256,640]{2,1,0:T(8,128)(2,1)S(1)} %copy-done.6, f32[2,2,64,540]{3,2,1,0:T(8,128)S(1)} %copy-done, ...), custom_call_target="tpu_custom_call" | custom-call | flops 251658240 | bytes 2211840 | tf_op jit(solution)/shard_map/pallas_call | solution.py:461
  55.1 9.4 %all_to_all.15.sums_ref = f32[32,1,256]{2,1,0:T(1,128)S(1)} all-to-all(f32[32,1,256]{2,1,0:T(1,128)S(1)} %get-tuple-element.13), channel_id=1, replica_groups=mesh['order'=8,'outer'=2,'inner'=2] {'order','outer','inner'}, dimensions={0} | all-to-all | bytes 65536 | tf_op jit(solution)/shard_map/all_to_all | solution.py:468
  64.4 0.0 copy-done.2
  64.4 2.1 %shard_map.137 = (f32[2,2,64,540]{3,2,1,0:T(8,128)}, f32[2,2,64,540]{3,2,1,0:T(8,128)}, f32[2,2,64,540]{3,2,1,0:T(8,128)}) custom-call(s32[12]{0:T(128)S(1)} %pad_add_fusion.scal, f32[32,1,256]{2,1,0:T(1,128)S(1)} %all_to_all.15.sums_ref, f32[2,2,64,540]{3,2,1,0:T(8,128)S(1)} %get-tuple-element.14.app_ref, f32[2,2,64,540]{3,2,1,0:T(8,128)S(1)} %copy-done.2, ...), custom_call_target="tpu_custom_call" | custom-call | flops 1382400 | bytes 3870720 | tf_op jit(solution)/shard_map/pallas_call | solution.py:471
  (4 shorter events, 0.1 us)
Async XLA Ops:
  0.6 5.4 %copy-start = (f32[2,2,64,540]{3,2,1,0:T(8,128)S(1)}, f32[2,2,64,540]{3,2,1,0:T(8,128)}, u32[]{:S(2)}) copy-start(f32[2,2,64,540]{3,2,1,0:T(8,128)} %dir_ref.3) | copy-start | bytes 1658884
  0.7 5.4 %copy-start.11 = (f32[16,2]{0,1:T(2,128)S(1)}, f32[16,2]{0,1:T(2,128)}, u32[]{:S(2)}) copy-start(f32[16,2]{0,1:T(2,128)} %param.18) | copy-start | bytes 388
  0.7 5.5 %copy-start.12 = (s32[16]{0:T(128)S(1)}, s32[16]{0:T(128)}, u32[]{:S(2)}) copy-start(s32[16]{0:T(128)} %param.15) | copy-start | bytes 196
  0.7 5.6 %copy-start.7 = (s32[8,4320]{1,0:T(8,128)S(1)}, s32[8,4320]{1,0:T(8,128)}, u32[]{:S(2)}) copy-start(s32[8,4320]{1,0:T(8,128)} %class_ref.1) | copy-start | bytes 414724
  0.7 5.6 %copy-start.8 = (s32[8,4320]{1,0:T(8,128)S(1)}, s32[8,4320]{1,0:T(8,128)}, u32[]{:S(2)}) copy-start(s32[8,4320]{1,0:T(8,128)} %land_ref.1) | copy-start | bytes 414724
  0.7 5.6 %copy-start.9 = (f32[128,128]{1,0:T(8,128)S(1)}, f32[128,128]{1,0:T(8,128)}, u32[]{:S(2)}) copy-start(f32[128,128]{1,0:T(8,128)} %constant.56.clone.basis_ref) | copy-start | bytes 196612
  3.1 16.5 %collective-permute-start.1 = (f32[2,64,1152]{2,1,0:T(8,128)}, f32[2,64,1152]{2,1,0:T(8,128)S(1)}, u32[]{:S(2)}, u32[]{:S(2)}) collective-permute-start(f32[2,64,1152]{2,1,0:T(8,128)} %get-tuple-element.15), channel_id=1, source_target_pairs={{0,2},{2,0},{1,3},{3,1},{4,6},{6,4},{5,7},{7,5},{8,10},{10,8},{9,1... | collective-permute-start | bytes 1769480 | tf_op jit(solution)/shard_map/ppermute | solution.py:300
  6.1 2.3 %collective-permute-start = (f32[2,2,64,540]{3,2,1,0:T(8,128)S(1)}, f32[2,2,64,540]{3,2,1,0:T(8,128)S(1)}, u32[]{:S(2)}, u32[]{:S(2)}) collective-permute-start(f32[2,2,64,540]{3,2,1,0:T(8,128)S(1)} %copy-done), channel_id=1, source_target_pairs={{0,1},{1,0},{2,3},{3,2},{4,5},{5,4},{6,7},{7,6},{8,9},{9,8},{10,11... | collective-permute-start | bytes 1658888 | tf_op jit(solution)/shard_map/ppermute | solution.py:300
  21.6 14.9 %all-to-all-start = ((f32[16,2,8,128]{3,2,1,0:T(8,128)}), f32[16,2,8,128]{3,2,1,0:T(8,128)S(1)}, u32[]{:S(2)}, u32[]{:S(2)}) async-start(f32[16,2,8,128]{3,2,1,0:T(8,128)} %bitcast.2), calls=%async_computation | async-start | bytes 262144 | tf_op jit(solution)/shard_map/all_to_all | solution.py:407
  28.7 12.0 %copy-start.10 = (f32[540]{0:T(1024)S(1)}, f32[540]{0:T(1024)}, u32[]{:S(2)}) copy-start(f32[540]{0:T(1024)} %param.19) | copy-start | bytes 6484
  29.6 11.2 %collective-permute-start.2 = (f32[2,2,64,640]{3,2,1,0:T(8,128)}, f32[2,2,64,640]{3,2,1,0:T(8,128)S(1)}, u32[]{:S(2)}, u32[]{:S(2)}) collective-permute-start(f32[2,2,64,640]{3,2,1,0:T(8,128)} %pad_maximum_fusion), channel_id=1, source_target_pairs={{0,1},{1,0},{2,3},{3,2},{4,5},{5,4},{6,7},{7,6},{8,9},{9,8},{10,11... | collective-permute-start | bytes 1966088 | tf_op jit(solution)/shard_map/ppermute | solution.py:300
  38.0 13.3 %copy-start.1 = (f32[2,2,64,540]{3,2,1,0:T(8,128)S(1)}, f32[2,2,64,540]{3,2,1,0:T(8,128)}, u32[]{:S(2)}) copy-start(f32[2,2,64,540]{3,2,1,0:T(8,128)} %res_ref.3) | copy-start | bytes 1658884
  38.0 13.3 %all-to-all-start.1 = ((f32[32,2,8,128]{3,2,1,0:T(8,128)}), f32[32,2,8,128]{3,2,1,0:T(8,128)S(1)}, u32[]{:S(2)}, u32[]{:S(2)}) async-start(f32[32,2,8,128]{3,2,1,0:T(8,128)} %shard_map.134), calls=%async_computation.1 | async-start | bytes 524288 | tf_op jit(solution)/shard_map/all_to_all | solution.py:457
  41.5 0.8 %copy-start.3 = (bf16[2,256,640]{2,1,0:T(8,128)(2,1)}, bf16[2,256,640]{2,1,0:T(8,128)(2,1)S(1)}, u32[]{:S(2)}) copy-start(bf16[2,256,640]{2,1,0:T(8,128)(2,1)S(1)} %get-tuple-element.11.hi_ref) | copy-start | bytes 1966084
  42.4 0.8 %copy-start.5 = (bf16[2,256,640]{2,1,0:T(8,128)(2,1)}, bf16[2,256,640]{2,1,0:T(8,128)(2,1)S(1)}, u32[]{:S(2)}) copy-start(bf16[2,256,640]{2,1,0:T(8,128)(2,1)S(1)} %get-tuple-element.12.lo_ref) | copy-start | bytes 1966084
  51.4 1.1 %copy-start.4 = (bf16[2,256,640]{2,1,0:T(8,128)(2,1)S(1)}, bf16[2,256,640]{2,1,0:T(8,128)(2,1)}, u32[]{:S(2)}) copy-start(bf16[2,256,640]{2,1,0:T(8,128)(2,1)} %copy-done.3) | copy-start | bytes 1966084
  52.5 1.1 %copy-start.6 = (bf16[2,256,640]{2,1,0:T(8,128)(2,1)S(1)}, bf16[2,256,640]{2,1,0:T(8,128)(2,1)}, u32[]{:S(2)}) copy-start(bf16[2,256,640]{2,1,0:T(8,128)(2,1)} %copy-done.5) | copy-start | bytes 1966084
  53.5 10.9 %copy-start.2 = (f32[2,2,64,540]{3,2,1,0:T(8,128)S(1)}, f32[2,2,64,540]{3,2,1,0:T(8,128)}, u32[]{:S(2)}) copy-start(f32[2,2,64,540]{3,2,1,0:T(8,128)} %pos_ref.1) | copy-start | bytes 1658884

commit v2 on v1

v2 whole, which is shorter than its diff:
```python
import functools
import math

import jax
import jax.numpy as jnp
import numpy as np
from jax import lax
from jax.experimental import pallas as pl
from jax.experimental.pallas import tpu as pltpu
from jax.sharding import Mesh
from jax.sharding import PartitionSpec as P

LANES = 128
HIGHEST = lax.Precision.HIGHEST
VMEM_LEAST = 16 * 1024 * 1024
VMEM_MOST = 48 * 1024 * 1024
WHOLE = pl.BlockSpec(memory_space=pltpu.VMEM)
SCALARS = pl.BlockSpec(memory_space=pltpu.SMEM)
IN_HBM = pl.BlockSpec(memory_space=pltpu.HBM)


def split_bf16(x):
    hi = x.astype(jnp.bfloat16)
    lo = (x - hi.astype(jnp.float32)).astype(jnp.bfloat16)
    return hi, lo


def dot_pairs(a, b, dims, rows, columns):
    product = lax.dot_general(a, b, (dims, ((), ())), preferred_element_type=jnp.float32)
    low = product[:rows, columns:] + product[rows:, :columns]
    return product[:rows, :columns] + (low + product[rows:, columns:])


def params(moved):
    grant = min(VMEM_MOST, max(VMEM_LEAST, 3 * moved))
    return pltpu.CompilerParams(vmem_limit_bytes=grant)


def call(kernel, out_shape, in_specs, flops, moved, scratch=(), out_spec=WHOLE):
    return pl.pallas_call(
        kernel,
        out_shape=out_shape,
        in_specs=in_specs,
        out_specs=jax.tree.map(lambda _: out_spec, out_shape),
        scratch_shapes=scratch,
        compiler_params=params(moved),
        cost_estimate=pl.CostEstimate(flops=flops, bytes_accessed=moved, transcendentals=0),
    )


class Place:
    def __init__(self, geo, order_ref):
        self.geo = geo
        self.a, self.b = lax.axis_index("outer"), lax.axis_index("inner")
        self.first = lax.axis_index("order") * geo.m_local
        self.order_ref = order_ref

    def order(self, m):
        return self.order_ref[self.first + m]

    def outer(self, shift):
        return lax.rem(self.a + (self.geo.outer - shift), self.geo.outer)

    def inner(self, shift):
        return lax.rem(self.b + (self.geo.inner - shift), self.geo.inner)

    def among(self, table, b=None):
        index = self.a * self.geo.inner + (self.b if b is None else b)
        flat = [value for row in table for value in row]
        result = jnp.int32(flat[0])
        for i, value in enumerate(flat[1:], 1):
            result = jnp.where(index == i, jnp.int32(value), result)
        return result


def window_of(geo, leg_ref, m, block):
    start = geo.window_starts[block]
    width = min(geo.window, leg_ref.shape[2] - start)
    piece = leg_ref[m, :, start : start + width]
    if width < geo.window:
        fill = jnp.zeros((piece.shape[0], geo.window - width), jnp.float32)
        piece = jnp.concatenate([piece, fill], axis=1)
    return piece


def cut_windows(geo, leg_ref, *send_refs):
    a = lax.axis_index("outer")
    for shift, ref in enumerate(send_refs, 1):
        for block in range(geo.outer):

            @pl.when(lax.rem(a + shift, geo.outer) == block)
            def _(ref=ref, block=block):
                for m in range(ref.shape[0]):
                    ref[m] = window_of(geo, leg_ref, m, block)


def to_line(stacked):
    rows, width = stacked.shape
    folded = jnp.zeros((rows, LANES), jnp.float32)
    for start in range(0, width, LANES):
        piece = stacked[:, start : min(start + LANES, width)]
        if piece.shape[1] < LANES:
            fill = jnp.zeros((rows, LANES - piece.shape[1]), jnp.float32)
            piece = jnp.concatenate([piece, fill], axis=1)
        folded = folded + piece
    return jnp.sum(jnp.transpose(folded), axis=0, keepdims=True)


def residual_norm(geo, order_ref, res_ref, out_ref):
    place = Place(geo, order_ref)
    m_local, sin_cos, samples, width = res_ref.shape
    total = jnp.zeros((samples, width), jnp.float32)
    for m in range(m_local):
        valid = own_mask(place, m, samples, width)
        for s in range(sin_cos):
            residual = jnp.where(valid, res_ref[m, s], 0.0)
            total = total + residual * residual
    line = to_line(jnp.concatenate([total, jnp.zeros_like(total)], axis=0))
    line = line[:, : out_ref.shape[2]]
    for o in range(out_ref.shape[0]):
        out_ref[o] = jnp.broadcast_to(line, out_ref.shape[1:])


def prepare(geo, order_ref, leg_hbm, *refs):
    parts = refs[: geo.inner]
    out_ref, rows_ref, leg_ref, sem = refs[geo.inner :]
    fetch = pltpu.make_async_copy(leg_hbm, leg_ref, sem)
    fetch.start()
    place = Place(geo, order_ref)
    m_local, sin_cos, samples, width = parts[0].shape
    window = out_ref.shape[2]
    rows = sin_cos * samples
    start = place.among([[s] * geo.inner for s in geo.window_starts])
    degree = start + lax.broadcasted_iota(jnp.int32, (rows, window), 1)
    for m in range(m_local):
        valid = degree >= place.order(m)
        total = None
        for shift, part in enumerate(parts):
            block = part[m].reshape(rows, width)
            block = jnp.concatenate([block, jnp.zeros((rows, window - width), jnp.float32)], axis=1)
            block = pltpu.roll(block, place.among(geo.places, place.inner(shift)), 1)
            total = block if total is None else total + block
        total = jnp.where(valid, total, 0.0)
        hi, lo = split_bf16(total)
        out_ref[m, :rows] = hi
        out_ref[m, rows:] = lo
    fetch.wait()
    for block in range(geo.outer):

        @pl.when(place.a == block)
        def _(block=block):
            for m in range(m_local):
                rows_ref[m] = synthesis(window_of(geo, leg_ref, m, block), out_ref, m)


def synthesis(leg, dir_ref, m):
    rows, line = leg.shape[0], dir_ref.shape[1] // 2
    halves = jnp.concatenate(split_bf16(leg), axis=0)
    return dot_pairs(halves, dir_ref[m], ((1,), (1,)), rows, line)


def synthesise_rest(geo, own_ref, *refs):
    legs, (dir_ref, out_hbm, out_ref, sems) = refs[:-4], refs[-4:]
    place = Place(geo, None)
    rows = out_ref.shape[3]
    copies = []
    for m in range(own_ref.shape[0]):
        for shift in range(geo.outer):
            part = own_ref[m] if shift == 0 else synthesis(legs[shift - 1][m], dir_ref, m)
            a = place.outer(shift)
            for o in range(out_ref.shape[1]):
                out_ref[m, o, a] = part[o * rows : (o + 1) * rows]
        copy = pltpu.make_async_copy(out_ref.at[m], out_hbm.at[:, :, m], sems.at[m])
        copy.start()
        copies.append(copy)
    for copy in copies:
        copy.wait()


def weight_tables(longitudes, period, class_ref, land_ref, value_ref, basis_ref, out_ref):
    classes = class_ref[...]
    on_land = land_ref[...] == 1
    weight = jnp.zeros(classes.shape, jnp.float32)
    for c in range(value_ref.shape[0]):
        value = jnp.where(on_land, value_ref[c, 1], value_ref[c, 0])
        weight = jnp.where(classes == c, value, weight)
    rows = classes.shape[0]
    folded = jnp.zeros((rows, LANES), jnp.float32)
    for start in range(0, longitudes, LANES):
        piece = weight[:, start : min(start + LANES, longitudes)]
        if piece.shape[1] < LANES:
            piece = jnp.concatenate(
                [piece, jnp.zeros((rows, LANES - piece.shape[1]), jnp.float32)], axis=1
            )
        folded = folded + piece
    moments = lax.dot_general(
        folded,
        basis_ref[...],
        (((1,), (0,)), ((), ())),
        precision=HIGHEST,
        preferred_element_type=jnp.float32,
    )
    lane = lax.broadcasted_iota(jnp.int32, (rows, LANES), 1)
    sign = jnp.where(lane < LANES // 2, 1.0, -1.0)
    count = out_ref.shape[1]
    for n in range(count):
        even = jnp.broadcast_to(moments[:, n : n + 1], (rows, LANES))
        odd = jnp.broadcast_to(moments[:, count + n : count + n + 1], (rows, LANES))
        out_ref[0, n] = even
        out_ref[1, n] = sign * even
        out_ref[2, n] = odd
        out_ref[3, n] = sign * odd


def grid_rows(geo, stride, order_ref, recv_ref, table_ref, out_ref, plain, swapped, done):
    orders = plain.shape[0]
    m_local = recv_ref.shape[1]
    slot = [lax.div(order_ref[m], jnp.int32(stride)) for m in range(orders)]
    for m in range(orders):
        o, i = divmod(m, m_local)
        total = recv_ref[o * geo.outer, i]
        for a in range(1, geo.outer):
            total = total + recv_ref[o * geo.outer + a, i]
        at = slot[m]
        plain[at] = total
        swapped[at] = pltpu.roll(total, LANES // 2, 1)
    for i in range(orders):
        total = None
        for j in range(orders):
            cos_part = table_ref[0, abs(i - j)] + table_ref[1, i + j]
            if i >= j:
                sin_part = table_ref[2, i + j] - table_ref[3, i - j]
            else:
                sin_part = table_ref[2, i + j] + table_ref[3, j - i]
            term = cos_part * plain[j] + sin_part * swapped[j]
            total = term if total is None else total + term
        done[i] = total
    copies = geo.outer * geo.inner
    for m in range(orders):
        o, i = divmod(m, m_local)
        value = done[slot[m]]
        for c in range(copies):
            out_ref[o * copies + c, i] = value


def cut_blocks(geo, leg_hbm, *refs):
    legs, outs, (leg_ref, sem) = refs[: geo.outer - 1], refs[geo.outer - 1 : -2], refs[-2:]
    fetch = pltpu.make_async_copy(leg_hbm, leg_ref, sem)
    fetch.start()
    place = Place(geo, None)
    width = geo.block_window

    def each(own):
        for shift, ref in enumerate(outs):
            target = lax.rem(place.b + shift, geo.inner)
            for a in range(geo.outer):
                for b in range(geo.inner):

                    @pl.when((place.a == a) & (target == b))
                    def _(ref=ref, a=a, b=b):
                        start = geo.block_starts[a][b]
                        for m in range(leg_ref.shape[0]):
                            if own:
                                ref[0, m] = window_of(geo, leg_ref, m, a)[:, start : start + width]
                            else:
                                for i, leg in enumerate(legs):
                                    ref[i + 1, m] = leg[m, :, start : start + width]

    each(False)
    fetch.wait()
    each(True)


def own_mask(place, m, rows, width):
    geo = place.geo
    degree = place.among(geo.own_starts) + lax.broadcasted_iota(jnp.int32, (rows, width), 1)
    return degree >= place.order(m)


def project(geo, order_ref, recv_ref, *refs):
    legs = refs[: geo.inner]
    dir_hbm, res_hbm, damp_ref, norm_ref, app_ref, sums_ref, dir_ref, res_ref, sems = refs[geo.inner :]
    fetches = [
        pltpu.make_async_copy(src, dst, sems.at[i])
        for i, (src, dst) in enumerate(((dir_hbm, dir_ref), (res_hbm, res_ref)))
    ]
    for fetch in fetches:
        fetch.start()
    place = Place(geo, order_ref)
    m_local, sin_cos, samples, width = dir_ref.shape
    window = geo.block_window
    copies = geo.outer * geo.inner
    order_devices = recv_ref.shape[0] // copies
    damping = damp_ref[...]
    rows = sin_cos * samples
    offsets = [
        [p - s for p, s in zip(*pair)] for pair in zip(geo.places, geo.block_starts)
    ]
    back = window - place.among(offsets)
    totals = []
    for m in range(m_local):
        tiles, blocks = [], []
        for b in range(geo.inner):
            for a in range(geo.outer):
                band = place.outer(a) * geo.inner + place.inner(b)
                blocks.append(legs[b][a, m])
                for o in range(order_devices):
                    tiles.append(recv_ref[o * copies + band, m])
        hi, lo = split_bf16(jnp.concatenate(tiles, axis=0))
        high, low = split_bf16(jnp.concatenate(blocks, axis=0))
        dims = (((0,), (0,)), ((), ()))
        both = jnp.concatenate([hi, lo], axis=1)
        first = lax.dot_general(both, high, dims, preferred_element_type=jnp.float32)
        second = lax.dot_general(hi, low, dims, preferred_element_type=jnp.float32)
        summed = first[:rows] + (first[rows:] + second)
        totals.append(pltpu.roll(summed, back, 1)[:, :width])
    for fetch in fetches:
        fetch.wait()
    sums = [None] * 3
    for m in range(m_local):
        valid = own_mask(place, m, samples, width)
        for s in range(sin_cos):
            direction = jnp.where(valid, dir_ref[m, s], 0.0)
            residual = jnp.where(valid, res_ref[m, s], 0.0)
            part = totals[m][s * samples : (s + 1) * samples]
            applied = jnp.where(valid, part + damping * direction, 0.0)
            app_ref[m, s] = applied
            terms = (direction * applied, residual * applied, applied * applied)
            sums = [t if old is None else old + t for old, t in zip(sums, terms)]
    norm = jnp.sum(norm_ref[...], axis=0)[0:1, :samples]
    norm = jnp.where(lax.axis_index("order") == 0, norm, 0.0)
    line = to_line(jnp.concatenate(sums + [jnp.zeros_like(sums[0])], axis=0))
    line = jnp.concatenate([line[:, : 3 * samples], norm], axis=1)
    for device in range(sums_ref.shape[0]):
        sums_ref[device] = line


def update(geo, order_ref, sums_ref, app_ref, pos_ref, dir_ref, res_ref, *refs):
    outs, bufs, sems = refs[:3], refs[3:6], refs[6]
    place = Place(geo, order_ref)
    m_local, sin_cos, samples, width = dir_ref.shape
    totals = jnp.sum(sums_ref[...], axis=0)
    curvature, cross, square, before = [
        totals[:, i * samples : (i + 1) * samples] for i in range(4)
    ]
    step_row = before / curvature
    after = before - 2.0 * step_row * cross + step_row * step_row * square
    ratio_row = after / before
    row = lax.broadcasted_iota(jnp.int32, (samples, samples), 0)
    column = lax.broadcasted_iota(jnp.int32, (samples, samples), 1)
    diagonal = row == column
    step = jnp.sum(jnp.where(diagonal, step_row, 0.0), axis=1, keepdims=True)
    ratio = jnp.sum(jnp.where(diagonal, ratio_row, 0.0), axis=1, keepdims=True)
    copies = []
    for m in range(m_local):
        valid = own_mask(place, m, samples, width)
        for s in range(sin_cos):
            direction = jnp.where(valid, dir_ref[m, s], 0.0)
            residual = jnp.where(valid, res_ref[m, s], 0.0)
            position = jnp.where(valid, pos_ref[m, s], 0.0)
            new_residual = residual - step * app_ref[m, s]
            values = (position + step * direction, new_residual, new_residual + ratio * direction)
            for i in range(3):
                bufs[i][m, s] = values[i]
                copy = pltpu.make_async_copy(bufs[i].at[m, s], outs[i].at[m, s], sems.at[i, m, s])
                copy.start()
                copies.append(copy)
    for copy in copies:
        copy.wait()


class Geometry:
    def __init__(self, outer, inner, degrees, m_local):
        self.outer, self.inner, self.m_local = outer, inner, m_local
        block = degrees // (outer * inner)

        def down(x):
            return x // LANES * LANES

        def up(x):
            return -(-x // LANES) * LANES

        own = [[(a * inner + b) * block for b in range(inner)] for a in range(outer)]
        self.own_starts = own
        self.window_starts = [down(row[0]) for row in own]
        self.window = max(
            up(row[-1] + block) - start for row, start in zip(own, self.window_starts)
        )
        self.places = [
            [x - start for x in row] for row, start in zip(own, self.window_starts)
        ]
        self.block_window = max(up(p + block) - down(p) for row in self.places for p in row)
        self.block_starts = [
            [min(down(p), self.window - self.block_window) for p in row] for row in self.places
        ]


def far(x):
    return pltpu.with_memory_space_constraint(x, pltpu.HBM)


def rotate(x, axis, size, shift):
    return lax.ppermute(x, axis, [(i, (i + shift) % size) for i in range(size)])


def plain_grid(geo, grid_in, order_of, class_idx, land, class_weight, period):
    order_devices = grid_in.shape[0] // geo.outer
    m_local, rows, width = grid_in.shape[1:]
    orders = order_devices * m_local
    longitudes = class_idx.shape[1]
    stacked = grid_in.reshape(order_devices, geo.outer, m_local, rows, 2, width // 2)
    stacked = jnp.sum(stacked, axis=1).reshape(orders, rows, 2, width // 2)
    phases = order_of[:, None] * jnp.arange(period, dtype=jnp.int32)[None, :] % longitudes
    angles = phases.astype(jnp.float32) * (2.0 * math.pi / longitudes)
    harmonic = jnp.stack([jnp.cos(angles), jnp.sin(angles)])
    surface = jnp.einsum("mrsk,smp->rkp", stacked, harmonic, precision=HIGHEST)
    onehot = class_idx[:, :, None] == jnp.arange(class_weight.shape[0], dtype=jnp.int32)
    by_class = jnp.dot(onehot.astype(jnp.float32), class_weight, precision=HIGHEST)
    weight = jnp.where(land == 1, by_class[:, :, 1], by_class[:, :, 0])
    folded = jnp.sum(weight.reshape(rows, longitudes // period, period), axis=1)
    weighted = surface * folded[:, None, :]
    spectra = jnp.einsum("rkp,smp->mrsk", weighted, harmonic, precision=HIGHEST)
    spectra = (spectra * (2.0 / longitudes)).reshape(order_devices, 1, m_local, rows, width)
    copies = geo.outer * geo.inner
    spectra = jnp.broadcast_to(spectra, (order_devices, copies, m_local, rows, width))
    return spectra.reshape(order_devices * copies, m_local, rows, width)


def shards(
    outer,
    inner,
    position,
    residual,
    direction,
    legendre,
    order_of,
    class_idx,
    land,
    class_weight,
    damping,
):
    m_local, sin_cos, samples, deg_local = position.shape
    degrees, band_rows = legendre.shape[1:]
    rows_here, longitudes = class_idx.shape
    orders = order_of.shape[0]
    order_devices = orders // m_local
    devices = order_devices * outer * inner
    line = sin_cos * samples
    geo = Geometry(outer, inner, degrees, m_local)
    by_row = jnp.transpose(legendre, (0, 2, 1))
    cut = jax.ShapeDtypeStruct((m_local, band_rows, geo.window), jnp.float32)
    cuts = call(
        functools.partial(cut_windows, geo),
        (cut,) * (outer - 1),
        [WHOLE],
        m_local * band_rows * geo.window,
        8 * outer * m_local * band_rows * geo.window,
    )(by_row)
    received = [rotate(cuts[s - 1], "outer", outer, s) for s in range(1, outer)]
    siblings = [rotate(direction, "inner", inner, s) for s in range(1, inner)]

    norm_lanes = -(-samples // LANES) * LANES
    norm = call(
        functools.partial(residual_norm, geo),
        jax.ShapeDtypeStruct((order_devices, 8, norm_lanes), jnp.float32),
        [SCALARS, WHOLE],
        3 * m_local * line * deg_local,
        4 * m_local * line * deg_local,
    )(order_of, residual)
    norm = lax.all_to_all(norm, "order", split_axis=0, concat_axis=0, tiled=True)

    own_flops = 8 * m_local * line * geo.window * band_rows
    leg_moved = 4 * m_local * band_rows * degrees
    leg_scratch = [pltpu.VMEM(by_row.shape, jnp.float32), pltpu.SemaphoreType.DMA(())]
    dir_window, own_rows = call(
        functools.partial(prepare, geo),
        (
            jax.ShapeDtypeStruct((m_local, 2 * line, geo.window), jnp.bfloat16),
            jax.ShapeDtypeStruct((m_local, band_rows, line), jnp.float32),
        ),
        [SCALARS, IN_HBM] + [WHOLE] * inner,
        own_flops,
        8 * m_local * line * geo.window + leg_moved,
        leg_scratch,
    )(order_of, far(by_row), direction, *siblings)

    stride = longitudes // (2 * orders)
    period = longitudes // stride if longitudes % stride == 0 else longitudes
    small = orders <= 32 and LANES % period == 0 and line == LANES and longitudes % period == 0
    if small:
        count = 2 * orders
        n = np.arange(count)[None, :]
        p = np.arange(LANES)[:, None]
        angle = 2.0 * math.pi * ((n * p) % period) / period
        basis = np.zeros((LANES, -(-2 * count // LANES) * LANES), np.float32)
        basis[:, :count] = np.cos(angle) / longitudes
        basis[:, count : 2 * count] = np.sin(angle) / longitudes
        tables = call(
            functools.partial(weight_tables, longitudes, period),
            jax.ShapeDtypeStruct((4, count, rows_here, LANES), jnp.float32),
            [WHOLE, WHOLE, SCALARS, WHOLE],
            100 * rows_here * longitudes,
            8 * rows_here * longitudes,
        )(class_idx, land, class_weight, jnp.asarray(basis))

    *received, norm = lax.optimization_barrier((*received, norm))
    to_rows = call(
        functools.partial(synthesise_rest, geo),
        pltpu.HBM((order_devices, outer, m_local, rows_here, line), jnp.float32),
        [WHOLE] * (outer + 1),
        own_flops * (outer - 1),
        4 * m_local * (line + band_rows) * geo.window,
        [
            pltpu.VMEM((m_local, order_devices, outer, rows_here, line), jnp.float32),
            pltpu.SemaphoreType.DMA((m_local,)),
        ],
        IN_HBM,
    )(own_rows, *received, dir_window)
    grid_in = lax.all_to_all(
        to_rows.reshape(order_devices * outer, m_local, rows_here, line),
        ("order", "outer"),
        split_axis=0,
        concat_axis=0,
        tiled=True,
    )

    block = jax.ShapeDtypeStruct((outer, m_local, band_rows, geo.block_window), jnp.float32)
    own_block, *blocks = call(
        functools.partial(cut_blocks, geo),
        (block,) * inner,
        [IN_HBM] + [WHOLE] * (outer - 1),
        inner * outer * m_local * band_rows * geo.block_window,
        8 * inner * outer * m_local * band_rows * geo.block_window + leg_moved,
        leg_scratch,
    )(far(by_row), *received)
    from_inner = [rotate(blocks[s - 1], "inner", inner, s) for s in range(1, inner)]

    if small:
        to_orders = call(
            functools.partial(grid_rows, geo, stride),
            jax.ShapeDtypeStruct((devices, m_local, rows_here, line), jnp.float32),
            [SCALARS, WHOLE, WHOLE],
            6 * orders * orders * rows_here * line,
            8 * orders * rows_here * line,
            [pltpu.VMEM((orders, rows_here, line), jnp.float32)] * 3,
        )(order_of, grid_in, tables)
    else:
        to_orders = plain_grid(geo, grid_in, order_of, class_idx, land, class_weight, period)
    spectra = lax.all_to_all(
        to_orders, ("order", "outer", "inner"), split_axis=0, concat_axis=0, tiled=True
    )
    coefficients = jax.ShapeDtypeStruct(position.shape, jnp.float32)
    applied, sums = call(
        functools.partial(project, geo),
        (coefficients, jax.ShapeDtypeStruct((devices, 1, 4 * samples), jnp.float32)),
        [SCALARS] + [WHOLE] * (1 + inner) + [IN_HBM] * 2 + [WHOLE] * 2,
        6 * m_local * line * geo.block_window * band_rows * outer * inner,
        16 * m_local * line * deg_local,
        [pltpu.VMEM(position.shape, jnp.float32)] * 2 + [pltpu.SemaphoreType.DMA((2,))],
    )(order_of, spectra, own_block, *from_inner, far(direction), far(residual), damping[None, :], norm)
    sums = lax.all_to_all(
        sums, ("order", "outer", "inner"), split_axis=0, concat_axis=0, tiled=True
    )
    return call(
        functools.partial(update, geo),
        (coefficients,) * 3,
        [SCALARS] + [WHOLE] * 5,
        10 * m_local * line * deg_local,
        28 * m_local * line * deg_local,
        [pltpu.VMEM(position.shape, jnp.float32)] * 3
        + [pltpu.SemaphoreType.DMA((3, m_local, sin_cos))],
        IN_HBM,
    )(order_of, sums, applied, position, direction, residual)


def solution(mesh):
    order_devices, bands = mesh.shape["order"], mesh.shape["lat"]
    outer = 2 if bands % 2 == 0 else 1
    inner = bands // outer
    split = Mesh(mesh.devices.reshape(order_devices, outer, inner), ("order", "outer", "inner"))
    lat = ("outer", "inner")
    coefficients = P("order", None, None, lat)
    grid = P(("outer", "inner", "order"), None)
    return jax.shard_map(
        functools.partial(shards, outer, inner),
        mesh=split,
        in_specs=(
            coefficients,
            coefficients,
            coefficients,
            P("order", None, lat),
            P(),
            grid,
            grid,
            P(),
            P(lat),
        ),
        out_specs=(coefficients,) * 3,
        check_vma=False,
    )
```

time: 66.9 us -> 65.1 us (0.973)
  waiting for transfers between devices: 23.7 us -> 17.2 us
  starting transfers between devices: 12.8 us -> 18.3 us
  Pallas kernels: 11.7 us -> 15.5 us
  other arithmetic: 3.45 us -> 0 us
  local copies, waits for them, and re-layouts: 4.74 us -> 3.31 us
    ppermute x3, waiting for transfers between devices: 8.69 us -> 0.01 us  [rotate(): return lax.ppermute(x, axis, [(i, (i + shift) % size) for i in range(size)])]
    all_to_all x0 -> x1, starting transfers between devices: none -> 5.81 us  [shards(): lax.all_to_all(norm, 'order', split_axis=0, concat_axis=0, tiled=True)]
    pallas_call x5 -> x6, Pallas kernels: 6.72 us -> 9.27 us  [the longest x1 2.98 us: shards(): call(functools.partial(prepare, geo), (jax.ShapeDtypeStruct((m_local, 2 *...]
    select_n x2 -> x0, other arithmetic: 2.42 us -> none  [the longest x1 2.41 us: pick(): result = jnp.where(index == i, choices[i], result)]
    all_to_all x1, waiting for transfers between devices: 8.16 us -> 10.6 us  [shards(): lax.all_to_all(to_orders, ('order', 'outer', 'inner'), split_axis=0, conc...]
    all_to_all x1, waiting for transfers between devices: 6.84 us -> 4.91 us  [shards(): lax.all_to_all(to_rows.reshape(order_devices * outer, m_local, rows_here,...]
    all_to_all x0 -> x1, waiting for transfers between devices: none -> 1.76 us  [shards(): lax.all_to_all(norm, 'order', split_axis=0, concat_axis=0, tiled=True)]
    pallas_call x1, Pallas kernels: 1.51 us -> 2.58 us  [shards(): call(functools.partial(project, geo), (coefficients, jax.ShapeDtypeStruct...]
  transfers between devices with their start and end apart: 5 -> 6, of which waited for: 3 -> 3; matrix products, arithmetic and copies ran while one was open for 3% -> 0% of each run, Pallas kernels for 9% -> 13%
where the time goes in v2:
time: 65.1 us; the launch traced here: 64.6 us
  starting transfers between devices  18.3 us (28%)
  waiting for transfers between devices  17.2 us (26%)
  Pallas kernels  15.5 us (24%)
  blocking collectives  9.35 us (14%)
  local copies, waits for them, and re-layouts  3.31 us (5%)
  between operations  0.82 us (1%)
    all_to_all x1, waiting for transfers between devices, shards(): lax.all_to_all(to_orders, ('order', 'outer', 'inner'), split_axis=0, conc...  10.6 us
    all_to_all x1, blocking collectives, shards(): lax.all_to_all(sums, ('order', 'outer', 'inner'), split_axis=0, concat_ax...  9.35 us
    all_to_all x1, starting transfers between devices, shards(): lax.all_to_all(to_rows.reshape(order_devices * outer, m_local, rows_here,...  6.92 us
    all_to_all x1, starting transfers between devices, shards(): lax.all_to_all(norm, 'order', split_axis=0, concat_axis=0, tiled=True)  5.81 us
    all_to_all x1, waiting for transfers between devices, shards(): lax.all_to_all(to_rows.reshape(order_devices * outer, m_local, rows_here,...  4.91 us
    unnamed x29, local copies, waits for them, and re-layouts  3.3 us
    ppermute x3, starting transfers between devices, rotate(): return lax.ppermute(x, axis, [(i, (i + shift) % size) for i in range(size)])  3.04 us
    pallas_call x1, Pallas kernels, shards(): call(functools.partial(prepare, geo), (jax.ShapeDtypeStruct((m_local, 2 *...  2.98 us
  transfers between devices with their start and end apart: 6, of which 3 were waited for; matrix products, arithmetic and copies ran while one was open for 0% of the time, Pallas kernels for 13%

profile of v2, /device:TPU:0, one launch (start us, length us, event | category | flops | bytes accessed | tf_op | source)
XLA Modules:
  0.0 64.6 jit_solution(3402737405529917521)
XLA Ops:
  0.6 0.0 copy-start.11
  0.6 0.0 copy-start
  0.7 1.2 %copy-done = f32[2,2160,64]{1,2,0:T(8,128)S(1)} copy-done((f32[2,2160,64]{1,2,0:T(8,128)S(1)}, f32[2,2160,64]{1,2,0:T(8,128)}, u32[]{:S(2)}) %copy-start) | copy-done | bytes 1105944
  1.9 0.0 copy-start.3
  1.9 0.0 copy-start.1
  1.9 0.9 %shard_map.122 = f32[2,64,1152]{2,1,0:T(8,128)} custom-call(f32[2,64,2160]{2,1,0:T(8,128)S(1)} %bitcast.4), custom_call_target="tpu_custom_call" | custom-call | flops 147456 | bytes 2359296 | tf_op jit(solution)/shard_map/pallas_call | solution.py:452
  2.8 3.0 %collective-permute-start.1 = (f32[2,64,1152]{2,1,0:T(8,128)}, f32[2,64,1152]{2,1,0:T(8,128)S(1)}, u32[]{:S(2)}, u32[]{:S(2)}) collective-permute-start(f32[2,64,1152]{2,1,0:T(8,128)} %shard_map.122), channel_id=1, source_target_pairs={{0,2},{2,0},{1,3},{3,1},{4,6},{6,4},{5,7},{7,5},{8,10},{10,8},{9,1... | collective-permute-start | bytes 1769480 | tf_op jit(solution)/shard_map/ppermute | solution.py:403
  5.7 0.0 copy-done.3
  5.7 0.0 collective-permute-start
  5.7 0.0 copy-done.11
  5.7 0.0 copy-done.1
  5.7 1.3 %shard_map.123 = f32[8,8,128]{2,1,0:T(8,128)} custom-call(s32[16]{0:T(128)S(1)} %copy-done.11, f32[2,2,64,540]{3,2,1,0:T(8,128)S(1)} %copy-done.1), custom_call_target="tpu_custom_call" | custom-call | flops 414720 | bytes 552960 | tf_op jit(solution)/shard_map/pallas_call | solution.py:463
  7.1 5.8 %all-to-all-start = ((f32[8,8,128]{2,1,0:T(8,128)}), f32[8,8,128]{2,1,0:T(8,128)S(1)}, u32[]{:S(2)}, u32[]{:S(2)}) async-start(f32[8,8,128]{2,1,0:T(8,128)} %shard_map.123), calls=%async_computation | async-start | bytes 65536 | tf_op jit(solution)/shard_map/all_to_all | solution.py:470
  12.9 0.0 collective-permute-done.refs_1_
  12.9 0.0 copy-start.6
  12.9 0.8 %copy-done.6 = f32[2,2,64,540]{3,2,1,0:T(8,128)} copy-done((f32[2,2,64,540]{3,2,1,0:T(8,128)}, f32[2,2,64,540]{3,2,1,0:T(8,128)S(1)}, u32[]{:S(2)}) %copy-start.6) | copy-done | bytes 552984
  13.7 0.0 copy-start.7
  13.7 1.1 %copy-done.7 = f32[2,2,64,540]{3,2,1,0:T(8,128)S(1)} copy-done((f32[2,2,64,540]{3,2,1,0:T(8,128)S(1)}, f32[2,2,64,540]{3,2,1,0:T(8,128)}, u32[]{:S(2)}) %copy-start.7) | copy-done | bytes 552984
  14.8 3.0 %shard_map.121 = (bf16[2,256,1152]{2,1,0:T(8,128)(2,1)S(1)}, f32[2,64,128]{2,1,0:T(8,128)S(1)}) custom-call(s32[16]{0:T(128)S(1)} %copy-done.11, f32[2,64,2160]{2,1,0:T(8,128)} %bitcast.2, f32[2,2,64,540]{3,2,1,0:T(8,128)S(1)} %copy-done.3, f32[2,2,64,540]{3,2,1,0:T(8,128)S(1)} %copy-done.7), custom_call_target="tpu_custom_call" | custom-call | flops 150994944 | bytes 3465216 | tf_op jit(solution)/shard_map/pallas_call | solution.py:475
  17.8 1.8 %all-to-all-done.refs_5_ = f32[8,8,128]{2,1,0:T(8,128)S(1)} async-done(((f32[8,8,128]{2,1,0:T(8,128)}), f32[8,8,128]{2,1,0:T(8,128)S(1)}, u32[]{:S(2)}, u32[]{:S(2)}) %all-to-all-start) | async-done | bytes 32800 | tf_op jit(solution)/shard_map/all_to_all | solution.py:470
  19.6 0.0 collective-permute-done.1.refs_0_
  19.6 1.2 %shard_map.124 = f32[8,2,2,8,128]{4,3,2,1,0:T(8,128)} custom-call(f32[2,64,128]{2,1,0:T(8,128)S(1)} %get-tuple-element.11.own_ref, f32[2,64,1152]{2,1,0:T(8,128)S(1)} %collective-permute-done.1.refs_0_, bf16[2,256,1152]{2,1,0:T(8,128)(2,1)S(1)} %get-tuple-element.13.refs_1_), custom_call_target="tpu_custom_call" | custom-call | flops 150994944 | bytes 1769472 | tf_op jit(solution)/shard_map/pallas_call | solution.py:507
  20.8 0.0 copy-start.13
  20.8 0.0 copy-start.8
  20.8 0.0 copy-start.9
  20.8 0.0 copy-start.10
  20.8 6.9 %all-to-all-start.1 = ((f32[16,2,8,128]{3,2,1,0:T(8,128)}), f32[16,2,8,128]{3,2,1,0:T(8,128)S(1)}, u32[]{:S(2)}, u32[]{:S(2)}) async-start(f32[16,2,8,128]{3,2,1,0:T(8,128)} %bitcast.5), calls=%async_computation.1 | async-start | bytes 262144 | tf_op jit(solution)/shard_map/all_to_all | solution.py:519
  27.7 1.3 %shard_map.127 = (f32[2,2,64,640]{3,2,1,0:T(8,128)S(1)}, f32[2,2,64,640]{3,2,1,0:T(8,128)S(1)}) custom-call(f32[2,64,2160]{2,1,0:T(8,128)} %bitcast.3, f32[2,64,1152]{2,1,0:T(8,128)S(1)} %collective-permute-done.1.refs_0_), custom_call_target="tpu_custom_call" | custom-call | flops 327680 | bytes 3727360 | tf_op jit(solution)/shard_map/pallas_call | solution.py:528
  29.1 0.0 copy-start.12
  29.1 0.1 collective-permute-start.2
  29.2 0.0 copy-done.13
  29.2 0.1 copy.13.value_ref
  29.3 0.0 copy-done.8
  29.3 0.0 copy-done.9
  29.3 0.0 copy-done.10
  29.3 1.4 %shard_map.125.table_ref = f32[4,32,8,128]{3,2,1,0:T(8,128)S(1)} custom-call(s32[8,4320]{1,0:T(8,128)S(1)} %copy-done.8, s32[8,4320]{1,0:T(8,128)S(1)} %copy-done.9, f32[16,2]{1,0:T(8,128)S(1)} %copy.13.value_ref, f32[128,128]{1,0:T(8,128)S(1)} %copy-done.10), custom_call_target="tpu_custom_call" | custom-call | flops 3456000 | bytes 276480 | tf_op jit(solution)/shard_map/pallas_call | solution.py:498
  30.6 4.9 %all-to-all-done.1.recv_ref = f32[16,2,8,128]{3,2,1,0:T(8,128)S(1)} async-done(((f32[16,2,8,128]{3,2,1,0:T(8,128)}), f32[16,2,8,128]{3,2,1,0:T(8,128)S(1)}, u32[]{:S(2)}, u32[]{:S(2)}) %all-to-all-start.1) | async-done | bytes 131104 | tf_op jit(solution)/shard_map/all_to_all | solution.py:519
  35.5 1.6 %shard_map.126 = f32[32,2,8,128]{3,2,1,0:T(8,128)} custom-call(s32[16]{0:T(128)S(1)} %copy-done.11, f32[16,2,8,128]{3,2,1,0:T(8,128)S(1)} %all-to-all-done.1.recv_ref, f32[4,32,8,128]{3,2,1,0:T(8,128)S(1)} %shard_map.125.table_ref), custom_call_target="tpu_custom_call" | custom-call | flops 1572864 | bytes 131072 | tf_op jit(solution)/shard_map/pallas_call | solution.py:539
  37.1 2.6 %all-to-all-start.2 = ((f32[32,2,8,128]{3,2,1,0:T(8,128)}), f32[32,2,8,128]{3,2,1,0:T(8,128)S(1)}, u32[]{:S(2)}, u32[]{:S(2)}) async-start(f32[32,2,8,128]{3,2,1,0:T(8,128)} %shard_map.126), calls=%async_computation.2 | async-start | bytes 524288 | tf_op jit(solution)/shard_map/all_to_all | solution.py:549
  39.7 0.0 copy-done.12
  39.7 0.0 collective-permute-done.2.refs_1_
  39.8 10.6 %all-to-all-done.2.recv_ref = f32[32,2,8,128]{3,2,1,0:T(8,128)S(1)} async-done(((f32[32,2,8,128]{3,2,1,0:T(8,128)}), f32[32,2,8,128]{3,2,1,0:T(8,128)S(1)}, u32[]{:S(2)}, u32[]{:S(2)}) %all-to-all-start.2) | async-done | bytes 262176 | tf_op jit(solution)/shard_map/all_to_all | solution.py:549
  50.3 0.0 copy-start.2
  50.3 0.0 copy-start.4
  50.3 0.0 copy-start.5
  50.3 2.6 %shard_map.128 = (f32[2,2,64,540]{3,2,1,0:T(8,128)S(1)}, f32[32,1,256]{2,1,0:T(1,128)S(1)}) custom-call(s32[16]{0:T(128)S(1)} %copy-done.11, f32[32,2,8,128]{3,2,1,0:T(8,128)S(1)} %all-to-all-done.2.recv_ref, f32[2,2,64,640]{3,2,1,0:T(8,128)S(1)} %get-tuple-element.14.refs_0_, f32[2,2,64,640]{3,2,1,0:T(8,128)S(1)} %collective-permute-done.2.refs_1_, ...), custom_call_target="tpu_custom_call" | custom-call | flops 251658240 | bytes 2211840 | tf_op jit(solution)/shard_map/pallas_call | solution.py:553
  52.9 9.3 %all_to_all.20.sums_ref = f32[32,1,256]{2,1,0:T(1,128)S(1)} all-to-all(f32[32,1,256]{2,1,0:T(1,128)S(1)} %get-tuple-element.17), channel_id=1, replica_groups=mesh['order'=8,'outer'=2,'inner'=2] {'order','outer','inner'}, dimensions={0} | all-to-all | bytes 65536 | tf_op jit(solution)/shard_map/all_to_all | solution.py:561
  62.3 0.0 copy-done.2
  62.3 0.0 copy-done.4
  62.3 0.0 copy-done.5
  62.3 2.3 %shard_map.129 = (f32[2,2,64,540]{3,2,1,0:T(8,128)}, f32[2,2,64,540]{3,2,1,0:T(8,128)}, f32[2,2,64,540]{3,2,1,0:T(8,128)}) custom-call(s32[16]{0:T(128)S(1)} %copy-done.11, f32[32,1,256]{2,1,0:T(1,128)S(1)} %all_to_all.20.sums_ref, f32[2,2,64,540]{3,2,1,0:T(8,128)S(1)} %get-tuple-element.18.app_ref, f32[2,2,64,540]{3,2,1,0:T(8,128)S(1)} %copy-done.5, ...), custom_call_target="tpu_custom_call" | custom-call | flops 1382400 | bytes 3870720 | tf_op jit(solution)/shard_map/pallas_call | solution.py:564
  (1 shorter events, 0.0 us)
Async XLA Ops:
  0.6 5.1 %copy-start.11 = (s32[16]{0:T(128)S(1)}, s32[16]{0:T(128)}, u32[]{:S(2)}) copy-start(s32[16]{0:T(128)} %order_ref.9) | copy-start | bytes 196
  0.6 1.3 %copy-start = (f32[2,2160,64]{1,2,0:T(8,128)S(1)}, f32[2,2160,64]{1,2,0:T(8,128)}, u32[]{:S(2)}) copy-start(f32[2,2160,64]{1,2,0:T(8,128)} %param.13) | copy-start | bytes 3317764
  1.9 3.8 %copy-start.3 = (f32[2,2,64,540]{3,2,1,0:T(8,128)S(1)}, f32[2,2,64,540]{3,2,1,0:T(8,128)}, u32[]{:S(2)}) copy-start(f32[2,2,64,540]{3,2,1,0:T(8,128)} %dir_ref.1) | copy-start | bytes 1658884
  1.9 3.8 %copy-start.1 = (f32[2,2,64,540]{3,2,1,0:T(8,128)S(1)}, f32[2,2,64,540]{3,2,1,0:T(8,128)}, u32[]{:S(2)}) copy-start(f32[2,2,64,540]{3,2,1,0:T(8,128)} %res_ref.3) | copy-start | bytes 1658884
  2.8 16.8 %collective-permute-start.1 = (f32[2,64,1152]{2,1,0:T(8,128)}, f32[2,64,1152]{2,1,0:T(8,128)S(1)}, u32[]{:S(2)}, u32[]{:S(2)}) collective-permute-start(f32[2,64,1152]{2,1,0:T(8,128)} %shard_map.122), channel_id=1, source_target_pairs={{0,2},{2,0},{1,3},{3,1},{4,6},{6,4},{5,7},{7,5},{8,10},{10,8},{9,1... | collective-permute-start | bytes 1769480 | tf_op jit(solution)/shard_map/ppermute | solution.py:403
  5.7 7.2 %collective-permute-start = (f32[2,2,64,540]{3,2,1,0:T(8,128)S(1)}, f32[2,2,64,540]{3,2,1,0:T(8,128)S(1)}, u32[]{:S(2)}, u32[]{:S(2)}) collective-permute-start(f32[2,2,64,540]{3,2,1,0:T(8,128)S(1)} %copy-done.3), channel_id=1, source_target_pairs={{0,1},{1,0},{2,3},{3,2},{4,5},{5,4},{6,7},{7,6},{8,9},{9,8},{10,11... | collective-permute-start | bytes 1658888 | tf_op jit(solution)/shard_map/ppermute | solution.py:403
  7.1 12.5 %all-to-all-start = ((f32[8,8,128]{2,1,0:T(8,128)}), f32[8,8,128]{2,1,0:T(8,128)S(1)}, u32[]{:S(2)}, u32[]{:S(2)}) async-start(f32[8,8,128]{2,1,0:T(8,128)} %shard_map.123), calls=%async_computation | async-start | bytes 65536 | tf_op jit(solution)/shard_map/all_to_all | solution.py:470
  12.9 0.8 %copy-start.6 = (f32[2,2,64,540]{3,2,1,0:T(8,128)}, f32[2,2,64,540]{3,2,1,0:T(8,128)S(1)}, u32[]{:S(2)}) copy-start(f32[2,2,64,540]{3,2,1,0:T(8,128)S(1)} %collective-permute-done.refs_1_) | copy-start | bytes 1658884
  13.7 1.1 %copy-start.7 = (f32[2,2,64,540]{3,2,1,0:T(8,128)S(1)}, f32[2,2,64,540]{3,2,1,0:T(8,128)}, u32[]{:S(2)}) copy-start(f32[2,2,64,540]{3,2,1,0:T(8,128)} %copy-done.6) | copy-start | bytes 1658884
  20.8 8.4 %copy-start.13 = (f32[16,2]{0,1:T(2,128)S(1)}, f32[16,2]{0,1:T(2,128)}, u32[]{:S(2)}) copy-start(f32[16,2]{0,1:T(2,128)} %param.17) | copy-start | bytes 388
  20.8 8.5 %copy-start.8 = (s32[8,4320]{1,0:T(8,128)S(1)}, s32[8,4320]{1,0:T(8,128)}, u32[]{:S(2)}) copy-start(s32[8,4320]{1,0:T(8,128)} %class_ref.1) | copy-start | bytes 414724
  20.8 8.5 %copy-start.9 = (s32[8,4320]{1,0:T(8,128)S(1)}, s32[8,4320]{1,0:T(8,128)}, u32[]{:S(2)}) copy-start(s32[8,4320]{1,0:T(8,128)} %land_ref.1) | copy-start | bytes 414724
  20.8 8.5 %copy-start.10 = (f32[128,128]{1,0:T(8,128)S(1)}, f32[128,128]{1,0:T(8,128)}, u32[]{:S(2)}) copy-start(f32[128,128]{1,0:T(8,128)} %constant.2.clone.basis_ref) | copy-start | bytes 196612
  20.8 14.7 %all-to-all-start.1 = ((f32[16,2,8,128]{3,2,1,0:T(8,128)}), f32[16,2,8,128]{3,2,1,0:T(8,128)S(1)}, u32[]{:S(2)}, u32[]{:S(2)}) async-start(f32[16,2,8,128]{3,2,1,0:T(8,128)} %bitcast.5), calls=%async_computation.1 | async-start | bytes 262144 | tf_op jit(solution)/shard_map/all_to_all | solution.py:519
  29.1 10.6 %copy-start.12 = (f32[540]{0:T(1024)S(1)}, f32[540]{0:T(1024)}, u32[]{:S(2)}) copy-start(f32[540]{0:T(1024)} %param.18) | copy-start | bytes 6484
  29.1 10.7 %collective-permute-start.2 = (f32[2,2,64,640]{3,2,1,0:T(8,128)S(1)}, f32[2,2,64,640]{3,2,1,0:T(8,128)S(1)}, u32[]{:S(2)}, u32[]{:S(2)}) collective-permute-start(f32[2,2,64,640]{3,2,1,0:T(8,128)S(1)} %get-tuple-element.15), channel_id=1, source_target_pairs={{0,1},{1,0},{2,3},{3,2},{4,5},{5,4},{6,7},{7,6},{8,9},{9,8},{10,11... | collective-permute-start | bytes 1966088 | tf_op jit(solution)/shard_map/ppermute | solution.py:403
  37.1 13.2 %all-to-all-start.2 = ((f32[32,2,8,128]{3,2,1,0:T(8,128)}), f32[32,2,8,128]{3,2,1,0:T(8,128)S(1)}, u32[]{:S(2)}, u32[]{:S(2)}) async-start(f32[32,2,8,128]{3,2,1,0:T(8,128)} %shard_map.126), calls=%async_computation.2 | async-start | bytes 524288 | tf_op jit(solution)/shard_map/all_to_all | solution.py:549
  50.3 11.9 %copy-start.2 = (f32[2,2,64,540]{3,2,1,0:T(8,128)S(1)}, f32[2,2,64,540]{3,2,1,0:T(8,128)}, u32[]{:S(2)}) copy-start(f32[2,2,64,540]{3,2,1,0:T(8,128)} %res_ref.3) | copy-start | bytes 1658884
  50.3 11.9 %copy-start.4 = (f32[2,2,64,540]{3,2,1,0:T(8,128)S(1)}, f32[2,2,64,540]{3,2,1,0:T(8,128)}, u32[]{:S(2)}) copy-start(f32[2,2,64,540]{3,2,1,0:T(8,128)} %dir_ref.1) | copy-start | bytes 1658884
  50.3 11.9 %copy-start.5 = (f32[2,2,64,540]{3,2,1,0:T(8,128)S(1)}, f32[2,2,64,540]{3,2,1,0:T(8,128)}, u32[]{:S(2)}) copy-start(f32[2,2,64,540]{3,2,1,0:T(8,128)} %pos_ref.1) | copy-start | bytes 1658884

commit v3 on v2

v3 whole, which is shorter than its diff:
```python
import functools
import math

import jax
import jax.numpy as jnp
import numpy as np
from jax import lax
from jax.experimental import pallas as pl
from jax.experimental.pallas import tpu as pltpu
from jax.sharding import Mesh
from jax.sharding import PartitionSpec as P

LANES = 128
HIGHEST = lax.Precision.HIGHEST
VMEM_LEAST = 16 * 1024 * 1024
VMEM_MOST = 48 * 1024 * 1024
WHOLE = pl.BlockSpec(memory_space=pltpu.VMEM)
SCALARS = pl.BlockSpec(memory_space=pltpu.SMEM)
IN_HBM = pl.BlockSpec(memory_space=pltpu.HBM)


def repeat(count, body):
    lax.fori_loop(0, count, lambda i, carry: (body(i), carry)[1], 0)


def split_bf16(x):
    hi = x.astype(jnp.bfloat16)
    lo = (x - hi.astype(jnp.float32)).astype(jnp.bfloat16)
    return hi, lo


def dot_pairs(a, b, dims, rows, columns):
    product = lax.dot_general(a, b, (dims, ((), ())), preferred_element_type=jnp.float32)
    low = product[:rows, columns:] + product[rows:, :columns]
    return product[:rows, :columns] + (low + product[rows:, columns:])


def params(moved):
    grant = min(VMEM_MOST, max(VMEM_LEAST, 3 * moved))
    return pltpu.CompilerParams(vmem_limit_bytes=grant)


def call(kernel, out_shape, in_specs, flops, moved, scratch=(), out_spec=WHOLE):
    return pl.pallas_call(
        kernel,
        out_shape=out_shape,
        in_specs=in_specs,
        out_specs=jax.tree.map(lambda _: out_spec, out_shape),
        scratch_shapes=scratch,
        compiler_params=params(moved),
        cost_estimate=pl.CostEstimate(flops=flops, bytes_accessed=moved, transcendentals=0),
    )


class Place:
    def __init__(self, geo, order_ref):
        self.geo = geo
        self.a, self.b = lax.axis_index("outer"), lax.axis_index("inner")
        self.first = lax.axis_index("order") * geo.m_local
        self.order_ref = order_ref

    def order(self, m):
        return self.order_ref[self.first + m]

    def outer(self, shift):
        return lax.rem(self.a + (self.geo.outer - shift), self.geo.outer)

    def inner(self, shift):
        return lax.rem(self.b + (self.geo.inner - shift), self.geo.inner)

    def among(self, table, b=None):
        index = self.a * self.geo.inner + (self.b if b is None else b)
        return choose(index, [value for row in table for value in row])


def choose(index, values):
    result = jnp.int32(values[0])
    for i, value in enumerate(values[1:], 1):
        result = jnp.where(index == i, jnp.int32(value), result)
    return result


def take(leg_ref, m, index, starts, width):
    degrees = leg_ref.shape[2]
    start = pl.multiple_of(choose(index, starts), LANES)
    last = None
    for i, first in enumerate(starts):
        first = first + width - LANES
        tile = leg_ref[m, :, first : min(first + LANES, degrees)]
        if tile.shape[1] < LANES:
            fill = jnp.zeros((tile.shape[0], LANES - tile.shape[1]), jnp.float32)
            tile = jnp.concatenate([tile, fill], axis=1)
        last = tile if last is None else jnp.where(index == i, tile, last)
    return jnp.concatenate([leg_ref[m, :, pl.ds(start, width - LANES)], last], axis=1)


def lane_start(place, table, b=None):
    return pl.multiple_of(place.among(table, b), LANES)


def cut_windows(geo, leg_hbm, *refs):
    send_refs, (leg_ref, sem) = refs[:-2], refs[-2:]
    fetch = pltpu.make_async_copy(leg_hbm, leg_ref, sem)
    fetch.start()
    a = lax.axis_index("outer")
    fetch.wait()
    for shift, ref in enumerate(send_refs, 1):
        block = lax.rem(a + shift, geo.outer)

        def one(m, ref=ref, block=block):
            ref[m] = take(leg_ref, m, block, geo.window_starts, geo.window)

        repeat(ref.shape[0], one)


def fold(x):
    rows, width = x.shape
    folded = None
    for start in range(0, width, LANES):
        piece = x[:, start : min(start + LANES, width)]
        if piece.shape[1] < LANES:
            fill = jnp.zeros((rows, LANES - piece.shape[1]), jnp.float32)
            piece = jnp.concatenate([piece, fill], axis=1)
        folded = piece if folded is None else folded + piece
    return folded


def to_line(folded):
    return jnp.sum(jnp.transpose(folded), axis=0, keepdims=True)


def prepare(geo, order_ref, leg_hbm, *refs):
    parts = refs[: geo.inner]
    out_ref, rows_ref, *cuts, leg_ref, sem = refs[geo.inner :]
    fetch = pltpu.make_async_copy(leg_hbm, leg_ref, sem)
    fetch.start()
    place = Place(geo, order_ref)
    m_local, sin_cos, samples, width = parts[0].shape
    window = out_ref.shape[2]
    line = sin_cos * samples
    start = place.among([[s] * geo.inner for s in geo.window_starts])
    piece = 16
    steps = samples // piece
    shifts = [place.among(geo.places, place.inner(shift)) for shift in range(geo.inner)]
    degree = start + lax.broadcasted_iota(jnp.int32, (piece, window), 1)

    def one(i):
        m, rest = lax.div(i, sin_cos * steps), lax.rem(i, sin_cos * steps)
        s, k = lax.div(rest, steps), lax.rem(rest, steps) * piece
        total = None
        for shift, part in zip(shifts, parts):
            block = part[m, s, pl.ds(pl.multiple_of(k, piece), piece), :]
            fill = jnp.zeros((piece, window - width), jnp.float32)
            block = pltpu.roll(jnp.concatenate([block, fill], axis=1), shift, 1)
            total = block if total is None else total + block
        total = jnp.where(degree >= place.order(m), total, 0.0)
        hi, lo = split_bf16(total)
        at = rest * piece
        out_ref[m, pl.ds(pl.multiple_of(at, piece), piece)] = hi
        out_ref[m, pl.ds(pl.multiple_of(line + at, piece), piece)] = lo

    repeat(m_local * sin_cos * steps, one)
    fetch.wait()

    def rows(m):
        leg = take(leg_ref, m, place.a, geo.window_starts, window)
        rows_ref[m] = synthesis(leg, out_ref, m)
        for shift, ref in enumerate(cuts):
            index = place.a * geo.inner + lax.rem(place.b + shift, geo.inner)
            ref[m] = take(leg_ref, m, index, geo.row_starts, geo.block_window)

    repeat(m_local, rows)


def synthesis(leg, dir_ref, m):
    rows, line = leg.shape[0], dir_ref.shape[1] // 2
    halves = jnp.concatenate(split_bf16(leg), axis=0)
    return dot_pairs(halves, dir_ref[m], ((1,), (1,)), rows, line)


def synthesise_rest(geo, own_ref, *refs):
    others = geo.outer - 1
    legs, (dir_ref, out_ref, *cuts) = refs[:others], refs[others:]
    place = Place(geo, None)
    rows = out_ref.shape[3]
    starts = [
        lane_start(place, geo.block_starts, lax.rem(place.b + shift, geo.inner))
        for shift in range(geo.inner)
    ]

    def put(m, shift, part):
        a = place.outer(shift)
        for o in range(out_ref.shape[0]):
            out_ref[o, a, m] = part[o * rows : (o + 1) * rows]

    def one(m):
        put(m, 0, own_ref[m])
        for shift in range(1, geo.outer):
            put(m, shift, synthesis(legs[shift - 1][m], dir_ref, m))
            for start, ref in zip(starts, cuts):
                ref[shift - 1, m] = legs[shift - 1][m, :, pl.ds(start, geo.block_window)]

    repeat(own_ref.shape[0], one)


def weight_tables(longitudes, period, class_ref, land_ref, value_ref, basis_ref, out_ref):
    classes = class_ref[...]
    on_land = land_ref[...] == 1
    weight = jnp.zeros(classes.shape, jnp.float32)
    for c in range(value_ref.shape[0]):
        value = jnp.where(on_land, value_ref[c, 1], value_ref[c, 0])
        weight = jnp.where(classes == c, value, weight)
    rows = classes.shape[0]
    folded = jnp.zeros((rows, LANES), jnp.float32)
    for start in range(0, longitudes, LANES):
        piece = weight[:, start : min(start + LANES, longitudes)]
        if piece.shape[1] < LANES:
            piece = jnp.concatenate(
                [piece, jnp.zeros((rows, LANES - piece.shape[1]), jnp.float32)], axis=1
            )
        folded = folded + piece
    moments = lax.dot_general(
        folded,
        basis_ref[...],
        (((1,), (0,)), ((), ())),
        precision=HIGHEST,
        preferred_element_type=jnp.float32,
    )
    lane = lax.broadcasted_iota(jnp.int32, (rows, LANES), 1)
    sign = jnp.where(lane < LANES // 2, 1.0, -1.0)
    count = out_ref.shape[1]
    for n in range(count):
        even = jnp.broadcast_to(moments[:, n : n + 1], (rows, LANES))
        odd = jnp.broadcast_to(moments[:, count + n : count + n + 1], (rows, LANES))
        out_ref[0, n] = even
        out_ref[1, n] = sign * even
        out_ref[2, n] = odd
        out_ref[3, n] = sign * odd


def grid_rows(geo, stride, order_ref, recv_ref, table_ref, out_ref, plain, swapped, done):
    orders = plain.shape[0]
    m_local, each = recv_ref.shape[1], out_ref.shape[1]
    slot = [lax.div(order_ref[m], jnp.int32(stride)) for m in range(orders)]
    for m in range(orders):
        o, i = divmod(m, m_local)
        total = recv_ref[o * geo.outer, i]
        for a in range(1, geo.outer):
            total = total + recv_ref[o * geo.outer + a, i]
        at = slot[m]
        plain[at] = total
        swapped[at] = pltpu.roll(total, LANES // 2, 1)
    for i in range(orders):
        total = None
        for j in range(orders):
            cos_part = table_ref[0, abs(i - j)] + table_ref[1, i + j]
            if i >= j:
                sin_part = table_ref[2, i + j] - table_ref[3, i - j]
            else:
                sin_part = table_ref[2, i + j] + table_ref[3, j - i]
            term = cos_part * plain[j] + sin_part * swapped[j]
            total = term if total is None else total + term
        done[i] = total
    for m in range(orders):
        o, i = divmod(m, m_local)
        b, i = divmod(i, each)
        value = done[slot[m]]
        for a in range(geo.outer):
            out_ref[(o * geo.outer + a) * geo.inner + b, i] = value


def own_mask(place, m, rows, width):
    geo = place.geo
    degree = place.among(geo.own_starts) + lax.broadcasted_iota(jnp.int32, (rows, width), 1)
    return degree >= place.order(m)


def project(geo, shift, order_ref, recv_ref, *refs):
    legs, refs = refs[: 2 * geo.inner], refs[2 * geo.inner :]
    dir_ref, res_ref, damp_ref = refs[:3]
    before_ref = refs[3] if shift else None
    app_ref, sums_ref = refs[-2:]
    place = Place(geo, order_ref)
    each, sin_cos, samples, width = app_ref.shape
    first = place.inner(shift) * each
    window = geo.block_window
    copies = geo.outer * geo.inner
    order_devices = recv_ref.shape[0] // copies
    damping = damp_ref[...]
    rows = sin_cos * samples
    offsets = [
        [p - s for p, s in zip(*pair)] for pair in zip(geo.places, geo.block_starts)
    ]
    back = window - place.among(offsets)

    def products(i):
        tiles, blocks = [], []
        for b in range(geo.inner):
            for a in range(geo.outer):
                band = place.outer(a) * geo.inner + place.inner(b)
                if a == 0:
                    blocks.append(legs[b][first + i])
                else:
                    blocks.append(legs[geo.inner + b][a - 1, first + i])
                for o in range(order_devices):
                    tiles.append(recv_ref[o * copies + band, i])
        hi, lo = split_bf16(jnp.concatenate(tiles, axis=0))
        high, low = split_bf16(jnp.concatenate(blocks, axis=0))
        dims = (((0,), (0,)), ((), ()))
        both = jnp.concatenate([hi, lo], axis=1)
        main = lax.dot_general(both, high, dims, preferred_element_type=jnp.float32)
        rest = lax.dot_general(hi, low, dims, preferred_element_type=jnp.float32)
        summed = main[:rows] + (main[rows:] + rest)
        summed = pltpu.roll(summed, back, 1)[:, :width]
        for s in range(sin_cos):
            app_ref[i, s] = summed[s * samples : (s + 1) * samples]

    repeat(each, products)

    def apply(at, sums):
        i, s = lax.div(at, sin_cos), lax.rem(at, sin_cos)
        valid = own_mask(place, first + i, samples, width)
        direction = jnp.where(valid, dir_ref[first + i, s], 0.0)
        residual = jnp.where(valid, res_ref[first + i, s], 0.0)
        applied = jnp.where(valid, app_ref[i, s] + damping * direction, 0.0)
        app_ref[i, s] = applied
        terms = (
            residual * residual,
            direction * applied,
            residual * applied,
            applied * applied,
        )
        return tuple(old + fold(t) for old, t in zip(sums, terms))

    if shift:
        start = tuple(before_ref[i * samples : (i + 1) * samples] for i in range(4))
    else:
        start = (jnp.zeros((samples, LANES), jnp.float32),) * 4
    sums = lax.fori_loop(0, each * sin_cos, apply, start)
    stacked = jnp.concatenate(sums, axis=0)
    if shift < geo.inner - 1:
        sums_ref[...] = stacked
    else:
        line = to_line(stacked)

        def give(device):
            sums_ref[device] = line

        repeat(sums_ref.shape[0], give)


def update(geo, order_ref, sums_ref, *refs):
    apps, refs = refs[: geo.inner], refs[geo.inner :]
    pos_ref, dir_ref, res_ref, *refs = refs
    outs, bufs, sems = refs[:3], refs[3:6], refs[6]
    place = Place(geo, order_ref)
    m_local, sin_cos, samples, width = dir_ref.shape
    totals = jnp.sum(sums_ref[...], axis=0)
    before, curvature, cross, square = [
        totals[:, i * samples : (i + 1) * samples] for i in range(4)
    ]
    step_row = before / curvature
    after = before - 2.0 * step_row * cross + step_row * step_row * square
    ratio_row = after / before
    row = lax.broadcasted_iota(jnp.int32, (samples, samples), 0)
    column = lax.broadcasted_iota(jnp.int32, (samples, samples), 1)
    diagonal = row == column
    step = jnp.sum(jnp.where(diagonal, step_row, 0.0), axis=1, keepdims=True)
    ratio = jnp.sum(jnp.where(diagonal, ratio_row, 0.0), axis=1, keepdims=True)

    def copy(i, m, s):
        return pltpu.make_async_copy(bufs[i].at[m, s], outs[i].at[m, s], sems.at[i, m, s])

    each = m_local // geo.inner
    for shift, app_ref in enumerate(apps):

        def one(at, shift=shift, app_ref=app_ref):
            i, s = lax.div(at, sin_cos), lax.rem(at, sin_cos)
            m = place.inner(shift) * each + i
            valid = own_mask(place, m, samples, width)
            direction = jnp.where(valid, dir_ref[m, s], 0.0)
            residual = jnp.where(valid, res_ref[m, s], 0.0)
            position = jnp.where(valid, pos_ref[m, s], 0.0)
            new_residual = residual - step * app_ref[i, s]
            values = (
                position + step * direction,
                new_residual,
                new_residual + ratio * direction,
            )
            for i in range(3):
                bufs[i][m, s] = values[i]
                copy(i, m, s).start()

        repeat(each * sin_cos, one)

    def end(at):
        for i in range(3):
            copy(i, lax.div(at, sin_cos), lax.rem(at, sin_cos)).wait()

    repeat(m_local * sin_cos, end)


class Geometry:
    def __init__(self, outer, inner, degrees, m_local):
        self.outer, self.inner, self.m_local = outer, inner, m_local
        block = degrees // (outer * inner)

        def down(x):
            return x // LANES * LANES

        def up(x):
            return -(-x // LANES) * LANES

        own = [[(a * inner + b) * block for b in range(inner)] for a in range(outer)]
        self.own_starts = own
        self.window_starts = [down(row[0]) for row in own]
        self.window = max(
            up(row[-1] + block) - start for row, start in zip(own, self.window_starts)
        )
        self.places = [
            [x - start for x in row] for row, start in zip(own, self.window_starts)
        ]
        self.block_window = max(up(p + block) - down(p) for row in self.places for p in row)
        self.block_starts = [
            [min(down(p), self.window - self.block_window) for p in row] for row in self.places
        ]
        self.row_starts = [
            w + s for w, row in zip(self.window_starts, self.block_starts) for s in row
        ]


def far(x):
    return pltpu.with_memory_space_constraint(x, pltpu.HBM)


def rotate(x, axis, size, shift):
    return lax.ppermute(x, axis, [(i, (i + shift) % size) for i in range(size)])


def plain_grid(geo, grid_in, order_of, class_idx, land, class_weight, period):
    order_devices = grid_in.shape[0] // geo.outer
    m_local, rows, width = grid_in.shape[1:]
    orders = order_devices * m_local
    longitudes = class_idx.shape[1]
    stacked = grid_in.reshape(order_devices, geo.outer, m_local, rows, 2, width // 2)
    stacked = jnp.sum(stacked, axis=1).reshape(orders, rows, 2, width // 2)
    phases = order_of[:, None] * jnp.arange(period, dtype=jnp.int32)[None, :] % longitudes
    angles = phases.astype(jnp.float32) * (2.0 * math.pi / longitudes)
    harmonic = jnp.stack([jnp.cos(angles), jnp.sin(angles)])
    surface = jnp.einsum("mrsk,smp->rkp", stacked, harmonic, precision=HIGHEST)
    onehot = class_idx[:, :, None] == jnp.arange(class_weight.shape[0], dtype=jnp.int32)
    by_class = jnp.dot(onehot.astype(jnp.float32), class_weight, precision=HIGHEST)
    weight = jnp.where(land == 1, by_class[:, :, 1], by_class[:, :, 0])
    folded = jnp.sum(weight.reshape(rows, longitudes // period, period), axis=1)
    weighted = surface * folded[:, None, :]
    spectra = jnp.einsum("rkp,smp->mrsk", weighted, harmonic, precision=HIGHEST)
    each = m_local // geo.inner
    spectra = spectra * (2.0 / longitudes)
    spectra = spectra.reshape(order_devices, 1, geo.inner, each, rows, width)
    spectra = jnp.broadcast_to(
        spectra, (order_devices, geo.outer, geo.inner, each, rows, width)
    )
    return spectra.reshape(order_devices * geo.outer * geo.inner, each, rows, width)


def shards(
    outer,
    inner,
    position,
    residual,
    direction,
    legendre,
    order_of,
    class_idx,
    land,
    class_weight,
    damping,
):
    m_local, sin_cos, samples, deg_local = position.shape
    degrees, band_rows = legendre.shape[1:]
    rows_here, longitudes = class_idx.shape
    orders = order_of.shape[0]
    order_devices = orders // m_local
    devices = order_devices * outer * inner
    each = m_local // inner
    line = sin_cos * samples
    geo = Geometry(outer, inner, degrees, m_local)
    by_row = jnp.transpose(legendre, (0, 2, 1))
    cut = pltpu.VMEM((m_local, band_rows, geo.window), jnp.float32)
    leg_moved = 4 * m_local * band_rows * degrees
    leg_scratch = [pltpu.VMEM(by_row.shape, jnp.float32), pltpu.SemaphoreType.DMA(())]
    cuts = call(
        functools.partial(cut_windows, geo),
        (cut,) * (outer - 1),
        [IN_HBM],
        m_local * band_rows * geo.window,
        8 * outer * m_local * band_rows * geo.window,
        leg_scratch,
    )(far(by_row))
    received = [rotate(cuts[s - 1], "outer", outer, s) for s in range(1, outer)]
    stride = longitudes // (2 * orders)
    period = longitudes // stride if longitudes % stride == 0 else longitudes
    small = orders <= 16 and LANES % period == 0 and line == LANES and longitudes % period == 0
    if small:
        count = 2 * orders
        n = np.arange(count)[None, :]
        p = np.arange(LANES)[:, None]
        angle = 2.0 * math.pi * ((n * p) % period) / period
        basis = np.zeros((LANES, -(-2 * count // LANES) * LANES), np.float32)
        basis[:, :count] = np.cos(angle) / longitudes
        basis[:, count : 2 * count] = np.sin(angle) / longitudes
        tables = call(
            functools.partial(weight_tables, longitudes, period),
            jax.ShapeDtypeStruct((4, count, rows_here, LANES), jnp.float32),
            [WHOLE, WHOLE, SCALARS, WHOLE],
            100 * rows_here * longitudes,
            8 * rows_here * longitudes,
        )(class_idx, land, class_weight, jnp.asarray(basis))

    siblings = [rotate(direction, "inner", inner, s) for s in range(1, inner)]
    if small:
        siblings, tables = lax.optimization_barrier((siblings, tables))
    own_flops = 8 * m_local * line * geo.window * band_rows
    dir_window, own_rows, *own_blocks = call(
        functools.partial(prepare, geo),
        (
            jax.ShapeDtypeStruct((m_local, 2 * line, geo.window), jnp.bfloat16),
            jax.ShapeDtypeStruct((m_local, band_rows, line), jnp.float32),
        )
        + (jax.ShapeDtypeStruct((m_local, band_rows, geo.block_window), jnp.float32),) * inner,
        [SCALARS, IN_HBM] + [WHOLE] * inner,
        own_flops,
        8 * m_local * line * geo.window + leg_moved,
        leg_scratch,
    )(order_of, far(by_row), direction, *siblings)
    first_legs = [own_blocks[0]]
    first_legs += [rotate(own_blocks[s], "inner", inner, s) for s in range(1, inner)]

    received, first_legs = lax.optimization_barrier((received, first_legs))
    block = jax.ShapeDtypeStruct((outer - 1, m_local, band_rows, geo.block_window), jnp.float32)
    to_rows, *blocks = call(
        functools.partial(synthesise_rest, geo),
        (jax.ShapeDtypeStruct((order_devices, outer, m_local, rows_here, line), jnp.float32),)
        + (block,) * inner,
        [WHOLE] * (outer + 1),
        own_flops * (outer - 1),
        4 * m_local * (line + band_rows) * geo.window,
    )(own_rows, *received, dir_window)
    rest_legs = [blocks[0]]
    rest_legs += [rotate(blocks[s], "inner", inner, s) for s in range(1, inner)]
    grid_in = lax.all_to_all(
        to_rows.reshape(order_devices * outer, m_local, rows_here, line),
        ("order", "outer"),
        split_axis=0,
        concat_axis=0,
        tiled=True,
    )

    grid_in, rest_legs = lax.optimization_barrier((grid_in, rest_legs))
    if small:
        to_orders = call(
            functools.partial(grid_rows, geo, stride),
            jax.ShapeDtypeStruct((devices, each, rows_here, line), jnp.float32),
            [SCALARS, WHOLE, WHOLE],
            6 * orders * orders * rows_here * line,
            8 * orders * rows_here * line,
            [pltpu.VMEM((orders, rows_here, line), jnp.float32)] * 3,
        )(order_of, grid_in, tables)
    else:
        to_orders = plain_grid(geo, grid_in, order_of, class_idx, land, class_weight, period)
    spectra = lax.all_to_all(
        to_orders, ("order", "outer", "inner"), split_axis=0, concat_axis=0, tiled=True
    )
    shares = [spectra] + [rotate(spectra, "inner", inner, s) for s in range(1, inner)]
    coefficients = jax.ShapeDtypeStruct(position.shape, jnp.float32)
    part = (each,) + position.shape[1:]
    sums = ()
    applied = []
    for shift, share in enumerate(shares):
        if shift < inner - 1:
            sums_out = jax.ShapeDtypeStruct((4 * samples, LANES), jnp.float32)
        else:
            sums_out = jax.ShapeDtypeStruct((devices, 1, 4 * samples), jnp.float32)
        result, sums = call(
            functools.partial(project, geo, shift),
            (jax.ShapeDtypeStruct(part, jnp.float32), sums_out),
            [SCALARS] + [WHOLE] * (4 + 2 * inner + (shift > 0)),
            6 * each * line * geo.block_window * band_rows * outer * inner,
            16 * each * line * deg_local,
        )(
            order_of,
            share,
            *first_legs,
            *rest_legs,
            direction,
            residual,
            damping[None, :],
            *((sums,) if shift else ()),
        )
        applied.append(result)
    sums = lax.all_to_all(
        sums, ("order", "outer", "inner"), split_axis=0, concat_axis=0, tiled=True
    )
    return call(
        functools.partial(update, geo),
        (coefficients,) * 3,
        [SCALARS] + [WHOLE] * (4 + inner),
        10 * m_local * line * deg_local,
        28 * m_local * line * deg_local,
        [pltpu.VMEM(position.shape, jnp.float32)] * 3
        + [pltpu.SemaphoreType.DMA((3, m_local, sin_cos))],
        IN_HBM,
    )(order_of, sums, *applied, position, direction, residual)


def solution(mesh):
    order_devices, bands = mesh.shape["order"], mesh.shape["lat"]
    outer = 2 if bands % 2 == 0 else 1
    inner = bands // outer
    split = Mesh(mesh.devices.reshape(order_devices, outer, inner), ("order", "outer", "inner"))
    lat = ("outer", "inner")
    coefficients = P("order", None, None, lat)
    grid = P(("outer", "inner", "order"), None)
    return jax.shard_map(
        functools.partial(shards, outer, inner),
        mesh=split,
        in_specs=(
            coefficients,
            coefficients,
            coefficients,
            P("order", None, lat),
            P(),
            grid,
            grid,
            P(),
            P(lat),
        ),
        out_specs=(coefficients,) * 3,
        check_vma=False,
    )
```

time: 65.1 us -> 60.3 us (0.926)
  blocking collectives: 9.35 us -> 34.1 us
  starting transfers between devices: 18.3 us -> 3.68 us
  waiting for transfers between devices: 17.2 us -> 8.99 us
  local copies, waits for them, and re-layouts: 3.31 us -> 0.13 us
  Pallas kernels: 15.5 us -> 12.4 us
    all_to_all x0 -> x2, blocking collectives: none -> 25.2 us  [the longest x1 15 us: shards(): lax.all_to_all(to_rows.reshape(order_devices * outer, m_local, rows_here,...]
    all_to_all x3 -> x0, waiting for transfers between devices: 17.2 us -> none  [the longest x1 10.6 us: shards(): lax.all_to_all(to_orders, ('order', 'outer', 'inner'), split_axis=0, conc...]
    all_to_all x3 -> x0, starting transfers between devices: 15.3 us -> none  [the longest x1 6.92 us: shards(): lax.all_to_all(to_rows.reshape(order_devices * outer, m_local, rows_here,...]
    ppermute x3 -> x5, waiting for transfers between devices: 0.01 us -> 8.99 us  [rotate(): return lax.ppermute(x, axis, [(i, (i + shift) % size) for i in range(size)])]
    unnamed x29 -> x19, local copies, waits for them, and re-layouts: 3.3 us -> 0.12 us
    pallas_call x5 -> x4, Pallas kernels: 7.28 us -> 4.81 us  [the longest x2 2.71 us: shards(): call(functools.partial(project, geo, shift), (jax.ShapeDtypeStruct(part,...]
    pallas_call x1, Pallas kernels: 1.58 us -> 0.87 us  [shards(): call(functools.partial(grid_rows, geo, stride), jax.ShapeDtypeStruct((dev...]
    ppermute x3 -> x5, starting transfers between devices: 3.04 us -> 3.68 us  [rotate(): return lax.ppermute(x, axis, [(i, (i + shift) % size) for i in range(size)])]
  transfers between devices with their start and end apart: 6 -> 5, of which waited for: 3 -> 1; matrix products, arithmetic and copies ran while one was open for 0% -> 0% of each run, Pallas kernels for 13% -> 12%
where the time goes in v3:
time: 60.3 us; the launch traced here: 60.1 us
  blocking collectives  34.1 us (57%)
  Pallas kernels  12.4 us (21%)
  waiting for transfers between devices  8.99 us (15%)
  starting transfers between devices  3.68 us (6%)
  between operations  0.77 us (1%)
    all_to_all x1, blocking collectives, shards(): lax.all_to_all(to_rows.reshape(order_devices * outer, m_local, rows_here,...  15 us
    all_to_all x1, blocking collectives, shards(): lax.all_to_all(to_orders, ('order', 'outer', 'inner'), split_axis=0, conc...  10.2 us
    ppermute x5, waiting for transfers between devices, rotate(): return lax.ppermute(x, axis, [(i, (i + shift) % size) for i in range(size)])  8.99 us
    all_to_all x1, blocking collectives, shards(): lax.all_to_all(sums, ('order', 'outer', 'inner'), split_axis=0, concat_ax...  8.95 us
    ppermute x5, starting transfers between devices, rotate(): return lax.ppermute(x, axis, [(i, (i + shift) % size) for i in range(size)])  3.68 us
    pallas_call x1, Pallas kernels, shards(): call(functools.partial(prepare, geo), (jax.ShapeDtypeStruct((m_local, 2 *...  3.23 us
    pallas_call x2, Pallas kernels, shards(): call(functools.partial(project, geo, shift), (jax.ShapeDtypeStruct(part,...  2.71 us
    pallas_call x1, Pallas kernels, shards(): call(functools.partial(update, geo), (coefficients,) * 3, [SCALARS] + [WH...  2.15 us
  transfers between devices with their start and end apart: 5, of which 1 were waited for; matrix products, arithmetic and copies ran while one was open for 0% of the time, Pallas kernels for 12%

profile of v3, /device:TPU:0, one launch (start us, length us, event | category | flops | bytes accessed | tf_op | source)
XLA Modules:
  0.0 60.1 jit_solution(11026429248738107828)
XLA Ops:
  0.6 0.0 copy-start.5
  0.6 0.0 copy-start.8
  0.7 0.0 copy-start.3
  0.7 0.0 copy-start.4
  0.7 0.5 collective-permute-start
  1.2 0.0 copy-start
  1.2 0.0 copy-start.6
  1.2 1.4 %shard_map.123 = f32[2,64,1152]{2,1,0:T(8,128)S(1)} custom-call(f32[2,64,2160]{2,1,0:T(8,128)} %bitcast.3), custom_call_target="tpu_custom_call" | custom-call | flops 147456 | bytes 2359296 | tf_op jit(solution)/shard_map/pallas_call | solution.py:492
  2.6 2.6 %collective-permute-start.1 = (f32[2,64,1152]{2,1,0:T(8,128)S(1)}, f32[2,64,1152]{2,1,0:T(8,128)S(1)}, u32[]{:S(2)}, u32[]{:S(2)}) collective-permute-start(f32[2,64,1152]{2,1,0:T(8,128)S(1)} %shard_map.123), channel_id=1, source_target_pairs={{0,2},{2,0},{1,3},{3,1},{4,6},{6,4},{5,7},{7,5},{8,10},{10,8},{9,1... | collective-permute-start | bytes 1769480 | tf_op jit(solution)/shard_map/ppermute | solution.py:437
  5.2 0.0 copy-done.8
  5.2 0.1 copy.13.value_ref
  5.3 0.0 copy-done.5
  5.3 0.0 copy-done.3
  5.3 0.0 copy-done.4
  5.3 1.4 %shard_map.121.table_ref = f32[4,32,8,128]{3,2,1,0:T(8,128)S(1)} custom-call(s32[8,4320]{1,0:T(8,128)S(1)} %copy-done.3, s32[8,4320]{1,0:T(8,128)S(1)} %copy-done.4, f32[16,2]{1,0:T(8,128)S(1)} %copy.13.value_ref, f32[128,128]{1,0:T(8,128)S(1)} %copy-done.5), custom_call_target="tpu_custom_call" | custom-call | flops 3456000 | bytes 276480 | tf_op jit(solution)/shard_map/pallas_call | solution.py:512
  6.7 0.0 collective-permute-done.refs_1_
  6.7 0.0 copy-done
  6.7 0.0 copy-done.6
  6.7 3.2 %shard_map.122 = (bf16[2,256,1152]{2,1,0:T(8,128)(2,1)S(1)}, f32[2,64,128]{2,1,0:T(8,128)S(1)}, f32[2,64,640]{2,1,0:T(8,128)S(1)}, f32[2,64,640]{2,1,0:T(8,128)S(1)}) custom-call(s32[16]{0:T(128)S(1)} %copy-done.6, f32[2,64,2160]{2,1,0:T(8,128)} %bitcast.4, f32[2,2,64,540]{3,2,1,0:T(8,128)S(1)} %copy-done, f32[2,2,64,540]{3,2,1,0:T(8,128)S(1)} %collective-permute-done.refs_1_), custom_call_target="tpu_custom_call" | custom-call | flops 150994944 | bytes 3465216 | tf_op jit(solution)/shard_map/pallas_call | solution.py:524
  9.9 0.2 collective-permute-start.2
  10.2 9.0 %collective-permute-done.1.refs_0_ = f32[2,64,1152]{2,1,0:T(8,128)S(1)} collective-permute-done((f32[2,64,1152]{2,1,0:T(8,128)S(1)}, f32[2,64,1152]{2,1,0:T(8,128)S(1)}, u32[]{:S(2)}, u32[]{:S(2)}) %collective-permute-start.1) | collective-permute-done | bytes 589856 | tf_op jit(solution)/shard_map/ppermute | solution.py:437
  19.2 0.0 collective-permute-done.2.refs_1_
  19.2 0.0 copy-start.7
  19.2 0.0 copy-start.1
  19.2 0.7 %shard_map.124 = (f32[8,2,2,8,128]{4,3,2,1,0:T(8,128)S(1)}, f32[1,2,64,640]{3,2,1,0:T(8,128)S(1)}, f32[1,2,64,640]{3,2,1,0:T(8,128)S(1)}) custom-call(f32[2,64,128]{2,1,0:T(8,128)S(1)} %get-tuple-element.23.own_ref, f32[2,64,1152]{2,1,0:T(8,128)S(1)} %collective-permute-done.1.refs_0_, bf16[2,256,1152]{2,1,0:T(8,128)(2,1)S(1)} %get-tuple-element.27.refs_1_), custom_call_target="tpu_custom_call" | custom-call | flops 150994944 | bytes 1769472 | tf_op jit(solution)/shard_map/pallas_call | solution.py:541
  19.9 0.1 collective-permute-start.3
  20.0 15.0 %all_to_all.15.recv_ref = f32[16,2,8,128]{3,2,1,0:T(8,128)S(1)} all-to-all(f32[16,2,8,128]{3,2,1,0:T(8,128)S(1)} %bitcast.2), channel_id=1, replica_groups=mesh['order'=8,'outer'=2,'inner'=2] {'order','outer'}, dimensions={0} | all-to-all | bytes 262144 | tf_op jit(solution)/shard_map/all_to_all | solution.py:551
  35.0 0.0 collective-permute-done.3.refs_3_
  35.0 0.9 %shard_map.125 = f32[32,1,8,128]{3,2,1,0:T(8,128)S(1)} custom-call(s32[16]{0:T(128)S(1)} %copy-done.6, f32[16,2,8,128]{3,2,1,0:T(8,128)S(1)} %all_to_all.15.recv_ref, f32[4,32,8,128]{3,2,1,0:T(8,128)S(1)} %shard_map.121.table_ref), custom_call_target="tpu_custom_call" | custom-call | flops 1572864 | bytes 131072 | tf_op jit(solution)/shard_map/pallas_call | solution.py:561
  35.8 10.2 %all_to_all.16.recv_ref = f32[32,1,8,128]{3,2,1,0:T(8,128)S(1)} all-to-all(f32[32,1,8,128]{3,2,1,0:T(8,128)S(1)} %shard_map.125), channel_id=1, replica_groups=mesh['order'=8,'outer'=2,'inner'=2] {'order','outer','inner'}, dimensions={0} | all-to-all | bytes 262144 | tf_op jit(solution)/shard_map/all_to_all | solution.py:571
  46.0 0.2 collective-permute-start.4
  46.2 0.0 copy-done.7
  46.2 0.0 copy-done.1
  46.2 1.2 %shard_map.126 = (f32[1,2,64,540]{3,2,1,0:T(8,128)S(1)}, f32[256,128]{1,0:T(8,128)S(1)}) custom-call(s32[16]{0:T(128)S(1)} %copy-done.6, f32[32,1,8,128]{3,2,1,0:T(8,128)S(1)} %all_to_all.16.recv_ref, f32[2,64,640]{2,1,0:T(8,128)S(1)} %get-tuple-element.33.refs_0_, f32[2,64,640]{2,1,0:T(8,128)S(1)} %collective-permute-done.2.refs_1_, ...), custom_call_target="tpu_custom_call" | custom-call | flops 125829120 | bytes 1105920 | tf_op jit(solution)/shard_map/pallas_call | solution.py:584
  47.5 0.0 collective-permute-done.4.recv_ref
  47.5 0.0 copy-start.2
  47.5 1.5 %shard_map.127 = (f32[1,2,64,540]{3,2,1,0:T(8,128)S(1)}, f32[32,1,256]{2,1,0:T(1,128)S(1)}) custom-call(s32[16]{0:T(128)S(1)} %copy-done.6, f32[32,1,8,128]{3,2,1,0:T(8,128)S(1)} %collective-permute-done.4.recv_ref, f32[2,64,640]{2,1,0:T(8,128)S(1)} %get-tuple-element.33.refs_0_, f32[2,64,640]{2,1,0:T(8,128)S(1)} %collective-permute-done.2.refs_1_, ...), custom_call_target="tpu_custom_call" | custom-call | flops 125829120 | bytes 1105920 | tf_op jit(solution)/shard_map/pallas_call | solution.py:584
  49.0 9.0 %all_to_all.17.sums_ref = f32[32,1,256]{2,1,0:T(1,128)S(1)} all-to-all(f32[32,1,256]{2,1,0:T(1,128)S(1)} %get-tuple-element.38), channel_id=1, replica_groups=mesh['order'=8,'outer'=2,'inner'=2] {'order','outer','inner'}, dimensions={0} | all-to-all | bytes 65536 | tf_op jit(solution)/shard_map/all_to_all | solution.py:601
  57.9 0.0 copy-done.2
  58.0 2.1 %shard_map.128 = (f32[2,2,64,540]{3,2,1,0:T(8,128)}, f32[2,2,64,540]{3,2,1,0:T(8,128)}, f32[2,2,64,540]{3,2,1,0:T(8,128)}) custom-call(s32[16]{0:T(128)S(1)} %copy-done.6, f32[32,1,256]{2,1,0:T(1,128)S(1)} %all_to_all.17.sums_ref, f32[1,2,64,540]{3,2,1,0:T(8,128)S(1)} %get-tuple-element.39.refs_0_, f32[1,2,64,540]{3,2,1,0:T(8,128)S(1)} %get-tuple-element.40.refs_1_, ...), custom_call_target="tpu_custom_call" | custom-call | flops 1382400 | bytes 3870720 | tf_op jit(solution)/shard_map/pallas_call | solution.py:604
  (1 shorter events, 0.0 us)
Async XLA Ops:
  0.6 4.7 %copy-start.5 = (f32[128,128]{1,0:T(8,128)S(1)}, f32[128,128]{1,0:T(8,128)}, u32[]{:S(2)}) copy-start(f32[128,128]{1,0:T(8,128)} %constant.2.clone.basis_ref) | copy-start | bytes 196612
  0.6 4.6 %copy-start.8 = (f32[16,2]{0,1:T(2,128)S(1)}, f32[16,2]{0,1:T(2,128)}, u32[]{:S(2)}) copy-start(f32[16,2]{0,1:T(2,128)} %param.17) | copy-start | bytes 388
  0.7 4.6 %copy-start.3 = (s32[8,4320]{1,0:T(8,128)S(1)}, s32[8,4320]{1,0:T(8,128)}, u32[]{:S(2)}) copy-start(s32[8,4320]{1,0:T(8,128)} %class_ref.1) | copy-start | bytes 414724
  0.7 4.6 %copy-start.4 = (s32[8,4320]{1,0:T(8,128)S(1)}, s32[8,4320]{1,0:T(8,128)}, u32[]{:S(2)}) copy-start(s32[8,4320]{1,0:T(8,128)} %land_ref.1) | copy-start | bytes 414724
  0.7 6.0 %collective-permute-start = (f32[2,2,64,540]{3,2,1,0:T(8,128)}, f32[2,2,64,540]{3,2,1,0:T(8,128)S(1)}, u32[]{:S(2)}, u32[]{:S(2)}) collective-permute-start(f32[2,2,64,540]{3,2,1,0:T(8,128)} %refs_3_.1), channel_id=1, source_target_pairs={{0,1},{1,0},{2,3},{3,2},{4,5},{5,4},{6,7},{7,6},{8,9},{9,8},{10,11... | collective-permute-start | bytes 1658888 | tf_op jit(solution)/shard_map/ppermute | solution.py:437
  1.2 5.5 %copy-start = (f32[2,2,64,540]{3,2,1,0:T(8,128)S(1)}, f32[2,2,64,540]{3,2,1,0:T(8,128)}, u32[]{:S(2)}) copy-start(f32[2,2,64,540]{3,2,1,0:T(8,128)} %refs_3_.1) | copy-start | bytes 1658884
  1.2 5.5 %copy-start.6 = (s32[16]{0:T(128)S(1)}, s32[16]{0:T(128)}, u32[]{:S(2)}) copy-start(s32[16]{0:T(128)} %order_ref.9) | copy-start | bytes 196
  2.6 16.6 %collective-permute-start.1 = (f32[2,64,1152]{2,1,0:T(8,128)S(1)}, f32[2,64,1152]{2,1,0:T(8,128)S(1)}, u32[]{:S(2)}, u32[]{:S(2)}) collective-permute-start(f32[2,64,1152]{2,1,0:T(8,128)S(1)} %shard_map.123), channel_id=1, source_target_pairs={{0,2},{2,0},{1,3},{3,1},{4,6},{6,4},{5,7},{7,5},{8,10},{10,8},{9,1... | collective-permute-start | bytes 1769480 | tf_op jit(solution)/shard_map/ppermute | solution.py:437
  9.9 9.2 %collective-permute-start.2 = (f32[2,64,640]{2,1,0:T(8,128)S(1)}, f32[2,64,640]{2,1,0:T(8,128)S(1)}, u32[]{:S(2)}, u32[]{:S(2)}) collective-permute-start(f32[2,64,640]{2,1,0:T(8,128)S(1)} %get-tuple-element.25), channel_id=1, source_target_pairs={{0,1},{1,0},{2,3},{3,2},{4,5},{5,4},{6,7},{7,6},{8,9},{9,8},{10,11... | collective-permute-start | bytes 983048 | tf_op jit(solution)/shard_map/ppermute | solution.py:437
  19.2 27.1 %copy-start.7 = (f32[540]{0:T(1024)S(1)}, f32[540]{0:T(1024)}, u32[]{:S(2)}) copy-start(f32[540]{0:T(1024)} %param.18) | copy-start | bytes 6484
  19.2 27.1 %copy-start.1 = (f32[2,2,64,540]{3,2,1,0:T(8,128)S(1)}, f32[2,2,64,540]{3,2,1,0:T(8,128)}, u32[]{:S(2)}) copy-start(f32[2,2,64,540]{3,2,1,0:T(8,128)} %refs_4_.5) | copy-start | bytes 1658884
  19.9 15.1 %collective-permute-start.3 = (f32[1,2,64,640]{3,2,1,0:T(8,128)S(1)}, f32[1,2,64,640]{3,2,1,0:T(8,128)S(1)}, u32[]{:S(2)}, u32[]{:S(2)}) collective-permute-start(f32[1,2,64,640]{3,2,1,0:T(8,128)S(1)} %get-tuple-element.30), channel_id=1, source_target_pairs={{0,1},{1,0},{2,3},{3,2},{4,5},{5,4},{6,7},{7,6},{8,9},{9,8},{10,11... | collective-permute-start | bytes 983048 | tf_op jit(solution)/shard_map/ppermute | solution.py:437
  46.0 1.4 %collective-permute-start.4 = (f32[32,1,8,128]{3,2,1,0:T(8,128)S(1)}, f32[32,1,8,128]{3,2,1,0:T(8,128)S(1)}, u32[]{:S(2)}, u32[]{:S(2)}) collective-permute-start(f32[32,1,8,128]{3,2,1,0:T(8,128)S(1)} %all_to_all.16.recv_ref), channel_id=1, source_target_pairs={{0,1},{1,0},{2,3},{3,2},{4,5},{5,4},{6,7},{7,6},{8,9},{9,8},{10,11... | collective-permute-start | bytes 393224 | tf_op jit(solution)/shard_map/ppermute | solution.py:437
  47.5 10.5 %copy-start.2 = (f32[2,2,64,540]{3,2,1,0:T(8,128)S(1)}, f32[2,2,64,540]{3,2,1,0:T(8,128)}, u32[]{:S(2)}) copy-start(f32[2,2,64,540]{3,2,1,0:T(8,128)} %refs_2_.1) | copy-start | bytes 1658884

commit v4 on v3

--- a/solution.py
+++ b/solution.py
@@ -94,8 +94,18 @@
     return jnp.concatenate([leg_ref[m, :, pl.ds(start, width - LANES)], last], axis=1)
 
 
-def lane_start(place, table, b=None):
-    return pl.multiple_of(place.among(table, b), LANES)
+def exact_window(geo, leg_ref, m, block):
+    wide = take(leg_ref, m, block, geo.window_starts, geo.take_width)
+    back = lax.rem(geo.take_width - choose(block, geo.window_shifts), geo.take_width)
+    return pltpu.roll(wide, back, 1)[:, : geo.window]
+
+
+def inner_block(geo, window, target):
+    result = None
+    for b, start in enumerate(geo.block_starts):
+        piece = window[:, start : start + geo.block_window]
+        result = piece if result is None else jnp.where(target == b, piece, result)
+    return result
 
 
 def cut_windows(geo, leg_hbm, *refs):
@@ -104,13 +114,35 @@
     fetch.start()
     a = lax.axis_index("outer")
     fetch.wait()
+    m_local, rows = leg_ref.shape[:2]
+    lane = lax.broadcasted_iota(jnp.int32, (rows, LANES), 1)
     for shift, ref in enumerate(send_refs, 1):
         block = lax.rem(a + shift, geo.outer)
-
-        def one(m, ref=ref, block=block):
-            ref[m] = take(leg_ref, m, block, geo.window_starts, geo.window)
-
-        repeat(ref.shape[0], one)
+        tiles = [None] * geo.rest_tiles
+        for m in range(m_local):
+            window = exact_window(geo, leg_ref, m, block)
+            ref[:, m * geo.main : (m + 1) * geo.main] = window[:, : geo.main]
+            if geo.rest:
+                at, place = divmod(m, geo.rest_each)
+                tile = jnp.where(lane < geo.rest, window[:, geo.main :], 0.0)
+                if place:
+                    tile = pltpu.roll(tile, place * geo.rest, 1)
+                tiles[at] = tile if tiles[at] is None else tiles[at] + tile
+        for i, tile in enumerate(tiles):
+            start = m_local * geo.main + i * LANES
+            ref[:, start : start + LANES] = tile
+
+
+def unpack_window(geo, ref, m):
+    window = ref[:, m * geo.main : (m + 1) * geo.main]
+    if geo.rest:
+        at, place = divmod(m, geo.rest_each)
+        start = geo.m_local * geo.main + at * LANES
+        tile = ref[:, start : start + LANES]
+        if place:
+            tile = pltpu.roll(tile, LANES - place * geo.rest, 1)
+        window = jnp.concatenate([window, tile], axis=1)
+    return window
 
 
 def fold(x):
@@ -138,10 +170,10 @@
     m_local, sin_cos, samples, width = parts[0].shape
     window = out_ref.shape[2]
     line = sin_cos * samples
-    start = place.among([[s] * geo.inner for s in geo.window_starts])
+    start = place.a * geo.pair
     piece = 16
     steps = samples // piece
-    shifts = [place.among(geo.places, place.inner(shift)) for shift in range(geo.inner)]
+    shifts = [choose(place.inner(shift), geo.places) for shift in range(geo.inner)]
     degree = start + lax.broadcasted_iota(jnp.int32, (piece, window), 1)
 
     def one(i):
@@ -163,11 +195,10 @@
     fetch.wait()
 
     def rows(m):
-        leg = take(leg_ref, m, place.a, geo.window_starts, window)
+        leg = exact_window(geo, leg_ref, m, place.a)
         rows_ref[m] = synthesis(leg, out_ref, m)
         for shift, ref in enumerate(cuts):
-            index = place.a * geo.inner + lax.rem(place.b + shift, geo.inner)
-            ref[m] = take(leg_ref, m, index, geo.row_starts, geo.block_window)
+            ref[m] = inner_block(geo, leg, lax.rem(place.b + shift, geo.inner))
 
     repeat(m_local, rows)
 
@@ -183,24 +214,19 @@
     legs, (dir_ref, out_ref, *cuts) = refs[:others], refs[others:]
     place = Place(geo, None)
     rows = out_ref.shape[3]
-    starts = [
-        lane_start(place, geo.block_starts, lax.rem(place.b + shift, geo.inner))
-        for shift in range(geo.inner)
-    ]
 
     def put(m, shift, part):
         a = place.outer(shift)
         for o in range(out_ref.shape[0]):
             out_ref[o, a, m] = part[o * rows : (o + 1) * rows]
 
-    def one(m):
+    for m in range(own_ref.shape[0]):
         put(m, 0, own_ref[m])
         for shift in range(1, geo.outer):
-            put(m, shift, synthesis(legs[shift - 1][m], dir_ref, m))
-            for start, ref in zip(starts, cuts):
-                ref[shift - 1, m] = legs[shift - 1][m, :, pl.ds(start, geo.block_window)]
-
-    repeat(own_ref.shape[0], one)
+            leg = unpack_window(geo, legs[shift - 1], m)
+            put(m, shift, synthesis(leg, dir_ref, m))
+            for ahead, ref in enumerate(cuts):
+                ref[shift - 1, m] = inner_block(geo, leg, lax.rem(place.b + ahead, geo.inner))
 
 
 def weight_tables(longitudes, period, class_ref, land_ref, value_ref, basis_ref, out_ref):
@@ -288,10 +314,8 @@
     order_devices = recv_ref.shape[0] // copies
     damping = damp_ref[...]
     rows = sin_cos * samples
-    offsets = [
-        [p - s for p, s in zip(*pair)] for pair in zip(geo.places, geo.block_starts)
-    ]
-    back = window - place.among(offsets)
+    offsets = [p - s for p, s in zip(geo.places, geo.block_starts)]
+    back = window - choose(place.b, offsets)
 
     def products(i):
         tiles, blocks = [], []
@@ -411,22 +435,21 @@
         def up(x):
             return -(-x // LANES) * LANES
 
-        own = [[(a * inner + b) * block for b in range(inner)] for a in range(outer)]
-        self.own_starts = own
-        self.window_starts = [down(row[0]) for row in own]
-        self.window = max(
-            up(row[-1] + block) - start for row, start in zip(own, self.window_starts)
-        )
-        self.places = [
-            [x - start for x in row] for row, start in zip(own, self.window_starts)
-        ]
-        self.block_window = max(up(p + block) - down(p) for row in self.places for p in row)
-        self.block_starts = [
-            [min(down(p), self.window - self.block_window) for p in row] for row in self.places
-        ]
-        self.row_starts = [
-            w + s for w, row in zip(self.window_starts, self.block_starts) for s in row
-        ]
+        pair = degrees // outer
+        self.pair = pair
+        self.own_starts = [[(a * inner + b) * block for b in range(inner)] for a in range(outer)]
+        self.window_starts = [down(a * pair) for a in range(outer)]
+        self.window_shifts = [a * pair - s for a, s in enumerate(self.window_starts)]
+        self.take_width = max(up(s + pair) for s in self.window_shifts)
+        self.window = up(pair)
+        self.places = [b * block for b in range(inner)]
+        self.block_window = max(up(p + block) - down(p) for p in self.places)
+        self.block_starts = [min(down(p), self.window - self.block_window) for p in self.places]
+        self.main = down(pair)
+        self.rest = pair - self.main
+        self.rest_each = LANES // self.rest if self.rest else 1
+        self.rest_tiles = -(-m_local // self.rest_each) if self.rest else 0
+        self.packed = m_local * self.main + self.rest_tiles * LANES
 
 
 def far(x):
@@ -486,7 +509,7 @@
     line = sin_cos * samples
     geo = Geometry(outer, inner, degrees, m_local)
     by_row = jnp.transpose(legendre, (0, 2, 1))
-    cut = pltpu.VMEM((m_local, band_rows, geo.window), jnp.float32)
+    cut = pltpu.VMEM((band_rows, geo.packed), jnp.float32)
     leg_moved = 4 * m_local * band_rows * degrees
     leg_scratch = [pltpu.VMEM(by_row.shape, jnp.float32), pltpu.SemaphoreType.DMA(())]
     cuts = call(

time: 60.3 us -> 59.7 us (0.990)
  waiting for transfers between devices: 8.99 us -> 8.2 us
    ppermute x5, waiting for transfers between devices: 8.99 us -> 8.2 us  [rotate(): return lax.ppermute(x, axis, [(i, (i + shift) % size) for i in range(size)])]
  transfers between devices with their start and end apart: 5 -> 5, of which waited for: 1 -> 1; matrix products, arithmetic and copies ran while one was open for 0% -> 0% of each run, Pallas kernels for 12% -> 13%
where the time goes in v4:
time: 59.7 us; the launch traced here: 59.5 us
  blocking collectives  34.1 us (57%)
  Pallas kernels  12.6 us (21%)
  waiting for transfers between devices  8.2 us (14%)
  starting transfers between devices  3.68 us (6%)
  between operations  0.77 us (1%)
    all_to_all x1, blocking collectives, shards(): lax.all_to_all(to_rows.reshape(order_devices * outer, m_local, rows_here,...  15 us
    all_to_all x1, blocking collectives, shards(): lax.all_to_all(to_orders, ('order', 'outer', 'inner'), split_axis=0, conc...  10.2 us
    all_to_all x1, blocking collectives, shards(): lax.all_to_all(sums, ('order', 'outer', 'inner'), split_axis=0, concat_ax...  8.95 us
    ppermute x5, waiting for transfers between devices, rotate(): return lax.ppermute(x, axis, [(i, (i + shift) % size) for i in range(size)])  8.2 us
    ppermute x5, starting transfers between devices, rotate(): return lax.ppermute(x, axis, [(i, (i + shift) % size) for i in range(size)])  3.68 us
    pallas_call x1, Pallas kernels, shards(): call(functools.partial(prepare, geo), (jax.ShapeDtypeStruct((m_local, 2 *...  3.32 us
    pallas_call x2, Pallas kernels, shards(): call(functools.partial(project, geo, shift), (jax.ShapeDtypeStruct(part,...  2.7 us
    pallas_call x1, Pallas kernels, shards(): call(functools.partial(update, geo), (coefficients,) * 3, [SCALARS] + [WH...  2.15 us
  transfers between devices with their start and end apart: 5, of which 1 were waited for; matrix products, arithmetic and copies ran while one was open for 0% of the time, Pallas kernels for 13%

profile of v4, /device:TPU:0, one launch (start us, length us, event | category | flops | bytes accessed | tf_op | source)
XLA Modules:
  0.0 59.5 jit_solution(960377173381053044)
XLA Ops:
  0.6 0.0 copy-start.5
  0.6 0.0 copy-start.8
  0.7 0.0 copy-start.3
  0.7 0.0 copy-start.4
  0.7 0.5 collective-permute-start
  1.2 0.0 copy-start
  1.2 0.0 copy-start.6
  1.2 1.7 %shard_map.123 = f32[64,2176]{1,0:T(8,128)S(1)} custom-call(f32[2,64,2160]{2,1,0:T(8,128)} %bitcast.3), custom_call_target="tpu_custom_call" | custom-call | flops 147456 | bytes 2359296 | tf_op jit(solution)/shard_map/pallas_call | solution.py:515
  2.9 2.6 %collective-permute-start.1 = (f32[64,2176]{1,0:T(8,128)S(1)}, f32[64,2176]{1,0:T(8,128)S(1)}, u32[]{:S(2)}, u32[]{:S(2)}) collective-permute-start(f32[64,2176]{1,0:T(8,128)S(1)} %shard_map.123), channel_id=1, source_target_pairs={{0,2},{2,0},{1,3},{3,1},{4,6},{6,4},{5,7},{7,5},{8,10},{10,8},{9,1... | collective-permute-start | bytes 1671176 | tf_op jit(solution)/shard_map/ppermute | solution.py:460
  5.5 0.0 copy-done.8
  5.5 0.1 copy.13.value_ref
  5.6 0.0 copy-done.5
  5.6 0.0 copy-done.3
  5.6 0.0 copy-done.4
  5.6 1.4 %shard_map.121.table_ref = f32[4,32,8,128]{3,2,1,0:T(8,128)S(1)} custom-call(s32[8,4320]{1,0:T(8,128)S(1)} %copy-done.3, s32[8,4320]{1,0:T(8,128)S(1)} %copy-done.4, f32[16,2]{1,0:T(8,128)S(1)} %copy.13.value_ref, f32[128,128]{1,0:T(8,128)S(1)} %copy-done.5), custom_call_target="tpu_custom_call" | custom-call | flops 3456000 | bytes 276480 | tf_op jit(solution)/shard_map/pallas_call | solution.py:535
  6.9 0.0 collective-permute-done.refs_1_
  7.0 0.0 copy-done
  7.0 0.0 copy-done.6
  7.0 3.3 %shard_map.122 = (bf16[2,256,1152]{2,1,0:T(8,128)(2,1)S(1)}, f32[2,64,128]{2,1,0:T(8,128)S(1)}, f32[2,64,640]{2,1,0:T(8,128)S(1)}, f32[2,64,640]{2,1,0:T(8,128)S(1)}) custom-call(s32[16]{0:T(128)S(1)} %copy-done.6, f32[2,64,2160]{2,1,0:T(8,128)} %bitcast.4, f32[2,2,64,540]{3,2,1,0:T(8,128)S(1)} %copy-done, f32[2,2,64,540]{3,2,1,0:T(8,128)S(1)} %collective-permute-done.refs_1_), custom_call_target="tpu_custom_call" | custom-call | flops 150994944 | bytes 3465216 | tf_op jit(solution)/shard_map/pallas_call | solution.py:547
  10.3 0.2 collective-permute-start.2
  10.5 8.2 %collective-permute-done.1.refs_0_ = f32[64,2176]{1,0:T(8,128)S(1)} collective-permute-done((f32[64,2176]{1,0:T(8,128)S(1)}, f32[64,2176]{1,0:T(8,128)S(1)}, u32[]{:S(2)}, u32[]{:S(2)}) %collective-permute-start.1) | collective-permute-done | bytes 557088 | tf_op jit(solution)/shard_map/ppermute | solution.py:460
  18.7 0.0 collective-permute-done.2.refs_1_
  18.7 0.0 copy-start.7
  18.7 0.0 copy-start.1
  18.7 0.5 shard_map.124
  19.3 0.1 collective-permute-start.3
  19.4 15.0 %all_to_all.15.recv_ref = f32[16,2,8,128]{3,2,1,0:T(8,128)S(1)} all-to-all(f32[16,2,8,128]{3,2,1,0:T(8,128)S(1)} %bitcast.2), channel_id=1, replica_groups=mesh['order'=8,'outer'=2,'inner'=2] {'order','outer'}, dimensions={0} | all-to-all | bytes 262144 | tf_op jit(solution)/shard_map/all_to_all | solution.py:574
  34.3 0.0 collective-permute-done.3.refs_3_
  34.3 0.9 %shard_map.125 = f32[32,1,8,128]{3,2,1,0:T(8,128)S(1)} custom-call(s32[16]{0:T(128)S(1)} %copy-done.6, f32[16,2,8,128]{3,2,1,0:T(8,128)S(1)} %all_to_all.15.recv_ref, f32[4,32,8,128]{3,2,1,0:T(8,128)S(1)} %shard_map.121.table_ref), custom_call_target="tpu_custom_call" | custom-call | flops 1572864 | bytes 131072 | tf_op jit(solution)/shard_map/pallas_call | solution.py:584
  35.2 10.2 %all_to_all.16.recv_ref = f32[32,1,8,128]{3,2,1,0:T(8,128)S(1)} all-to-all(f32[32,1,8,128]{3,2,1,0:T(8,128)S(1)} %shard_map.125), channel_id=1, replica_groups=mesh['order'=8,'outer'=2,'inner'=2] {'order','outer','inner'}, dimensions={0} | all-to-all | bytes 262144 | tf_op jit(solution)/shard_map/all_to_all | solution.py:594
  45.4 0.2 collective-permute-start.4
  45.6 0.0 copy-done.7
  45.6 0.0 copy-done.1
  45.6 1.2 %shard_map.126 = (f32[1,2,64,540]{3,2,1,0:T(8,128)S(1)}, f32[256,128]{1,0:T(8,128)S(1)}) custom-call(s32[16]{0:T(128)S(1)} %copy-done.6, f32[32,1,8,128]{3,2,1,0:T(8,128)S(1)} %all_to_all.16.recv_ref, f32[2,64,640]{2,1,0:T(8,128)S(1)} %get-tuple-element.33.refs_0_, f32[2,64,640]{2,1,0:T(8,128)S(1)} %collective-permute-done.2.refs_1_, ...), custom_call_target="tpu_custom_call" | custom-call | flops 125829120 | bytes 1105920 | tf_op jit(solution)/shard_map/pallas_call | solution.py:607
  46.9 0.0 collective-permute-done.4.recv_ref
  46.9 0.0 copy-start.2
  46.9 1.5 %shard_map.127 = (f32[1,2,64,540]{3,2,1,0:T(8,128)S(1)}, f32[32,1,256]{2,1,0:T(1,128)S(1)}) custom-call(s32[16]{0:T(128)S(1)} %copy-done.6, f32[32,1,8,128]{3,2,1,0:T(8,128)S(1)} %collective-permute-done.4.recv_ref, f32[2,64,640]{2,1,0:T(8,128)S(1)} %get-tuple-element.33.refs_0_, f32[2,64,640]{2,1,0:T(8,128)S(1)} %collective-permute-done.2.refs_1_, ...), custom_call_target="tpu_custom_call" | custom-call | flops 125829120 | bytes 1105920 | tf_op jit(solution)/shard_map/pallas_call | solution.py:607
  48.4 9.0 %all_to_all.17.sums_ref = f32[32,1,256]{2,1,0:T(1,128)S(1)} all-to-all(f32[32,1,256]{2,1,0:T(1,128)S(1)} %get-tuple-element.38), channel_id=1, replica_groups=mesh['order'=8,'outer'=2,'inner'=2] {'order','outer','inner'}, dimensions={0} | all-to-all | bytes 65536 | tf_op jit(solution)/shard_map/all_to_all | solution.py:624
  57.3 0.0 copy-done.2
  57.3 2.1 %shard_map.128 = (f32[2,2,64,540]{3,2,1,0:T(8,128)}, f32[2,2,64,540]{3,2,1,0:T(8,128)}, f32[2,2,64,540]{3,2,1,0:T(8,128)}) custom-call(s32[16]{0:T(128)S(1)} %copy-done.6, f32[32,1,256]{2,1,0:T(1,128)S(1)} %all_to_all.17.sums_ref, f32[1,2,64,540]{3,2,1,0:T(8,128)S(1)} %get-tuple-element.39.refs_0_, f32[1,2,64,540]{3,2,1,0:T(8,128)S(1)} %get-tuple-element.40.refs_1_, ...), custom_call_target="tpu_custom_call" | custom-call | flops 1382400 | bytes 3870720 | tf_op jit(solution)/shard_map/pallas_call | solution.py:627
  (1 shorter events, 0.0 us)
Async XLA Ops:
  0.6 4.9 %copy-start.5 = (f32[128,128]{1,0:T(8,128)S(1)}, f32[128,128]{1,0:T(8,128)}, u32[]{:S(2)}) copy-start(f32[128,128]{1,0:T(8,128)} %constant.2.clone.basis_ref) | copy-start | bytes 196612
  0.6 4.8 %copy-start.8 = (f32[16,2]{0,1:T(2,128)S(1)}, f32[16,2]{0,1:T(2,128)}, u32[]{:S(2)}) copy-start(f32[16,2]{0,1:T(2,128)} %param.17) | copy-start | bytes 388
  0.7 4.9 %copy-start.3 = (s32[8,4320]{1,0:T(8,128)S(1)}, s32[8,4320]{1,0:T(8,128)}, u32[]{:S(2)}) copy-start(s32[8,4320]{1,0:T(8,128)} %class_ref.1) | copy-start | bytes 414724
  0.7 4.9 %copy-start.4 = (s32[8,4320]{1,0:T(8,128)S(1)}, s32[8,4320]{1,0:T(8,128)}, u32[]{:S(2)}) copy-start(s32[8,4320]{1,0:T(8,128)} %land_ref.1) | copy-start | bytes 414724
  0.7 6.3 %collective-permute-start = (f32[2,2,64,540]{3,2,1,0:T(8,128)}, f32[2,2,64,540]{3,2,1,0:T(8,128)S(1)}, u32[]{:S(2)}, u32[]{:S(2)}) collective-permute-start(f32[2,2,64,540]{3,2,1,0:T(8,128)} %refs_3_.1), channel_id=1, source_target_pairs={{0,1},{1,0},{2,3},{3,2},{4,5},{5,4},{6,7},{7,6},{8,9},{9,8},{10,11... | collective-permute-start | bytes 1658888 | tf_op jit(solution)/shard_map/ppermute | solution.py:460
  1.2 5.8 %copy-start = (f32[2,2,64,540]{3,2,1,0:T(8,128)S(1)}, f32[2,2,64,540]{3,2,1,0:T(8,128)}, u32[]{:S(2)}) copy-start(f32[2,2,64,540]{3,2,1,0:T(8,128)} %refs_3_.1) | copy-start | bytes 1658884
  1.2 5.8 %copy-start.6 = (s32[16]{0:T(128)S(1)}, s32[16]{0:T(128)}, u32[]{:S(2)}) copy-start(s32[16]{0:T(128)} %order_ref.9) | copy-start | bytes 196
  2.9 15.9 %collective-permute-start.1 = (f32[64,2176]{1,0:T(8,128)S(1)}, f32[64,2176]{1,0:T(8,128)S(1)}, u32[]{:S(2)}, u32[]{:S(2)}) collective-permute-start(f32[64,2176]{1,0:T(8,128)S(1)} %shard_map.123), channel_id=1, source_target_pairs={{0,2},{2,0},{1,3},{3,1},{4,6},{6,4},{5,7},{7,5},{8,10},{10,8},{9,1... | collective-permute-start | bytes 1671176 | tf_op jit(solution)/shard_map/ppermute | solution.py:460
  10.3 8.4 %collective-permute-start.2 = (f32[2,64,640]{2,1,0:T(8,128)S(1)}, f32[2,64,640]{2,1,0:T(8,128)S(1)}, u32[]{:S(2)}, u32[]{:S(2)}) collective-permute-start(f32[2,64,640]{2,1,0:T(8,128)S(1)} %get-tuple-element.25), channel_id=1, source_target_pairs={{0,1},{1,0},{2,3},{3,2},{4,5},{5,4},{6,7},{7,6},{8,9},{9,8},{10,11... | collective-permute-start | bytes 983048 | tf_op jit(solution)/shard_map/ppermute | solution.py:460
  18.7 26.9 %copy-start.7 = (f32[540]{0:T(1024)S(1)}, f32[540]{0:T(1024)}, u32[]{:S(2)}) copy-start(f32[540]{0:T(1024)} %param.18) | copy-start | bytes 6484
  18.7 26.9 %copy-start.1 = (f32[2,2,64,540]{3,2,1,0:T(8,128)S(1)}, f32[2,2,64,540]{3,2,1,0:T(8,128)}, u32[]{:S(2)}) copy-start(f32[2,2,64,540]{3,2,1,0:T(8,128)} %refs_4_.5) | copy-start | bytes 1658884
  19.3 15.1 %collective-permute-start.3 = (f32[1,2,64,640]{3,2,1,0:T(8,128)S(1)}, f32[1,2,64,640]{3,2,1,0:T(8,128)S(1)}, u32[]{:S(2)}, u32[]{:S(2)}) collective-permute-start(f32[1,2,64,640]{3,2,1,0:T(8,128)S(1)} %get-tuple-element.30), channel_id=1, source_target_pairs={{0,1},{1,0},{2,3},{3,2},{4,5},{5,4},{6,7},{7,6},{8,9},{9,8},{10,11... | collective-permute-start | bytes 983048 | tf_op jit(solution)/shard_map/ppermute | solution.py:460
  45.4 1.4 %collective-permute-start.4 = (f32[32,1,8,128]{3,2,1,0:T(8,128)S(1)}, f32[32,1,8,128]{3,2,1,0:T(8,128)S(1)}, u32[]{:S(2)}, u32[]{:S(2)}) collective-permute-start(f32[32,1,8,128]{3,2,1,0:T(8,128)S(1)} %all_to_all.16.recv_ref), channel_id=1, source_target_pairs={{0,1},{1,0},{2,3},{3,2},{4,5},{5,4},{6,7},{7,6},{8,9},{9,8},{10,11... | collective-permute-start | bytes 393224 | tf_op jit(solution)/shard_map/ppermute | solution.py:460
  46.9 10.5 %copy-start.2 = (f32[2,2,64,540]{3,2,1,0:T(8,128)S(1)}, f32[2,2,64,540]{3,2,1,0:T(8,128)}, u32[]{:S(2)}) copy-start(f32[2,2,64,540]{3,2,1,0:T(8,128)} %refs_2_.1) | copy-start | bytes 1658884

commit v5 on v4

--- a/solution.py
+++ b/solution.py
@@ -163,7 +163,7 @@
 
 def prepare(geo, order_ref, leg_hbm, *refs):
     parts = refs[: geo.inner]
-    out_ref, rows_ref, *cuts, leg_ref, sem = refs[geo.inner :]
+    out_ref, rows_ref, valid_ref, *cuts, leg_ref, sem = refs[geo.inner :]
     fetch = pltpu.make_async_copy(leg_hbm, leg_ref, sem)
     fetch.start()
     place = Place(geo, order_ref)
@@ -192,6 +192,9 @@
         out_ref[m, pl.ds(pl.multiple_of(line + at, piece), piece)] = lo
 
     repeat(m_local * sin_cos * steps, one)
+    own = place.among(geo.own_starts) + lax.broadcasted_iota(jnp.int32, valid_ref.shape[1:], 1)
+    for m in range(m_local):
+        valid_ref[m] = (own >= place.order(m)).astype(jnp.float32)
     fetch.wait()
 
     def rows(m):
@@ -267,7 +270,8 @@
 def grid_rows(geo, stride, order_ref, recv_ref, table_ref, out_ref, plain, swapped, done):
     orders = plain.shape[0]
     m_local, each = recv_ref.shape[1], out_ref.shape[1]
-    slot = [lax.div(order_ref[m], jnp.int32(stride)) for m in range(orders)]
+    at = order_ref[...]
+    slot = [lax.div(at[0, m], jnp.int32(stride)) for m in range(orders)]
     for m in range(orders):
         o, i = divmod(m, m_local)
         total = recv_ref[o * geo.outer, i]
@@ -295,18 +299,12 @@
             out_ref[(o * geo.outer + a) * geo.inner + b, i] = value
 
 
-def own_mask(place, m, rows, width):
-    geo = place.geo
-    degree = place.among(geo.own_starts) + lax.broadcasted_iota(jnp.int32, (rows, width), 1)
-    return degree >= place.order(m)
-
-
-def project(geo, shift, order_ref, recv_ref, *refs):
+def project(geo, shift, valid_ref, recv_ref, *refs):
     legs, refs = refs[: 2 * geo.inner], refs[2 * geo.inner :]
     dir_ref, res_ref, damp_ref = refs[:3]
     before_ref = refs[3] if shift else None
     app_ref, sums_ref = refs[-2:]
-    place = Place(geo, order_ref)
+    place = Place(geo, None)
     each, sin_cos, samples, width = app_ref.shape
     first = place.inner(shift) * each
     window = geo.block_window
@@ -343,10 +341,10 @@
 
     def apply(at, sums):
         i, s = lax.div(at, sin_cos), lax.rem(at, sin_cos)
-        valid = own_mask(place, first + i, samples, width)
-        direction = jnp.where(valid, dir_ref[first + i, s], 0.0)
-        residual = jnp.where(valid, res_ref[first + i, s], 0.0)
-        applied = jnp.where(valid, app_ref[i, s] + damping * direction, 0.0)
+        valid = valid_ref[first + i, 0:1]
+        direction = dir_ref[first + i, s] * valid
+        residual = res_ref[first + i, s] * valid
+        applied = app_ref[i, s] * valid + damping * direction
         app_ref[i, s] = applied
         terms = (
             residual * residual,
@@ -373,11 +371,11 @@
         repeat(sums_ref.shape[0], give)
 
 
-def update(geo, order_ref, sums_ref, *refs):
+def update(geo, valid_ref, sums_ref, *refs):
     apps, refs = refs[: geo.inner], refs[geo.inner :]
     pos_ref, dir_ref, res_ref, *refs = refs
     outs, bufs, sems = refs[:3], refs[3:6], refs[6]
-    place = Place(geo, order_ref)
+    place = Place(geo, None)
     m_local, sin_cos, samples, width = dir_ref.shape
     totals = jnp.sum(sums_ref[...], axis=0)
     before, curvature, cross, square = [
@@ -401,10 +399,10 @@
         def one(at, shift=shift, app_ref=app_ref):
             i, s = lax.div(at, sin_cos), lax.rem(at, sin_cos)
             m = place.inner(shift) * each + i
-            valid = own_mask(place, m, samples, width)
-            direction = jnp.where(valid, dir_ref[m, s], 0.0)
-            residual = jnp.where(valid, res_ref[m, s], 0.0)
-            position = jnp.where(valid, pos_ref[m, s], 0.0)
+            valid = valid_ref[m, 0:1]
+            direction = dir_ref[m, s] * valid
+            residual = res_ref[m, s] * valid
+            position = pos_ref[m, s] * valid
             new_residual = residual - step * app_ref[i, s]
             values = (
                 position + step * direction,
@@ -544,11 +542,12 @@
     if small:
         siblings, tables = lax.optimization_barrier((siblings, tables))
     own_flops = 8 * m_local * line * geo.window * band_rows
-    dir_window, own_rows, *own_blocks = call(
+    dir_window, own_rows, valid, *own_blocks = call(
         functools.partial(prepare, geo),
         (
             jax.ShapeDtypeStruct((m_local, 2 * line, geo.window), jnp.bfloat16),
             jax.ShapeDtypeStruct((m_local, band_rows, line), jnp.float32),
+            jax.ShapeDtypeStruct((m_local, 8, deg_local), jnp.float32),
         )
         + (jax.ShapeDtypeStruct((m_local, band_rows, geo.block_window), jnp.float32),) * inner,
         [SCALARS, IN_HBM] + [WHOLE] * inner,
@@ -584,11 +583,11 @@
         to_orders = call(
             functools.partial(grid_rows, geo, stride),
             jax.ShapeDtypeStruct((devices, each, rows_here, line), jnp.float32),
-            [SCALARS, WHOLE, WHOLE],
+            [WHOLE, WHOLE, WHOLE],
             6 * orders * orders * rows_here * line,
             8 * orders * rows_here * line,
             [pltpu.VMEM((orders, rows_here, line), jnp.float32)] * 3,
-        )(order_of, grid_in, tables)
+        )(order_of[None, :], grid_in, tables)
     else:
         to_orders = plain_grid(geo, grid_in, order_of, class_idx, land, class_weight, period)
     spectra = lax.all_to_all(
@@ -607,11 +606,11 @@
         result, sums = call(
             functools.partial(project, geo, shift),
             (jax.ShapeDtypeStruct(part, jnp.float32), sums_out),
-            [SCALARS] + [WHOLE] * (4 + 2 * inner + (shift > 0)),
+            [WHOLE] * (5 + 2 * inner + (shift > 0)),
             6 * each * line * geo.block_window * band_rows * outer * inner,
             16 * each * line * deg_local,
         )(
-            order_of,
+            valid,
             share,
             *first_legs,
             *rest_legs,
@@ -627,13 +626,13 @@
     return call(
         functools.partial(update, geo),
         (coefficients,) * 3,
-        [SCALARS] + [WHOLE] * (4 + inner),
+        [WHOLE] * (5 + inner),
         10 * m_local * line * deg_local,
         28 * m_local * line * deg_local,
         [pltpu.VMEM(position.shape, jnp.float32)] * 3
         + [pltpu.SemaphoreType.DMA((3, m_local, sin_cos))],
         IN_HBM,
-    )(order_of, sums, *applied, position, direction, residual)
+    )(valid, sums, *applied, position, direction, residual)
 
 
 def solution(mesh):

time: 59.7 us -> 58.1 us (0.973)
  Pallas kernels: 12.6 us -> 10.5 us
    pallas_call x2, Pallas kernels: 2.7 us -> 1.6 us  [shards(): call(functools.partial(project, geo, shift), (jax.ShapeDtypeStruct(part,...]
  transfers between devices with their start and end apart: 5 -> 5, of which waited for: 1 -> 2; matrix products, arithmetic and copies ran while one was open for 0% -> 0% of each run, Pallas kernels for 13% -> 12%
where the time goes in v5:
time: 58.1 us; the launch traced here: 57.9 us
  blocking collectives  34.2 us (59%)
  Pallas kernels  10.5 us (18%)
  waiting for transfers between devices  8.66 us (15%)
  starting transfers between devices  3.68 us (6%)
  between operations  0.75 us (1%)
    all_to_all x1, blocking collectives, shards(): lax.all_to_all(to_rows.reshape(order_devices * outer, m_local, rows_here,...  15 us
    all_to_all x1, blocking collectives, shards(): lax.all_to_all(to_orders, ('order', 'outer', 'inner'), split_axis=0, conc...  10.2 us
    all_to_all x1, blocking collectives, shards(): lax.all_to_all(sums, ('order', 'outer', 'inner'), split_axis=0, concat_ax...  9.02 us
    ppermute x5, waiting for transfers between devices, rotate(): return lax.ppermute(x, axis, [(i, (i + shift) % size) for i in range(size)])  8.66 us
    ppermute x5, starting transfers between devices, rotate(): return lax.ppermute(x, axis, [(i, (i + shift) % size) for i in range(size)])  3.68 us
    pallas_call x1, Pallas kernels, shards(): call(functools.partial(prepare, geo), (jax.ShapeDtypeStruct((m_local, 2 *...  3.32 us
    pallas_call x1, Pallas kernels, shards(): call(functools.partial(cut_windows, geo), (cut,) * (outer - 1), [IN_HBM],...  1.65 us
    pallas_call x1, Pallas kernels, shards(): call(functools.partial(update, geo), (coefficients,) * 3, [WHOLE] * (5 +...  1.61 us
  transfers between devices with their start and end apart: 5, of which 2 were waited for; matrix products, arithmetic and copies ran while one was open for 0% of the time, Pallas kernels for 12%

profile of v5, /device:TPU:0, one launch (start us, length us, event | category | flops | bytes accessed | tf_op | source)
XLA Modules:
  0.0 57.9 jit_solution(7023312087516024040)
XLA Ops:
  0.6 0.0 copy-start.5
  0.6 0.0 copy-start.8
  0.7 0.0 copy-start.3
  0.7 0.0 copy-start.4
  0.7 0.5 collective-permute-start
  1.2 0.0 copy-start
  1.2 0.0 copy-start.6
  1.2 1.7 %shard_map.123 = f32[64,2176]{1,0:T(8,128)S(1)} custom-call(f32[2,64,2160]{2,1,0:T(8,128)} %bitcast.5), custom_call_target="tpu_custom_call" | custom-call | flops 147456 | bytes 2359296 | tf_op jit(solution)/shard_map/pallas_call | solution.py:513
  2.9 2.6 %collective-permute-start.1 = (f32[64,2176]{1,0:T(8,128)S(1)}, f32[64,2176]{1,0:T(8,128)S(1)}, u32[]{:S(2)}, u32[]{:S(2)}) collective-permute-start(f32[64,2176]{1,0:T(8,128)S(1)} %shard_map.123), channel_id=1, source_target_pairs={{0,2},{2,0},{1,3},{3,1},{4,6},{6,4},{5,7},{7,5},{8,10},{10,8},{9,1... | collective-permute-start | bytes 1671176 | tf_op jit(solution)/shard_map/ppermute | solution.py:458
  5.5 0.0 copy-done.8
  5.5 0.1 copy.13.value_ref
  5.6 0.0 copy-done.5
  5.6 0.0 copy-done.3
  5.6 0.0 copy-done.4
  5.6 1.4 %shard_map.121.table_ref = f32[4,32,8,128]{3,2,1,0:T(8,128)S(1)} custom-call(s32[8,4320]{1,0:T(8,128)S(1)} %copy-done.3, s32[8,4320]{1,0:T(8,128)S(1)} %copy-done.4, f32[16,2]{1,0:T(8,128)S(1)} %copy.13.value_ref, f32[128,128]{1,0:T(8,128)S(1)} %copy-done.5), custom_call_target="tpu_custom_call" | custom-call | flops 3456000 | bytes 276480 | tf_op jit(solution)/shard_map/pallas_call | solution.py:533
  6.9 0.0 collective-permute-done.refs_1_
  7.0 0.0 copy-done
  7.0 0.0 copy-done.6
  7.0 3.3 %shard_map.122 = (bf16[2,256,1152]{2,1,0:T(8,128)(2,1)S(1)}, f32[2,64,128]{2,1,0:T(8,128)S(1)}, f32[2,8,540]{2,1,0:T(8,128)S(1)}, f32[2,64,640]{2,1,0:T(8,128)S(1)}, f32[2,64,640]{2,1,0:T(8,128)S(1)}) custom-call(s32[16]{0:T(128)S(1)} %copy-done.6, f32[2,64,2160]{2,1,0:T(8,128)} %bitcast.6, f32[2,2,64,540]{3,2,1,0:T(8,128)S(1)} %copy-done, ...), custom_call_target="tpu_custom_call" | custom-call | flops 150994944 | bytes 3465216 | tf_op jit(solution)/shard_map/pallas_call | solution.py:545
  10.3 0.2 collective-permute-start.2
  10.5 8.2 %collective-permute-done.1.refs_0_ = f32[64,2176]{1,0:T(8,128)S(1)} collective-permute-done((f32[64,2176]{1,0:T(8,128)S(1)}, f32[64,2176]{1,0:T(8,128)S(1)}, u32[]{:S(2)}, u32[]{:S(2)}) %collective-permute-start.1) | collective-permute-done | bytes 557088 | tf_op jit(solution)/shard_map/ppermute | solution.py:458
  18.7 0.0 collective-permute-done.2.refs_1_
  18.7 0.0 copy-start.7
  18.7 0.0 copy-start.1
  18.7 0.5 shard_map.124
  19.3 0.1 collective-permute-start.3
  19.4 15.0 %all_to_all.15.recv_ref = f32[16,2,8,128]{3,2,1,0:T(8,128)S(1)} all-to-all(f32[16,2,8,128]{3,2,1,0:T(8,128)S(1)} %bitcast.3), channel_id=1, replica_groups=mesh['order'=8,'outer'=2,'inner'=2] {'order','outer'}, dimensions={0} | all-to-all | bytes 262144 | tf_op jit(solution)/shard_map/all_to_all | solution.py:573
  34.3 0.0 collective-permute-done.3.refs_3_
  34.3 0.4 shard_map.125
  34.7 10.2 %all_to_all.16.recv_ref = f32[32,1,8,128]{3,2,1,0:T(8,128)S(1)} all-to-all(f32[32,1,8,128]{3,2,1,0:T(8,128)S(1)} %shard_map.125), channel_id=1, replica_groups=mesh['order'=8,'outer'=2,'inner'=2] {'order','outer','inner'}, dimensions={0} | all-to-all | bytes 262144 | tf_op jit(solution)/shard_map/all_to_all | solution.py:593
  44.9 0.2 collective-permute-start.4
  45.1 0.0 copy-done.7
  45.2 0.0 copy-done.1
  45.2 0.7 %shard_map.126 = (f32[1,2,64,540]{3,2,1,0:T(8,128)S(1)}, f32[256,128]{1,0:T(8,128)S(1)}) custom-call(f32[2,8,540]{2,1,0:T(8,128)S(1)} %get-tuple-element.24.valid_ref, f32[32,1,8,128]{3,2,1,0:T(8,128)S(1)} %all_to_all.16.recv_ref, f32[2,64,640]{2,1,0:T(8,128)S(1)} %get-tuple-element.35.refs_0_, f32[2,64,640]{2,1,0:T(8,128)S(1)} %collective-permute-done.2.refs_1_, ...), custom_call_target="tpu_custom_call" | custom-call | flops 125829120 | bytes 1105920 | tf_op jit(solution)/shard_map/pallas_call | solution.py:606
  45.8 0.5 collective-permute-done.4.recv_ref
  46.3 0.0 copy-start.2
  46.3 0.9 %shard_map.127 = (f32[1,2,64,540]{3,2,1,0:T(8,128)S(1)}, f32[32,1,256]{2,1,0:T(1,128)S(1)}) custom-call(f32[2,8,540]{2,1,0:T(8,128)S(1)} %get-tuple-element.24.valid_ref, f32[32,1,8,128]{3,2,1,0:T(8,128)S(1)} %collective-permute-done.4.recv_ref, f32[2,64,640]{2,1,0:T(8,128)S(1)} %get-tuple-element.35.refs_0_, ...), custom_call_target="tpu_custom_call" | custom-call | flops 125829120 | bytes 1105920 | tf_op jit(solution)/shard_map/pallas_call | solution.py:606
  47.2 9.0 %all_to_all.17.sums_ref = f32[32,1,256]{2,1,0:T(1,128)S(1)} all-to-all(f32[32,1,256]{2,1,0:T(1,128)S(1)} %get-tuple-element.40), channel_id=1, replica_groups=mesh['order'=8,'outer'=2,'inner'=2] {'order','outer','inner'}, dimensions={0} | all-to-all | bytes 65536 | tf_op jit(solution)/shard_map/all_to_all | solution.py:623
  56.2 0.0 copy-done.2
  56.2 1.6 %shard_map.128 = (f32[2,2,64,540]{3,2,1,0:T(8,128)}, f32[2,2,64,540]{3,2,1,0:T(8,128)}, f32[2,2,64,540]{3,2,1,0:T(8,128)}) custom-call(f32[2,8,540]{2,1,0:T(8,128)S(1)} %get-tuple-element.24.valid_ref, f32[32,1,256]{2,1,0:T(1,128)S(1)} %all_to_all.17.sums_ref, f32[1,2,64,540]{3,2,1,0:T(8,128)S(1)} %get-tuple-element.41.refs_0_, ...), custom_call_target="tpu_custom_call" | custom-call | flops 1382400 | bytes 3870720 | tf_op jit(solution)/shard_map/pallas_call | solution.py:626
  (1 shorter events, 0.0 us)
Async XLA Ops:
  0.6 4.9 %copy-start.5 = (f32[128,128]{1,0:T(8,128)S(1)}, f32[128,128]{1,0:T(8,128)}, u32[]{:S(2)}) copy-start(f32[128,128]{1,0:T(8,128)} %constant.2.clone.basis_ref) | copy-start | bytes 196612
  0.6 4.8 %copy-start.8 = (f32[16,2]{0,1:T(2,128)S(1)}, f32[16,2]{0,1:T(2,128)}, u32[]{:S(2)}) copy-start(f32[16,2]{0,1:T(2,128)} %param.17) | copy-start | bytes 388
  0.7 4.9 %copy-start.3 = (s32[8,4320]{1,0:T(8,128)S(1)}, s32[8,4320]{1,0:T(8,128)}, u32[]{:S(2)}) copy-start(s32[8,4320]{1,0:T(8,128)} %class_ref.1) | copy-start | bytes 414724
  0.7 4.9 %copy-start.4 = (s32[8,4320]{1,0:T(8,128)S(1)}, s32[8,4320]{1,0:T(8,128)}, u32[]{:S(2)}) copy-start(s32[8,4320]{1,0:T(8,128)} %land_ref.1) | copy-start | bytes 414724
  0.7 6.3 %collective-permute-start = (f32[2,2,64,540]{3,2,1,0:T(8,128)}, f32[2,2,64,540]{3,2,1,0:T(8,128)S(1)}, u32[]{:S(2)}, u32[]{:S(2)}) collective-permute-start(f32[2,2,64,540]{3,2,1,0:T(8,128)} %refs_3_.1), channel_id=1, source_target_pairs={{0,1},{1,0},{2,3},{3,2},{4,5},{5,4},{6,7},{7,6},{8,9},{9,8},{10,11... | collective-permute-start | bytes 1658888 | tf_op jit(solution)/shard_map/ppermute | solution.py:458
  1.2 5.8 %copy-start = (f32[2,2,64,540]{3,2,1,0:T(8,128)S(1)}, f32[2,2,64,540]{3,2,1,0:T(8,128)}, u32[]{:S(2)}) copy-start(f32[2,2,64,540]{3,2,1,0:T(8,128)} %refs_3_.1) | copy-start | bytes 1658884
  1.2 5.8 %copy-start.6 = (s32[16]{0:T(128)S(1)}, s32[16]{0:T(128)}, u32[]{:S(2)}) copy-start(s32[16]{0:T(128)} %order_ref.1) | copy-start | bytes 196
  2.9 15.9 %collective-permute-start.1 = (f32[64,2176]{1,0:T(8,128)S(1)}, f32[64,2176]{1,0:T(8,128)S(1)}, u32[]{:S(2)}, u32[]{:S(2)}) collective-permute-start(f32[64,2176]{1,0:T(8,128)S(1)} %shard_map.123), channel_id=1, source_target_pairs={{0,2},{2,0},{1,3},{3,1},{4,6},{6,4},{5,7},{7,5},{8,10},{10,8},{9,1... | collective-permute-start | bytes 1671176 | tf_op jit(solution)/shard_map/ppermute | solution.py:458
  10.3 8.4 %collective-permute-start.2 = (f32[2,64,640]{2,1,0:T(8,128)S(1)}, f32[2,64,640]{2,1,0:T(8,128)S(1)}, u32[]{:S(2)}, u32[]{:S(2)}) collective-permute-start(f32[2,64,640]{2,1,0:T(8,128)S(1)} %get-tuple-element.27), channel_id=1, source_target_pairs={{0,1},{1,0},{2,3},{3,2},{4,5},{5,4},{6,7},{7,6},{8,9},{9,8},{10,11... | collective-permute-start | bytes 983048 | tf_op jit(solution)/shard_map/ppermute | solution.py:458
  18.7 26.4 %copy-start.7 = (f32[540]{0:T(1024)S(1)}, f32[540]{0:T(1024)}, u32[]{:S(2)}) copy-start(f32[540]{0:T(1024)} %param.18) | copy-start | bytes 6484
  18.7 26.4 %copy-start.1 = (f32[2,2,64,540]{3,2,1,0:T(8,128)S(1)}, f32[2,2,64,540]{3,2,1,0:T(8,128)}, u32[]{:S(2)}) copy-start(f32[2,2,64,540]{3,2,1,0:T(8,128)} %refs_4_.5) | copy-start | bytes 1658884
  19.3 15.1 %collective-permute-start.3 = (f32[1,2,64,640]{3,2,1,0:T(8,128)S(1)}, f32[1,2,64,640]{3,2,1,0:T(8,128)S(1)}, u32[]{:S(2)}, u32[]{:S(2)}) collective-permute-start(f32[1,2,64,640]{3,2,1,0:T(8,128)S(1)} %get-tuple-element.32), channel_id=1, source_target_pairs={{0,1},{1,0},{2,3},{3,2},{4,5},{5,4},{6,7},{7,6},{8,9},{9,8},{10,11... | collective-permute-start | bytes 983048 | tf_op jit(solution)/shard_map/ppermute | solution.py:458
  44.9 1.3 %collective-permute-start.4 = (f32[32,1,8,128]{3,2,1,0:T(8,128)S(1)}, f32[32,1,8,128]{3,2,1,0:T(8,128)S(1)}, u32[]{:S(2)}, u32[]{:S(2)}) collective-permute-start(f32[32,1,8,128]{3,2,1,0:T(8,128)S(1)} %all_to_all.16.recv_ref), channel_id=1, source_target_pairs={{0,1},{1,0},{2,3},{3,2},{4,5},{5,4},{6,7},{7,6},{8,9},{9,8},{10,11... | collective-permute-start | bytes 393224 | tf_op jit(solution)/shard_map/ppermute | solution.py:458
  46.3 10.0 %copy-start.2 = (f32[2,2,64,540]{3,2,1,0:T(8,128)S(1)}, f32[2,2,64,540]{3,2,1,0:T(8,128)}, u32[]{:S(2)}) copy-start(f32[2,2,64,540]{3,2,1,0:T(8,128)} %refs_2_.1) | copy-start | bytes 1658884

commit v6 on v5

--- a/solution.py
+++ b/solution.py
@@ -40,7 +40,7 @@
     return pltpu.CompilerParams(vmem_limit_bytes=grant)
 
 
-def call(kernel, out_shape, in_specs, flops, moved, scratch=(), out_spec=WHOLE):
+def call(kernel, out_shape, in_specs, flops, moved, scratch=(), out_spec=WHOLE, cost=0):
     return pl.pallas_call(
         kernel,
         out_shape=out_shape,
@@ -48,7 +48,7 @@
         out_specs=jax.tree.map(lambda _: out_spec, out_shape),
         scratch_shapes=scratch,
         compiler_params=params(moved),
-        cost_estimate=pl.CostEstimate(flops=flops, bytes_accessed=moved, transcendentals=0),
+        cost_estimate=pl.CostEstimate(flops=flops, bytes_accessed=cost or moved, transcendentals=0),
     )
 
 
@@ -534,13 +534,12 @@
             functools.partial(weight_tables, longitudes, period),
             jax.ShapeDtypeStruct((4, count, rows_here, LANES), jnp.float32),
             [WHOLE, WHOLE, SCALARS, WHOLE],
-            100 * rows_here * longitudes,
+            1,
             8 * rows_here * longitudes,
+            cost=1,
         )(class_idx, land, class_weight, jnp.asarray(basis))
 
     siblings = [rotate(direction, "inner", inner, s) for s in range(1, inner)]
-    if small:
-        siblings, tables = lax.optimization_barrier((siblings, tables))
     own_flops = 8 * m_local * line * geo.window * band_rows
     dir_window, own_rows, valid, *own_blocks = call(
         functools.partial(prepare, geo),
@@ -551,14 +550,16 @@
         )
         + (jax.ShapeDtypeStruct((m_local, band_rows, geo.block_window), jnp.float32),) * inner,
         [SCALARS, IN_HBM] + [WHOLE] * inner,
-        own_flops,
+        1,
         8 * m_local * line * geo.window + leg_moved,
         leg_scratch,
+        cost=1,
     )(order_of, far(by_row), direction, *siblings)
     first_legs = [own_blocks[0]]
     first_legs += [rotate(own_blocks[s], "inner", inner, s) for s in range(1, inner)]
 
-    received, first_legs = lax.optimization_barrier((received, first_legs))
+    if small:
+        received, tables = lax.optimization_barrier((received, tables))
     block = jax.ShapeDtypeStruct((outer - 1, m_local, band_rows, geo.block_window), jnp.float32)
     to_rows, *blocks = call(
         functools.partial(synthesise_rest, geo),
@@ -578,7 +579,7 @@
         tiled=True,
     )
 
-    grid_in, rest_legs = lax.optimization_barrier((grid_in, rest_legs))
+    grid_in, first_legs, rest_legs = lax.optimization_barrier((grid_in, first_legs, rest_legs))
     if small:
         to_orders = call(
             functools.partial(grid_rows, geo, stride),

time: 58.1 us -> 57.4 us (0.988)
  transfers between devices with their start and end apart: 5 -> 5, of which waited for: 2 -> 3; matrix products, arithmetic and copies ran while one was open for 0% -> 0% of each run, Pallas kernels for 12% -> 10%
where the time goes in v6:
time: 57.4 us; the launch traced here: 57.1 us
  blocking collectives  34.2 us (60%)
  Pallas kernels  10.5 us (18%)
  waiting for transfers between devices  8.09 us (14%)
  starting transfers between devices  3.52 us (6%)
  between operations  0.75 us (1%)
    all_to_all x1, blocking collectives, shards(): lax.all_to_all(to_rows.reshape(order_devices * outer, m_local, rows_here,...  15 us
    all_to_all x1, blocking collectives, shards(): lax.all_to_all(to_orders, ('order', 'outer', 'inner'), split_axis=0, conc...  10.2 us
    all_to_all x1, blocking collectives, shards(): lax.all_to_all(sums, ('order', 'outer', 'inner'), split_axis=0, concat_ax...  9.02 us
    ppermute x5, waiting for transfers between devices, rotate(): return lax.ppermute(x, axis, [(i, (i + shift) % size) for i in range(size)])  8.09 us
    ppermute x5, starting transfers between devices, rotate(): return lax.ppermute(x, axis, [(i, (i + shift) % size) for i in range(size)])  3.52 us
    pallas_call x1, Pallas kernels, shards(): call(functools.partial(prepare, geo), (jax.ShapeDtypeStruct((m_local, 2 *...  3.31 us
    pallas_call x1, Pallas kernels, shards(): call(functools.partial(cut_windows, geo), (cut,) * (outer - 1), [IN_HBM],...  1.67 us
    pallas_call x1, Pallas kernels, shards(): call(functools.partial(update, geo), (coefficients,) * 3, [WHOLE] * (5 +...  1.61 us
  transfers between devices with their start and end apart: 5, of which 3 were waited for; matrix products, arithmetic and copies ran while one was open for 0% of the time, Pallas kernels for 10%

profile of v6, /device:TPU:0, one launch (start us, length us, event | category | flops | bytes accessed | tf_op | source)
XLA Modules:
  0.0 57.1 jit_solution(3690941400388105654)
XLA Ops:
  0.6 0.0 copy-start.5
  0.6 0.0 copy-start
  0.7 0.0 copy-start.8
  0.7 0.0 copy-start.3
  0.7 0.0 copy-start.4
  0.7 0.0 copy-start.6
  0.7 1.7 %shard_map.122 = f32[64,2176]{1,0:T(8,128)S(1)} custom-call(f32[2,64,2160]{2,1,0:T(8,128)} %bitcast.5), custom_call_target="tpu_custom_call" | custom-call | flops 147456 | bytes 2359296 | tf_op jit(solution)/shard_map/pallas_call | solution.py:513
  2.4 3.0 %collective-permute-start.1 = (f32[64,2176]{1,0:T(8,128)S(1)}, f32[64,2176]{1,0:T(8,128)S(1)}, u32[]{:S(2)}, u32[]{:S(2)}) collective-permute-start(f32[64,2176]{1,0:T(8,128)S(1)} %shard_map.122), channel_id=1, source_target_pairs={{0,2},{2,0},{1,3},{3,1},{4,6},{6,4},{5,7},{7,5},{8,10},{10,8},{9,1... | collective-permute-start | bytes 1671176 | tf_op jit(solution)/shard_map/ppermute | solution.py:458
  5.4 0.0 copy-done
  5.4 0.0 collective-permute-start
  5.4 0.0 copy-done.8
  5.4 0.1 copy.13.value_ref
  5.5 0.0 copy-done.5
  5.5 0.0 copy-done.3
  5.5 0.0 copy-done.4
  5.5 1.4 %shard_map.123.table_ref = f32[4,32,8,128]{3,2,1,0:T(8,128)S(1)} custom-call(s32[8,4320]{1,0:T(8,128)S(1)} %copy-done.3, s32[8,4320]{1,0:T(8,128)S(1)} %copy-done.4, f32[16,2]{1,0:T(8,128)S(1)} %copy.13.value_ref, f32[128,128]{1,0:T(8,128)S(1)} %copy-done.5), custom_call_target="tpu_custom_call" | custom-call | flops 1 | bytes 1 | tf_op jit(solution)/shard_map/pallas_call | solution.py:533
  6.9 0.6 %collective-permute-done.refs_1_ = f32[2,2,64,540]{3,2,1,0:T(8,128)S(1)} collective-permute-done((f32[2,2,64,540]{3,2,1,0:T(8,128)S(1)}, f32[2,2,64,540]{3,2,1,0:T(8,128)S(1)}, u32[]{:S(2)}, u32[]{:S(2)}) %collective-permute-start) | collective-permute-done | bytes 552992 | tf_op jit(solution)/shard_map/ppermute | solution.py:458
  7.5 0.0 copy-done.6
  7.5 3.3 %shard_map.121 = (bf16[2,256,1152]{2,1,0:T(8,128)(2,1)S(1)}, f32[2,64,128]{2,1,0:T(8,128)S(1)}, f32[2,8,540]{2,1,0:T(8,128)S(1)}, f32[2,64,640]{2,1,0:T(8,128)S(1)}, f32[2,64,640]{2,1,0:T(8,128)S(1)}) custom-call(s32[16]{0:T(128)S(1)} %copy-done.6, f32[2,64,2160]{2,1,0:T(8,128)} %bitcast.6, f32[2,2,64,540]{3,2,1,0:T(8,128)S(1)} %copy-done, ...), custom_call_target="tpu_custom_call" | custom-call | flops 1 | bytes 1 | tf_op jit(solution)/shard_map/pallas_call | solution.py:544
  10.8 0.2 collective-permute-start.2
  11.0 7.0 %collective-permute-done.1.refs_0_ = f32[64,2176]{1,0:T(8,128)S(1)} collective-permute-done((f32[64,2176]{1,0:T(8,128)S(1)}, f32[64,2176]{1,0:T(8,128)S(1)}, u32[]{:S(2)}, u32[]{:S(2)}) %collective-permute-start.1) | collective-permute-done | bytes 557088 | tf_op jit(solution)/shard_map/ppermute | solution.py:458
  18.0 0.0 copy-start.7
  18.0 0.0 copy-start.1
  18.0 0.5 shard_map.124
  18.6 0.1 collective-permute-start.3
  18.7 15.0 %all_to_all.15.recv_ref = f32[16,2,8,128]{3,2,1,0:T(8,128)S(1)} all-to-all(f32[16,2,8,128]{3,2,1,0:T(8,128)S(1)} %bitcast.3), channel_id=1, replica_groups=mesh['order'=8,'outer'=2,'inner'=2] {'order','outer'}, dimensions={0} | all-to-all | bytes 262144 | tf_op jit(solution)/shard_map/all_to_all | solution.py:574
  33.6 0.0 collective-permute-done.2.refs_1_
  33.6 0.0 collective-permute-done.3.refs_3_
  33.6 0.4 shard_map.125
  34.0 10.2 %all_to_all.16.recv_ref = f32[32,1,8,128]{3,2,1,0:T(8,128)S(1)} all-to-all(f32[32,1,8,128]{3,2,1,0:T(8,128)S(1)} %shard_map.125), channel_id=1, replica_groups=mesh['order'=8,'outer'=2,'inner'=2] {'order','outer','inner'}, dimensions={0} | all-to-all | bytes 262144 | tf_op jit(solution)/shard_map/all_to_all | solution.py:594
  44.2 0.2 collective-permute-start.4
  44.4 0.0 copy-done.7
  44.4 0.0 copy-done.1
  44.4 0.7 %shard_map.126 = (f32[1,2,64,540]{3,2,1,0:T(8,128)S(1)}, f32[256,128]{1,0:T(8,128)S(1)}) custom-call(f32[2,8,540]{2,1,0:T(8,128)S(1)} %get-tuple-element.22.valid_ref, f32[32,1,8,128]{3,2,1,0:T(8,128)S(1)} %all_to_all.16.recv_ref, f32[2,64,640]{2,1,0:T(8,128)S(1)} %get-tuple-element.33.refs_0_, f32[2,64,640]{2,1,0:T(8,128)S(1)} %collective-permute-done.2.refs_1_, ...), custom_call_target="tpu_custom_call" | custom-call | flops 125829120 | bytes 1105920 | tf_op jit(solution)/shard_map/pallas_call | solution.py:607
  45.1 0.5 collective-permute-done.4.recv_ref
  45.6 0.0 copy-start.2
  45.6 0.9 %shard_map.127 = (f32[1,2,64,540]{3,2,1,0:T(8,128)S(1)}, f32[32,1,256]{2,1,0:T(1,128)S(1)}) custom-call(f32[2,8,540]{2,1,0:T(8,128)S(1)} %get-tuple-element.22.valid_ref, f32[32,1,8,128]{3,2,1,0:T(8,128)S(1)} %collective-permute-done.4.recv_ref, f32[2,64,640]{2,1,0:T(8,128)S(1)} %get-tuple-element.33.refs_0_, ...), custom_call_target="tpu_custom_call" | custom-call | flops 125829120 | bytes 1105920 | tf_op jit(solution)/shard_map/pallas_call | solution.py:607
  46.5 9.0 %all_to_all.17.sums_ref = f32[32,1,256]{2,1,0:T(1,128)S(1)} all-to-all(f32[32,1,256]{2,1,0:T(1,128)S(1)} %get-tuple-element.38), channel_id=1, replica_groups=mesh['order'=8,'outer'=2,'inner'=2] {'order','outer','inner'}, dimensions={0} | all-to-all | bytes 65536 | tf_op jit(solution)/shard_map/all_to_all | solution.py:624
  55.5 0.0 copy-done.2
  55.5 1.6 %shard_map.128 = (f32[2,2,64,540]{3,2,1,0:T(8,128)}, f32[2,2,64,540]{3,2,1,0:T(8,128)}, f32[2,2,64,540]{3,2,1,0:T(8,128)}) custom-call(f32[2,8,540]{2,1,0:T(8,128)S(1)} %get-tuple-element.22.valid_ref, f32[32,1,256]{2,1,0:T(1,128)S(1)} %all_to_all.17.sums_ref, f32[1,2,64,540]{3,2,1,0:T(8,128)S(1)} %get-tuple-element.39.refs_0_, ...), custom_call_target="tpu_custom_call" | custom-call | flops 1382400 | bytes 3870720 | tf_op jit(solution)/shard_map/pallas_call | solution.py:627
  (1 shorter events, 0.0 us)
Async XLA Ops:
  0.6 4.9 %copy-start.5 = (f32[128,128]{1,0:T(8,128)S(1)}, f32[128,128]{1,0:T(8,128)}, u32[]{:S(2)}) copy-start(f32[128,128]{1,0:T(8,128)} %constant.2.clone.basis_ref) | copy-start | bytes 196612
  0.6 4.8 %copy-start = (f32[2,2,64,540]{3,2,1,0:T(8,128)S(1)}, f32[2,2,64,540]{3,2,1,0:T(8,128)}, u32[]{:S(2)}) copy-start(f32[2,2,64,540]{3,2,1,0:T(8,128)} %refs_3_.1) | copy-start | bytes 1658884
  0.7 4.8 %copy-start.8 = (f32[16,2]{0,1:T(2,128)S(1)}, f32[16,2]{0,1:T(2,128)}, u32[]{:S(2)}) copy-start(f32[16,2]{0,1:T(2,128)} %param.17) | copy-start | bytes 388
  0.7 4.8 %copy-start.3 = (s32[8,4320]{1,0:T(8,128)S(1)}, s32[8,4320]{1,0:T(8,128)}, u32[]{:S(2)}) copy-start(s32[8,4320]{1,0:T(8,128)} %class_ref.1) | copy-start | bytes 414724
  0.7 4.8 %copy-start.4 = (s32[8,4320]{1,0:T(8,128)S(1)}, s32[8,4320]{1,0:T(8,128)}, u32[]{:S(2)}) copy-start(s32[8,4320]{1,0:T(8,128)} %land_ref.1) | copy-start | bytes 414724
  0.7 6.8 %copy-start.6 = (s32[16]{0:T(128)S(1)}, s32[16]{0:T(128)}, u32[]{:S(2)}) copy-start(s32[16]{0:T(128)} %order_ref.1) | copy-start | bytes 196
  2.4 15.7 %collective-permute-start.1 = (f32[64,2176]{1,0:T(8,128)S(1)}, f32[64,2176]{1,0:T(8,128)S(1)}, u32[]{:S(2)}, u32[]{:S(2)}) collective-permute-start(f32[64,2176]{1,0:T(8,128)S(1)} %shard_map.122), channel_id=1, source_target_pairs={{0,2},{2,0},{1,3},{3,1},{4,6},{6,4},{5,7},{7,5},{8,10},{10,8},{9,1... | collective-permute-start | bytes 1671176 | tf_op jit(solution)/shard_map/ppermute | solution.py:458
  5.4 2.1 %collective-permute-start = (f32[2,2,64,540]{3,2,1,0:T(8,128)S(1)}, f32[2,2,64,540]{3,2,1,0:T(8,128)S(1)}, u32[]{:S(2)}, u32[]{:S(2)}) collective-permute-start(f32[2,2,64,540]{3,2,1,0:T(8,128)S(1)} %copy-done), channel_id=1, source_target_pairs={{0,1},{1,0},{2,3},{3,2},{4,5},{5,4},{6,7},{7,6},{8,9},{9,8},{10,11... | collective-permute-start | bytes 1658888 | tf_op jit(solution)/shard_map/ppermute | solution.py:458
  10.8 22.8 %collective-permute-start.2 = (f32[2,64,640]{2,1,0:T(8,128)S(1)}, f32[2,64,640]{2,1,0:T(8,128)S(1)}, u32[]{:S(2)}, u32[]{:S(2)}) collective-permute-start(f32[2,64,640]{2,1,0:T(8,128)S(1)} %get-tuple-element.28), channel_id=1, source_target_pairs={{0,1},{1,0},{2,3},{3,2},{4,5},{5,4},{6,7},{7,6},{8,9},{9,8},{10,11... | collective-permute-start | bytes 983048 | tf_op jit(solution)/shard_map/ppermute | solution.py:458
  18.0 26.4 %copy-start.7 = (f32[540]{0:T(1024)S(1)}, f32[540]{0:T(1024)}, u32[]{:S(2)}) copy-start(f32[540]{0:T(1024)} %param.18) | copy-start | bytes 6484
  18.0 26.4 %copy-start.1 = (f32[2,2,64,540]{3,2,1,0:T(8,128)S(1)}, f32[2,2,64,540]{3,2,1,0:T(8,128)}, u32[]{:S(2)}) copy-start(f32[2,2,64,540]{3,2,1,0:T(8,128)} %refs_4_.5) | copy-start | bytes 1658884
  18.6 15.1 %collective-permute-start.3 = (f32[1,2,64,640]{3,2,1,0:T(8,128)S(1)}, f32[1,2,64,640]{3,2,1,0:T(8,128)S(1)}, u32[]{:S(2)}, u32[]{:S(2)}) collective-permute-start(f32[1,2,64,640]{3,2,1,0:T(8,128)S(1)} %get-tuple-element.30), channel_id=1, source_target_pairs={{0,1},{1,0},{2,3},{3,2},{4,5},{5,4},{6,7},{7,6},{8,9},{9,8},{10,11... | collective-permute-start | bytes 983048 | tf_op jit(solution)/shard_map/ppermute | solution.py:458
  44.2 1.3 %collective-permute-start.4 = (f32[32,1,8,128]{3,2,1,0:T(8,128)S(1)}, f32[32,1,8,128]{3,2,1,0:T(8,128)S(1)}, u32[]{:S(2)}, u32[]{:S(2)}) collective-permute-start(f32[32,1,8,128]{3,2,1,0:T(8,128)S(1)} %all_to_all.16.recv_ref), channel_id=1, source_target_pairs={{0,1},{1,0},{2,3},{3,2},{4,5},{5,4},{6,7},{7,6},{8,9},{9,8},{10,11... | collective-permute-start | bytes 393224 | tf_op jit(solution)/shard_map/ppermute | solution.py:458
  45.6 10.0 %copy-start.2 = (f32[2,2,64,540]{3,2,1,0:T(8,128)S(1)}, f32[2,2,64,540]{3,2,1,0:T(8,128)}, u32[]{:S(2)}) copy-start(f32[2,2,64,540]{3,2,1,0:T(8,128)} %refs_2_.1) | copy-start | bytes 1658884

commit v7 on v6

--- a/solution.py
+++ b/solution.py
@@ -220,8 +220,8 @@
 
     def put(m, shift, part):
         a = place.outer(shift)
-        for o in range(out_ref.shape[0]):
-            out_ref[o, a, m] = part[o * rows : (o + 1) * rows]
+        for o in range(out_ref.shape[1]):
+            out_ref[a, o, m] = part[o * rows : (o + 1) * rows]
 
     for m in range(own_ref.shape[0]):
         put(m, 0, own_ref[m])
@@ -270,13 +270,14 @@
 def grid_rows(geo, stride, order_ref, recv_ref, table_ref, out_ref, plain, swapped, done):
     orders = plain.shape[0]
     m_local, each = recv_ref.shape[1], out_ref.shape[1]
+    order_devices = orders // m_local
     at = order_ref[...]
     slot = [lax.div(at[0, m], jnp.int32(stride)) for m in range(orders)]
     for m in range(orders):
         o, i = divmod(m, m_local)
-        total = recv_ref[o * geo.outer, i]
+        total = recv_ref[o, i]
         for a in range(1, geo.outer):
-            total = total + recv_ref[o * geo.outer + a, i]
+            total = total + recv_ref[a * order_devices + o, i]
         at = slot[m]
         plain[at] = total
         swapped[at] = pltpu.roll(total, LANES // 2, 1)
@@ -296,7 +297,7 @@
         b, i = divmod(i, each)
         value = done[slot[m]]
         for a in range(geo.outer):
-            out_ref[(o * geo.outer + a) * geo.inner + b, i] = value
+            out_ref[(b * geo.outer + a) * order_devices + o, i] = value
 
 
 def project(geo, shift, valid_ref, recv_ref, *refs):
@@ -319,13 +320,13 @@
         tiles, blocks = [], []
         for b in range(geo.inner):
             for a in range(geo.outer):
-                band = place.outer(a) * geo.inner + place.inner(b)
+                band = place.inner(b) * geo.outer + place.outer(a)
+                tile = recv_ref[pl.ds(band * order_devices, order_devices), i]
+                tiles.append(tile.reshape(-1, tile.shape[2]))
                 if a == 0:
                     blocks.append(legs[b][first + i])
                 else:
                     blocks.append(legs[geo.inner + b][a - 1, first + i])
-                for o in range(order_devices):
-                    tiles.append(recv_ref[o * copies + band, i])
         hi, lo = split_bf16(jnp.concatenate(tiles, axis=0))
         high, low = split_bf16(jnp.concatenate(blocks, axis=0))
         dims = (((0,), (0,)), ((), ()))
@@ -463,8 +464,8 @@
     m_local, rows, width = grid_in.shape[1:]
     orders = order_devices * m_local
     longitudes = class_idx.shape[1]
-    stacked = grid_in.reshape(order_devices, geo.outer, m_local, rows, 2, width // 2)
-    stacked = jnp.sum(stacked, axis=1).reshape(orders, rows, 2, width // 2)
+    stacked = grid_in.reshape(geo.outer, order_devices, m_local, rows, 2, width // 2)
+    stacked = jnp.sum(stacked, axis=0).reshape(orders, rows, 2, width // 2)
     phases = order_of[:, None] * jnp.arange(period, dtype=jnp.int32)[None, :] % longitudes
     angles = phases.astype(jnp.float32) * (2.0 * math.pi / longitudes)
     harmonic = jnp.stack([jnp.cos(angles), jnp.sin(angles)])
@@ -477,9 +478,10 @@
     spectra = jnp.einsum("rkp,smp->mrsk", weighted, harmonic, precision=HIGHEST)
     each = m_local // geo.inner
     spectra = spectra * (2.0 / longitudes)
-    spectra = spectra.reshape(order_devices, 1, geo.inner, each, rows, width)
+    spectra = spectra.reshape(order_devices, geo.inner, 1, each, rows, width)
+    spectra = jnp.transpose(spectra, (1, 2, 0, 3, 4, 5))
     spectra = jnp.broadcast_to(
-        spectra, (order_devices, geo.outer, geo.inner, each, rows, width)
+        spectra, (geo.inner, geo.outer, order_devices, each, rows, width)
     )
     return spectra.reshape(order_devices * geo.outer * geo.inner, each, rows, width)
 
@@ -563,7 +565,7 @@
     block = jax.ShapeDtypeStruct((outer - 1, m_local, band_rows, geo.block_window), jnp.float32)
     to_rows, *blocks = call(
         functools.partial(synthesise_rest, geo),
-        (jax.ShapeDtypeStruct((order_devices, outer, m_local, rows_here, line), jnp.float32),)
+        (jax.ShapeDtypeStruct((outer, order_devices, m_local, rows_here, line), jnp.float32),)
         + (block,) * inner,
         [WHOLE] * (outer + 1),
         own_flops * (outer - 1),
@@ -573,7 +575,7 @@
     rest_legs += [rotate(blocks[s], "inner", inner, s) for s in range(1, inner)]
     grid_in = lax.all_to_all(
         to_rows.reshape(order_devices * outer, m_local, rows_here, line),
-        ("order", "outer"),
+        ("outer", "order"),
         split_axis=0,
         concat_axis=0,
         tiled=True,
@@ -592,7 +594,7 @@
     else:
         to_orders = plain_grid(geo, grid_in, order_of, class_idx, land, class_weight, period)
     spectra = lax.all_to_all(
-        to_orders, ("order", "outer", "inner"), split_axis=0, concat_axis=0, tiled=True
+        to_orders, ("inner", "outer", "order"), split_axis=0, concat_axis=0, tiled=True
     )
     shares = [spectra] + [rotate(spectra, "inner", inner, s) for s in range(1, inner)]
     coefficients = jax.ShapeDtypeStruct(position.shape, jnp.float32)
@@ -622,7 +624,7 @@
         )
         applied.append(result)
     sums = lax.all_to_all(
-        sums, ("order", "outer", "inner"), split_axis=0, concat_axis=0, tiled=True
+        sums, ("inner", "outer", "order"), split_axis=0, concat_axis=0, tiled=True
     )
     return call(
         functools.partial(update, geo),

time: 57.4 us -> 57.3 us (level)
  no operation moved by 1% of the time
where the time goes in v7:
time: 57.3 us; the launch traced here: 57 us
  blocking collectives  34.1 us (60%)
  Pallas kernels  10.5 us (18%)
  waiting for transfers between devices  8.31 us (15%)
  starting transfers between devices  3.31 us (6%)
  between operations  0.75 us (1%)
    all_to_all x1, blocking collectives, shards(): lax.all_to_all(to_rows.reshape(order_devices * outer, m_local, rows_here,...  15 us
    all_to_all x1, blocking collectives, shards(): lax.all_to_all(to_orders, ('inner', 'outer', 'order'), split_axis=0, conc...  9.87 us
    all_to_all x1, blocking collectives, shards(): lax.all_to_all(sums, ('inner', 'outer', 'order'), split_axis=0, concat_ax...  9.22 us
    ppermute x5, waiting for transfers between devices, rotate(): return lax.ppermute(x, axis, [(i, (i + shift) % size) for i in range(size)])  8.31 us
    pallas_call x1, Pallas kernels, shards(): call(functools.partial(prepare, geo), (jax.ShapeDtypeStruct((m_local, 2 *...  3.31 us
    ppermute x5, starting transfers between devices, rotate(): return lax.ppermute(x, axis, [(i, (i + shift) % size) for i in range(size)])  3.31 us
    pallas_call x1, Pallas kernels, shards(): call(functools.partial(cut_windows, geo), (cut,) * (outer - 1), [IN_HBM],...  1.67 us
    pallas_call x1, Pallas kernels, shards(): call(functools.partial(update, geo), (coefficients,) * 3, [WHOLE] * (5 +...  1.61 us
  transfers between devices with their start and end apart: 5, of which 3 were waited for; matrix products, arithmetic and copies ran while one was open for 0% of the time, Pallas kernels for 10%

profile of v7, /device:TPU:0, one launch (start us, length us, event | category | flops | bytes accessed | tf_op | source)
XLA Modules:
  0.0 57.0 jit_solution(2705644846040283297)
XLA Ops:
  0.6 0.0 copy-start.5
  0.6 0.0 copy-start
  0.7 0.0 copy-start.8
  0.7 0.0 copy-start.3
  0.7 0.0 copy-start.4
  0.7 0.0 copy-start.6
  0.7 1.7 %shard_map.122 = f32[64,2176]{1,0:T(8,128)S(1)} custom-call(f32[2,64,2160]{2,1,0:T(8,128)} %bitcast.5), custom_call_target="tpu_custom_call" | custom-call | flops 147456 | bytes 2359296 | tf_op jit(solution)/shard_map/pallas_call | solution.py:515
  2.4 3.0 %collective-permute-start.1 = (f32[64,2176]{1,0:T(8,128)S(1)}, f32[64,2176]{1,0:T(8,128)S(1)}, u32[]{:S(2)}, u32[]{:S(2)}) collective-permute-start(f32[64,2176]{1,0:T(8,128)S(1)} %shard_map.122), channel_id=1, source_target_pairs={{0,2},{2,0},{1,3},{3,1},{4,6},{6,4},{5,7},{7,5},{8,10},{10,8},{9,1... | collective-permute-start | bytes 1671176 | tf_op jit(solution)/shard_map/ppermute | solution.py:459
  5.4 0.0 copy-done
  5.4 0.0 collective-permute-start
  5.4 0.0 copy-done.8
  5.4 0.1 copy.13.value_ref
  5.5 0.0 copy-done.5
  5.5 0.0 copy-done.3
  5.5 0.0 copy-done.4
  5.5 1.4 %shard_map.123.table_ref = f32[4,32,8,128]{3,2,1,0:T(8,128)S(1)} custom-call(s32[8,4320]{1,0:T(8,128)S(1)} %copy-done.3, s32[8,4320]{1,0:T(8,128)S(1)} %copy-done.4, f32[16,2]{1,0:T(8,128)S(1)} %copy.13.value_ref, f32[128,128]{1,0:T(8,128)S(1)} %copy-done.5), custom_call_target="tpu_custom_call" | custom-call | flops 1 | bytes 1 | tf_op jit(solution)/shard_map/pallas_call | solution.py:535
  6.9 0.6 %collective-permute-done.refs_1_ = f32[2,2,64,540]{3,2,1,0:T(8,128)S(1)} collective-permute-done((f32[2,2,64,540]{3,2,1,0:T(8,128)S(1)}, f32[2,2,64,540]{3,2,1,0:T(8,128)S(1)}, u32[]{:S(2)}, u32[]{:S(2)}) %collective-permute-start) | collective-permute-done | bytes 552992 | tf_op jit(solution)/shard_map/ppermute | solution.py:459
  7.5 0.0 copy-done.6
  7.5 3.3 %shard_map.121 = (bf16[2,256,1152]{2,1,0:T(8,128)(2,1)S(1)}, f32[2,64,128]{2,1,0:T(8,128)S(1)}, f32[2,8,540]{2,1,0:T(8,128)S(1)}, f32[2,64,640]{2,1,0:T(8,128)S(1)}, f32[2,64,640]{2,1,0:T(8,128)S(1)}) custom-call(s32[16]{0:T(128)S(1)} %copy-done.6, f32[2,64,2160]{2,1,0:T(8,128)} %bitcast.6, f32[2,2,64,540]{3,2,1,0:T(8,128)S(1)} %copy-done, ...), custom_call_target="tpu_custom_call" | custom-call | flops 1 | bytes 1 | tf_op jit(solution)/shard_map/pallas_call | solution.py:546
  10.8 0.2 collective-permute-start.2
  11.0 7.0 %collective-permute-done.1.refs_0_ = f32[64,2176]{1,0:T(8,128)S(1)} collective-permute-done((f32[64,2176]{1,0:T(8,128)S(1)}, f32[64,2176]{1,0:T(8,128)S(1)}, u32[]{:S(2)}, u32[]{:S(2)}) %collective-permute-start.1) | collective-permute-done | bytes 557088 | tf_op jit(solution)/shard_map/ppermute | solution.py:459
  18.0 0.0 copy-start.7
  18.0 0.0 copy-start.1
  18.0 0.5 shard_map.124
  18.6 0.1 collective-permute-start.3
  18.7 15.0 %all_to_all.15.recv_ref = f32[16,2,8,128]{3,2,1,0:T(8,128)S(1)} all-to-all(f32[16,2,8,128]{3,2,1,0:T(8,128)S(1)} %bitcast.3), channel_id=1, replica_groups=mesh['order'=8,'outer'=2,'inner'=2] {'outer','order'}, dimensions={0} | all-to-all | bytes 262144 | tf_op jit(solution)/shard_map/all_to_all | solution.py:576
  33.6 0.0 collective-permute-done.2.refs_1_
  33.6 0.0 collective-permute-done.3.refs_3_
  33.6 0.4 shard_map.125
  34.0 9.9 %all_to_all.16.recv_ref = f32[32,1,8,128]{3,2,1,0:T(8,128)S(1)} all-to-all(f32[32,1,8,128]{3,2,1,0:T(8,128)S(1)} %shard_map.125), channel_id=1, replica_groups=mesh['order'=8,'outer'=2,'inner'=2] {'inner','outer','order'}, dimensions={0} | all-to-all | bytes 262144 | tf_op jit(solution)/shard_map/all_to_all | solution.py:596
  43.9 0.0 collective-permute-start.4
  43.9 0.0 copy-done.7
  43.9 0.0 copy-done.1
  43.9 0.6 %shard_map.126 = (f32[1,2,64,540]{3,2,1,0:T(8,128)S(1)}, f32[256,128]{1,0:T(8,128)S(1)}) custom-call(f32[2,8,540]{2,1,0:T(8,128)S(1)} %get-tuple-element.22.valid_ref, f32[32,1,8,128]{3,2,1,0:T(8,128)S(1)} %all_to_all.16.recv_ref, f32[2,64,640]{2,1,0:T(8,128)S(1)} %get-tuple-element.33.refs_0_, f32[2,64,640]{2,1,0:T(8,128)S(1)} %collective-permute-done.2.refs_1_, ...), custom_call_target="tpu_custom_call" | custom-call | flops 125829120 | bytes 1105920 | tf_op jit(solution)/shard_map/pallas_call | solution.py:609
  44.6 0.7 %collective-permute-done.4.recv_ref = f32[32,1,8,128]{3,2,1,0:T(8,128)S(1)} collective-permute-done((f32[32,1,8,128]{3,2,1,0:T(8,128)S(1)}, f32[32,1,8,128]{3,2,1,0:T(8,128)S(1)}, u32[]{:S(2)}, u32[]{:S(2)}) %collective-permute-start.4) | collective-permute-done | bytes 131104 | tf_op jit(solution)/shard_map/ppermute | solution.py:459
  45.2 0.0 copy-start.2
  45.3 0.9 %shard_map.127 = (f32[1,2,64,540]{3,2,1,0:T(8,128)S(1)}, f32[32,1,256]{2,1,0:T(1,128)S(1)}) custom-call(f32[2,8,540]{2,1,0:T(8,128)S(1)} %get-tuple-element.22.valid_ref, f32[32,1,8,128]{3,2,1,0:T(8,128)S(1)} %collective-permute-done.4.recv_ref, f32[2,64,640]{2,1,0:T(8,128)S(1)} %get-tuple-element.33.refs_0_, ...), custom_call_target="tpu_custom_call" | custom-call | flops 125829120 | bytes 1105920 | tf_op jit(solution)/shard_map/pallas_call | solution.py:609
  46.2 9.2 %all_to_all.17.sums_ref = f32[32,1,256]{2,1,0:T(1,128)S(1)} all-to-all(f32[32,1,256]{2,1,0:T(1,128)S(1)} %get-tuple-element.38), channel_id=1, replica_groups=mesh['order'=8,'outer'=2,'inner'=2] {'inner','outer','order'}, dimensions={0} | all-to-all | bytes 65536 | tf_op jit(solution)/shard_map/all_to_all | solution.py:626
  55.4 0.0 copy-done.2
  55.4 1.6 %shard_map.128 = (f32[2,2,64,540]{3,2,1,0:T(8,128)}, f32[2,2,64,540]{3,2,1,0:T(8,128)}, f32[2,2,64,540]{3,2,1,0:T(8,128)}) custom-call(f32[2,8,540]{2,1,0:T(8,128)S(1)} %get-tuple-element.22.valid_ref, f32[32,1,256]{2,1,0:T(1,128)S(1)} %all_to_all.17.sums_ref, f32[1,2,64,540]{3,2,1,0:T(8,128)S(1)} %get-tuple-element.39.refs_0_, ...), custom_call_target="tpu_custom_call" | custom-call | flops 1382400 | bytes 3870720 | tf_op jit(solution)/shard_map/pallas_call | solution.py:629
  (1 shorter events, 0.0 us)
Async XLA Ops:
  0.6 4.9 %copy-start.5 = (f32[128,128]{1,0:T(8,128)S(1)}, f32[128,128]{1,0:T(8,128)}, u32[]{:S(2)}) copy-start(f32[128,128]{1,0:T(8,128)} %constant.2.clone.basis_ref) | copy-start | bytes 196612
  0.6 4.8 %copy-start = (f32[2,2,64,540]{3,2,1,0:T(8,128)S(1)}, f32[2,2,64,540]{3,2,1,0:T(8,128)}, u32[]{:S(2)}) copy-start(f32[2,2,64,540]{3,2,1,0:T(8,128)} %refs_3_.1) | copy-start | bytes 1658884
  0.7 4.8 %copy-start.8 = (f32[16,2]{0,1:T(2,128)S(1)}, f32[16,2]{0,1:T(2,128)}, u32[]{:S(2)}) copy-start(f32[16,2]{0,1:T(2,128)} %param.17) | copy-start | bytes 388
  0.7 4.8 %copy-start.3 = (s32[8,4320]{1,0:T(8,128)S(1)}, s32[8,4320]{1,0:T(8,128)}, u32[]{:S(2)}) copy-start(s32[8,4320]{1,0:T(8,128)} %class_ref.1) | copy-start | bytes 414724
  0.7 4.8 %copy-start.4 = (s32[8,4320]{1,0:T(8,128)S(1)}, s32[8,4320]{1,0:T(8,128)}, u32[]{:S(2)}) copy-start(s32[8,4320]{1,0:T(8,128)} %land_ref.1) | copy-start | bytes 414724
  0.7 6.8 %copy-start.6 = (s32[16]{0:T(128)S(1)}, s32[16]{0:T(128)}, u32[]{:S(2)}) copy-start(s32[16]{0:T(128)} %order_ref.1) | copy-start | bytes 196
  2.4 15.7 %collective-permute-start.1 = (f32[64,2176]{1,0:T(8,128)S(1)}, f32[64,2176]{1,0:T(8,128)S(1)}, u32[]{:S(2)}, u32[]{:S(2)}) collective-permute-start(f32[64,2176]{1,0:T(8,128)S(1)} %shard_map.122), channel_id=1, source_target_pairs={{0,2},{2,0},{1,3},{3,1},{4,6},{6,4},{5,7},{7,5},{8,10},{10,8},{9,1... | collective-permute-start | bytes 1671176 | tf_op jit(solution)/shard_map/ppermute | solution.py:459
  5.4 2.1 %collective-permute-start = (f32[2,2,64,540]{3,2,1,0:T(8,128)S(1)}, f32[2,2,64,540]{3,2,1,0:T(8,128)S(1)}, u32[]{:S(2)}, u32[]{:S(2)}) collective-permute-start(f32[2,2,64,540]{3,2,1,0:T(8,128)S(1)} %copy-done), channel_id=1, source_target_pairs={{0,1},{1,0},{2,3},{3,2},{4,5},{5,4},{6,7},{7,6},{8,9},{9,8},{10,11... | collective-permute-start | bytes 1658888 | tf_op jit(solution)/shard_map/ppermute | solution.py:459
  10.8 22.8 %collective-permute-start.2 = (f32[2,64,640]{2,1,0:T(8,128)S(1)}, f32[2,64,640]{2,1,0:T(8,128)S(1)}, u32[]{:S(2)}, u32[]{:S(2)}) collective-permute-start(f32[2,64,640]{2,1,0:T(8,128)S(1)} %get-tuple-element.28), channel_id=1, source_target_pairs={{0,1},{1,0},{2,3},{3,2},{4,5},{5,4},{6,7},{7,6},{8,9},{9,8},{10,11... | collective-permute-start | bytes 983048 | tf_op jit(solution)/shard_map/ppermute | solution.py:459
  18.0 25.9 %copy-start.7 = (f32[540]{0:T(1024)S(1)}, f32[540]{0:T(1024)}, u32[]{:S(2)}) copy-start(f32[540]{0:T(1024)} %param.18) | copy-start | bytes 6484
  18.0 25.9 %copy-start.1 = (f32[2,2,64,540]{3,2,1,0:T(8,128)S(1)}, f32[2,2,64,540]{3,2,1,0:T(8,128)}, u32[]{:S(2)}) copy-start(f32[2,2,64,540]{3,2,1,0:T(8,128)} %refs_4_.5) | copy-start | bytes 1658884
  18.6 15.1 %collective-permute-start.3 = (f32[1,2,64,640]{3,2,1,0:T(8,128)S(1)}, f32[1,2,64,640]{3,2,1,0:T(8,128)S(1)}, u32[]{:S(2)}, u32[]{:S(2)}) collective-permute-start(f32[1,2,64,640]{3,2,1,0:T(8,128)S(1)} %get-tuple-element.30), channel_id=1, source_target_pairs={{0,1},{1,0},{2,3},{3,2},{4,5},{5,4},{6,7},{7,6},{8,9},{9,8},{10,11... | collective-permute-start | bytes 983048 | tf_op jit(solution)/shard_map/ppermute | solution.py:459
  43.9 1.3 %collective-permute-start.4 = (f32[32,1,8,128]{3,2,1,0:T(8,128)S(1)}, f32[32,1,8,128]{3,2,1,0:T(8,128)S(1)}, u32[]{:S(2)}, u32[]{:S(2)}) collective-permute-start(f32[32,1,8,128]{3,2,1,0:T(8,128)S(1)} %all_to_all.16.recv_ref), channel_id=1, source_target_pairs={{0,1},{1,0},{2,3},{3,2},{4,5},{5,4},{6,7},{7,6},{8,9},{9,8},{10,11... | collective-permute-start | bytes 393224 | tf_op jit(solution)/shard_map/ppermute | solution.py:459
  45.2 10.2 %copy-start.2 = (f32[2,2,64,540]{3,2,1,0:T(8,128)S(1)}, f32[2,2,64,540]{3,2,1,0:T(8,128)}, u32[]{:S(2)}) copy-start(f32[2,2,64,540]{3,2,1,0:T(8,128)} %refs_2_.1) | copy-start | bytes 1658884

commit v8 on v7

--- a/solution.py
+++ b/solution.py
@@ -109,17 +109,21 @@
 
 
 def cut_windows(geo, leg_hbm, *refs):
-    send_refs, (leg_ref, sem) = refs[:-2], refs[-2:]
-    fetch = pltpu.make_async_copy(leg_hbm, leg_ref, sem)
-    fetch.start()
+    send_refs, (leg_ref, sems) = refs[:-2], refs[-2:]
+    m_local, rows = leg_ref.shape[:2]
+    fetches = [
+        pltpu.make_async_copy(leg_hbm.at[m], leg_ref.at[m], sems.at[m]) for m in range(m_local)
+    ]
+    for fetch in fetches:
+        fetch.start()
     a = lax.axis_index("outer")
-    fetch.wait()
-    m_local, rows = leg_ref.shape[:2]
     lane = lax.broadcasted_iota(jnp.int32, (rows, LANES), 1)
     for shift, ref in enumerate(send_refs, 1):
         block = lax.rem(a + shift, geo.outer)
         tiles = [None] * geo.rest_tiles
         for m in range(m_local):
+            if shift == 1:
+                fetches[m].wait()
             window = exact_window(geo, leg_ref, m, block)
             ref[:, m * geo.main : (m + 1) * geo.main] = window[:, : geo.main]
             if geo.rest:
@@ -347,20 +351,21 @@
         residual = res_ref[first + i, s] * valid
         applied = app_ref[i, s] * valid + damping * direction
         app_ref[i, s] = applied
-        terms = (
-            residual * residual,
-            direction * applied,
-            residual * applied,
-            applied * applied,
-        )
+        terms = (direction * applied, residual * applied, applied * applied)
         return tuple(old + fold(t) for old, t in zip(sums, terms))
 
+    def norm(at, old):
+        m, s = lax.div(at, sin_cos), lax.rem(at, sin_cos)
+        residual = res_ref[m, s] * valid_ref[m, 0:1]
+        return old + fold(residual * residual)
+
+    zero = jnp.zeros((samples, LANES), jnp.float32)
     if shift:
-        start = tuple(before_ref[i * samples : (i + 1) * samples] for i in range(4))
+        before, *start = [before_ref[i * samples : (i + 1) * samples] for i in range(4)]
     else:
-        start = (jnp.zeros((samples, LANES), jnp.float32),) * 4
-    sums = lax.fori_loop(0, each * sin_cos, apply, start)
-    stacked = jnp.concatenate(sums, axis=0)
+        before, start = lax.fori_loop(0, geo.m_local * sin_cos, norm, zero), [zero] * 3
+    sums = lax.fori_loop(0, each * sin_cos, apply, tuple(start))
+    stacked = jnp.concatenate((before,) + sums, axis=0)
     if shift < geo.inner - 1:
         sums_ref[...] = stacked
     else:
@@ -518,7 +523,7 @@
         [IN_HBM],
         m_local * band_rows * geo.window,
         8 * outer * m_local * band_rows * geo.window,
-        leg_scratch,
+        [pltpu.VMEM(by_row.shape, jnp.float32), pltpu.SemaphoreType.DMA((m_local,))],
     )(far(by_row))
     received = [rotate(cuts[s - 1], "outer", outer, s) for s in range(1, outer)]
     stride = longitudes // (2 * orders)

time: 57.3 us -> 57.1 us (level)
  no operation moved by 1% of the time
where the time goes in v8:
time: 57.1 us; the launch traced here: 56.9 us
  blocking collectives  34.1 us (60%)
  Pallas kernels  10.4 us (18%)
  waiting for transfers between devices  8.23 us (14%)
  starting transfers between devices  3.32 us (6%)
  between operations  0.76 us (1%)
    all_to_all x1, blocking collectives, shards(): lax.all_to_all(to_rows.reshape(order_devices * outer, m_local, rows_here,...  15 us
    all_to_all x1, blocking collectives, shards(): lax.all_to_all(to_orders, ('inner', 'outer', 'order'), split_axis=0, conc...  9.87 us
    all_to_all x1, blocking collectives, shards(): lax.all_to_all(sums, ('inner', 'outer', 'order'), split_axis=0, concat_ax...  9.22 us
    ppermute x5, waiting for transfers between devices, rotate(): return lax.ppermute(x, axis, [(i, (i + shift) % size) for i in range(size)])  8.23 us
    ppermute x5, starting transfers between devices, rotate(): return lax.ppermute(x, axis, [(i, (i + shift) % size) for i in range(size)])  3.32 us
    pallas_call x1, Pallas kernels, shards(): call(functools.partial(prepare, geo), (jax.ShapeDtypeStruct((m_local, 2 *...  3.3 us
    pallas_call x2, Pallas kernels, shards(): call(functools.partial(project, geo, shift), (jax.ShapeDtypeStruct(part,...  1.64 us
    pallas_call x1, Pallas kernels, shards(): call(functools.partial(update, geo), (coefficients,) * 3, [WHOLE] * (5 +...  1.61 us
  transfers between devices with their start and end apart: 5, of which 3 were waited for; matrix products, arithmetic and copies ran while one was open for 0% of the time, Pallas kernels for 10%

profile of v8, /device:TPU:0, one launch (start us, length us, event | category | flops | bytes accessed | tf_op | source)
XLA Modules:
  0.0 56.9 jit_solution(2467297416856345811)
XLA Ops:
  0.6 0.0 copy-start.5
  0.6 0.0 copy-start
  0.7 0.0 copy-start.8
  0.7 0.0 copy-start.3
  0.7 0.0 copy-start.4
  0.7 0.0 copy-start.6
  0.7 1.6 %shard_map.122 = f32[64,2176]{1,0:T(8,128)S(1)} custom-call(f32[2,64,2160]{2,1,0:T(8,128)} %bitcast.5), custom_call_target="tpu_custom_call" | custom-call | flops 147456 | bytes 2359296 | tf_op jit(solution)/shard_map/pallas_call | solution.py:520
  2.3 3.0 %collective-permute-start.1 = (f32[64,2176]{1,0:T(8,128)S(1)}, f32[64,2176]{1,0:T(8,128)S(1)}, u32[]{:S(2)}, u32[]{:S(2)}) collective-permute-start(f32[64,2176]{1,0:T(8,128)S(1)} %shard_map.122), channel_id=1, source_target_pairs={{0,2},{2,0},{1,3},{3,1},{4,6},{6,4},{5,7},{7,5},{8,10},{10,8},{9,1... | collective-permute-start | bytes 1671176 | tf_op jit(solution)/shard_map/ppermute | solution.py:464
  5.3 0.0 copy-done
  5.3 0.0 collective-permute-start
  5.3 0.0 copy-done.8
  5.3 0.1 copy.13.value_ref
  5.4 0.0 copy-done.5
  5.4 0.0 copy-done.3
  5.4 0.0 copy-done.4
  5.4 1.4 %shard_map.123.table_ref = f32[4,32,8,128]{3,2,1,0:T(8,128)S(1)} custom-call(s32[8,4320]{1,0:T(8,128)S(1)} %copy-done.3, s32[8,4320]{1,0:T(8,128)S(1)} %copy-done.4, f32[16,2]{1,0:T(8,128)S(1)} %copy.13.value_ref, f32[128,128]{1,0:T(8,128)S(1)} %copy-done.5), custom_call_target="tpu_custom_call" | custom-call | flops 1 | bytes 1 | tf_op jit(solution)/shard_map/pallas_call | solution.py:540
  6.8 0.6 %collective-permute-done.refs_1_ = f32[2,2,64,540]{3,2,1,0:T(8,128)S(1)} collective-permute-done((f32[2,2,64,540]{3,2,1,0:T(8,128)S(1)}, f32[2,2,64,540]{3,2,1,0:T(8,128)S(1)}, u32[]{:S(2)}, u32[]{:S(2)}) %collective-permute-start) | collective-permute-done | bytes 552992 | tf_op jit(solution)/shard_map/ppermute | solution.py:464
  7.4 0.0 copy-done.6
  7.4 3.3 %shard_map.121 = (bf16[2,256,1152]{2,1,0:T(8,128)(2,1)S(1)}, f32[2,64,128]{2,1,0:T(8,128)S(1)}, f32[2,8,540]{2,1,0:T(8,128)S(1)}, f32[2,64,640]{2,1,0:T(8,128)S(1)}, f32[2,64,640]{2,1,0:T(8,128)S(1)}) custom-call(s32[16]{0:T(128)S(1)} %copy-done.6, f32[2,64,2160]{2,1,0:T(8,128)} %bitcast.6, f32[2,2,64,540]{3,2,1,0:T(8,128)S(1)} %copy-done, ...), custom_call_target="tpu_custom_call" | custom-call | flops 1 | bytes 1 | tf_op jit(solution)/shard_map/pallas_call | solution.py:551
  10.7 0.2 collective-permute-start.2
  10.9 7.0 %collective-permute-done.1.refs_0_ = f32[64,2176]{1,0:T(8,128)S(1)} collective-permute-done((f32[64,2176]{1,0:T(8,128)S(1)}, f32[64,2176]{1,0:T(8,128)S(1)}, u32[]{:S(2)}, u32[]{:S(2)}) %collective-permute-start.1) | collective-permute-done | bytes 557088 | tf_op jit(solution)/shard_map/ppermute | solution.py:464
  17.9 0.0 copy-start.7
  17.9 0.0 copy-start.1
  17.9 0.5 shard_map.124
  18.5 0.1 collective-permute-start.3
  18.6 15.0 %all_to_all.15.recv_ref = f32[16,2,8,128]{3,2,1,0:T(8,128)S(1)} all-to-all(f32[16,2,8,128]{3,2,1,0:T(8,128)S(1)} %bitcast.3), channel_id=1, replica_groups=mesh['order'=8,'outer'=2,'inner'=2] {'outer','order'}, dimensions={0} | all-to-all | bytes 262144 | tf_op jit(solution)/shard_map/all_to_all | solution.py:581
  33.5 0.0 collective-permute-done.2.refs_1_
  33.5 0.0 collective-permute-done.3.refs_3_
  33.5 0.4 shard_map.125
  33.9 9.9 %all_to_all.16.recv_ref = f32[32,1,8,128]{3,2,1,0:T(8,128)S(1)} all-to-all(f32[32,1,8,128]{3,2,1,0:T(8,128)S(1)} %shard_map.125), channel_id=1, replica_groups=mesh['order'=8,'outer'=2,'inner'=2] {'inner','outer','order'}, dimensions={0} | all-to-all | bytes 262144 | tf_op jit(solution)/shard_map/all_to_all | solution.py:601
  43.8 0.0 collective-permute-start.4
  43.8 0.0 copy-done.7
  43.8 0.0 copy-done.1
  43.8 0.7 %shard_map.126 = (f32[1,2,64,540]{3,2,1,0:T(8,128)S(1)}, f32[256,128]{1,0:T(8,128)S(1)}) custom-call(f32[2,8,540]{2,1,0:T(8,128)S(1)} %get-tuple-element.22.valid_ref, f32[32,1,8,128]{3,2,1,0:T(8,128)S(1)} %all_to_all.16.recv_ref, f32[2,64,640]{2,1,0:T(8,128)S(1)} %get-tuple-element.33.refs_0_, f32[2,64,640]{2,1,0:T(8,128)S(1)} %collective-permute-done.2.refs_1_, ...), custom_call_target="tpu_custom_call" | custom-call | flops 125829120 | bytes 1105920 | tf_op jit(solution)/shard_map/pallas_call | solution.py:614
  44.6 0.6 %collective-permute-done.4.recv_ref = f32[32,1,8,128]{3,2,1,0:T(8,128)S(1)} collective-permute-done((f32[32,1,8,128]{3,2,1,0:T(8,128)S(1)}, f32[32,1,8,128]{3,2,1,0:T(8,128)S(1)}, u32[]{:S(2)}, u32[]{:S(2)}) %collective-permute-start.4) | collective-permute-done | bytes 131104 | tf_op jit(solution)/shard_map/ppermute | solution.py:464
  45.2 0.0 copy-start.2
  45.2 0.9 %shard_map.127 = (f32[1,2,64,540]{3,2,1,0:T(8,128)S(1)}, f32[32,1,256]{2,1,0:T(1,128)S(1)}) custom-call(f32[2,8,540]{2,1,0:T(8,128)S(1)} %get-tuple-element.22.valid_ref, f32[32,1,8,128]{3,2,1,0:T(8,128)S(1)} %collective-permute-done.4.recv_ref, f32[2,64,640]{2,1,0:T(8,128)S(1)} %get-tuple-element.33.refs_0_, ...), custom_call_target="tpu_custom_call" | custom-call | flops 125829120 | bytes 1105920 | tf_op jit(solution)/shard_map/pallas_call | solution.py:614
  46.1 9.2 %all_to_all.17.sums_ref = f32[32,1,256]{2,1,0:T(1,128)S(1)} all-to-all(f32[32,1,256]{2,1,0:T(1,128)S(1)} %get-tuple-element.38), channel_id=1, replica_groups=mesh['order'=8,'outer'=2,'inner'=2] {'inner','outer','order'}, dimensions={0} | all-to-all | bytes 65536 | tf_op jit(solution)/shard_map/all_to_all | solution.py:631
  55.3 0.0 copy-done.2
  55.3 1.6 %shard_map.128 = (f32[2,2,64,540]{3,2,1,0:T(8,128)}, f32[2,2,64,540]{3,2,1,0:T(8,128)}, f32[2,2,64,540]{3,2,1,0:T(8,128)}) custom-call(f32[2,8,540]{2,1,0:T(8,128)S(1)} %get-tuple-element.22.valid_ref, f32[32,1,256]{2,1,0:T(1,128)S(1)} %all_to_all.17.sums_ref, f32[1,2,64,540]{3,2,1,0:T(8,128)S(1)} %get-tuple-element.39.refs_0_, ...), custom_call_target="tpu_custom_call" | custom-call | flops 1382400 | bytes 3870720 | tf_op jit(solution)/shard_map/pallas_call | solution.py:634
  (1 shorter events, 0.0 us)
Async XLA Ops:
  0.6 4.8 %copy-start.5 = (f32[128,128]{1,0:T(8,128)S(1)}, f32[128,128]{1,0:T(8,128)}, u32[]{:S(2)}) copy-start(f32[128,128]{1,0:T(8,128)} %constant.2.clone.basis_ref) | copy-start | bytes 196612
  0.6 4.7 %copy-start = (f32[2,2,64,540]{3,2,1,0:T(8,128)S(1)}, f32[2,2,64,540]{3,2,1,0:T(8,128)}, u32[]{:S(2)}) copy-start(f32[2,2,64,540]{3,2,1,0:T(8,128)} %refs_3_.1) | copy-start | bytes 1658884
  0.7 4.7 %copy-start.8 = (f32[16,2]{0,1:T(2,128)S(1)}, f32[16,2]{0,1:T(2,128)}, u32[]{:S(2)}) copy-start(f32[16,2]{0,1:T(2,128)} %param.17) | copy-start | bytes 388
  0.7 4.7 %copy-start.3 = (s32[8,4320]{1,0:T(8,128)S(1)}, s32[8,4320]{1,0:T(8,128)}, u32[]{:S(2)}) copy-start(s32[8,4320]{1,0:T(8,128)} %class_ref.1) | copy-start | bytes 414724
  0.7 4.7 %copy-start.4 = (s32[8,4320]{1,0:T(8,128)S(1)}, s32[8,4320]{1,0:T(8,128)}, u32[]{:S(2)}) copy-start(s32[8,4320]{1,0:T(8,128)} %land_ref.1) | copy-start | bytes 414724
  0.7 6.7 %copy-start.6 = (s32[16]{0:T(128)S(1)}, s32[16]{0:T(128)}, u32[]{:S(2)}) copy-start(s32[16]{0:T(128)} %order_ref.1) | copy-start | bytes 196
  2.3 15.7 %collective-permute-start.1 = (f32[64,2176]{1,0:T(8,128)S(1)}, f32[64,2176]{1,0:T(8,128)S(1)}, u32[]{:S(2)}, u32[]{:S(2)}) collective-permute-start(f32[64,2176]{1,0:T(8,128)S(1)} %shard_map.122), channel_id=1, source_target_pairs={{0,2},{2,0},{1,3},{3,1},{4,6},{6,4},{5,7},{7,5},{8,10},{10,8},{9,1... | collective-permute-start | bytes 1671176 | tf_op jit(solution)/shard_map/ppermute | solution.py:464
  5.3 2.1 %collective-permute-start = (f32[2,2,64,540]{3,2,1,0:T(8,128)S(1)}, f32[2,2,64,540]{3,2,1,0:T(8,128)S(1)}, u32[]{:S(2)}, u32[]{:S(2)}) collective-permute-start(f32[2,2,64,540]{3,2,1,0:T(8,128)S(1)} %copy-done), channel_id=1, source_target_pairs={{0,1},{1,0},{2,3},{3,2},{4,5},{5,4},{6,7},{7,6},{8,9},{9,8},{10,11... | collective-permute-start | bytes 1658888 | tf_op jit(solution)/shard_map/ppermute | solution.py:464
  10.7 22.8 %collective-permute-start.2 = (f32[2,64,640]{2,1,0:T(8,128)S(1)}, f32[2,64,640]{2,1,0:T(8,128)S(1)}, u32[]{:S(2)}, u32[]{:S(2)}) collective-permute-start(f32[2,64,640]{2,1,0:T(8,128)S(1)} %get-tuple-element.28), channel_id=1, source_target_pairs={{0,1},{1,0},{2,3},{3,2},{4,5},{5,4},{6,7},{7,6},{8,9},{9,8},{10,11... | collective-permute-start | bytes 983048 | tf_op jit(solution)/shard_map/ppermute | solution.py:464
  17.9 25.9 %copy-start.7 = (f32[540]{0:T(1024)S(1)}, f32[540]{0:T(1024)}, u32[]{:S(2)}) copy-start(f32[540]{0:T(1024)} %param.18) | copy-start | bytes 6484
  17.9 25.9 %copy-start.1 = (f32[2,2,64,540]{3,2,1,0:T(8,128)S(1)}, f32[2,2,64,540]{3,2,1,0:T(8,128)}, u32[]{:S(2)}) copy-start(f32[2,2,64,540]{3,2,1,0:T(8,128)} %refs_4_.5) | copy-start | bytes 1658884
  18.5 15.1 %collective-permute-start.3 = (f32[1,2,64,640]{3,2,1,0:T(8,128)S(1)}, f32[1,2,64,640]{3,2,1,0:T(8,128)S(1)}, u32[]{:S(2)}, u32[]{:S(2)}) collective-permute-start(f32[1,2,64,640]{3,2,1,0:T(8,128)S(1)} %get-tuple-element.30), channel_id=1, source_target_pairs={{0,1},{1,0},{2,3},{3,2},{4,5},{5,4},{6,7},{7,6},{8,9},{9,8},{10,11... | collective-permute-start | bytes 983048 | tf_op jit(solution)/shard_map/ppermute | solution.py:464
  43.8 1.3 %collective-permute-start.4 = (f32[32,1,8,128]{3,2,1,0:T(8,128)S(1)}, f32[32,1,8,128]{3,2,1,0:T(8,128)S(1)}, u32[]{:S(2)}, u32[]{:S(2)}) collective-permute-start(f32[32,1,8,128]{3,2,1,0:T(8,128)S(1)} %all_to_all.16.recv_ref), channel_id=1, source_target_pairs={{0,1},{1,0},{2,3},{3,2},{4,5},{5,4},{6,7},{7,6},{8,9},{9,8},{10,11... | collective-permute-start | bytes 393224 | tf_op jit(solution)/shard_map/ppermute | solution.py:464
  45.2 10.1 %copy-start.2 = (f32[2,2,64,540]{3,2,1,0:T(8,128)S(1)}, f32[2,2,64,540]{3,2,1,0:T(8,128)}, u32[]{:S(2)}) copy-start(f32[2,2,64,540]{3,2,1,0:T(8,128)} %refs_2_.1) | copy-start | bytes 1658884

commit v9 on v7

--- a/solution.py
+++ b/solution.py
@@ -624,7 +624,7 @@
         )
         applied.append(result)
     sums = lax.all_to_all(
-        sums, ("inner", "outer", "order"), split_axis=0, concat_axis=0, tiled=True
+        sums, ("order", "outer", "inner"), split_axis=0, concat_axis=0, tiled=True
     )
     return call(
         functools.partial(update, geo),

time: 57.3 us -> 57.3 us (level)
  no operation moved by 1% of the time
where the time goes in v9:
time: 57.3 us; the launch traced here: 57.1 us
  blocking collectives  34.1 us (60%)
  Pallas kernels  10.5 us (18%)
  waiting for transfers between devices  8.31 us (15%)
  starting transfers between devices  3.31 us (6%)
  between operations  0.76 us (1%)
    all_to_all x1, blocking collectives, shards(): lax.all_to_all(to_rows.reshape(order_devices * outer, m_local, rows_here,...  15 us
    all_to_all x1, blocking collectives, shards(): lax.all_to_all(to_orders, ('inner', 'outer', 'order'), split_axis=0, conc...  9.87 us
    all_to_all x1, blocking collectives, shards(): lax.all_to_all(sums, ('order', 'outer', 'inner'), split_axis=0, concat_ax...  9.26 us
    ppermute x5, waiting for transfers between devices, rotate(): return lax.ppermute(x, axis, [(i, (i + shift) % size) for i in range(size)])  8.31 us
    pallas_call x1, Pallas kernels, shards(): call(functools.partial(prepare, geo), (jax.ShapeDtypeStruct((m_local, 2 *...  3.31 us
    ppermute x5, starting transfers between devices, rotate(): return lax.ppermute(x, axis, [(i, (i + shift) % size) for i in range(size)])  3.31 us
    pallas_call x1, Pallas kernels, shards(): call(functools.partial(cut_windows, geo), (cut,) * (outer - 1), [IN_HBM],...  1.67 us
    pallas_call x1, Pallas kernels, shards(): call(functools.partial(update, geo), (coefficients,) * 3, [WHOLE] * (5 +...  1.61 us
  transfers between devices with their start and end apart: 5, of which 3 were waited for; matrix products, arithmetic and copies ran while one was open for 0% of the time, Pallas kernels for 10%

profile of v9, /device:TPU:0, one launch (start us, length us, event | category | flops | bytes accessed | tf_op | source)
XLA Modules:
  0.0 57.1 jit_solution(16647456828826338186)
XLA Ops:
  0.6 0.0 copy-start.5
  0.6 0.0 copy-start
  0.7 0.0 copy-start.8
  0.7 0.0 copy-start.3
  0.7 0.0 copy-start.4
  0.7 0.0 copy-start.6
  0.7 1.7 %shard_map.122 = f32[64,2176]{1,0:T(8,128)S(1)} custom-call(f32[2,64,2160]{2,1,0:T(8,128)} %bitcast.5), custom_call_target="tpu_custom_call" | custom-call | flops 147456 | bytes 2359296 | tf_op jit(solution)/shard_map/pallas_call | solution.py:515
  2.4 3.0 %collective-permute-start.1 = (f32[64,2176]{1,0:T(8,128)S(1)}, f32[64,2176]{1,0:T(8,128)S(1)}, u32[]{:S(2)}, u32[]{:S(2)}) collective-permute-start(f32[64,2176]{1,0:T(8,128)S(1)} %shard_map.122), channel_id=1, source_target_pairs={{0,2},{2,0},{1,3},{3,1},{4,6},{6,4},{5,7},{7,5},{8,10},{10,8},{9,1... | collective-permute-start | bytes 1671176 | tf_op jit(solution)/shard_map/ppermute | solution.py:459
  5.4 0.0 copy-done
  5.4 0.0 collective-permute-start
  5.4 0.0 copy-done.8
  5.4 0.1 copy.13.value_ref
  5.5 0.0 copy-done.5
  5.5 0.0 copy-done.3
  5.5 0.0 copy-done.4
  5.5 1.4 %shard_map.123.table_ref = f32[4,32,8,128]{3,2,1,0:T(8,128)S(1)} custom-call(s32[8,4320]{1,0:T(8,128)S(1)} %copy-done.3, s32[8,4320]{1,0:T(8,128)S(1)} %copy-done.4, f32[16,2]{1,0:T(8,128)S(1)} %copy.13.value_ref, f32[128,128]{1,0:T(8,128)S(1)} %copy-done.5), custom_call_target="tpu_custom_call" | custom-call | flops 1 | bytes 1 | tf_op jit(solution)/shard_map/pallas_call | solution.py:535
  6.9 0.6 %collective-permute-done.refs_1_ = f32[2,2,64,540]{3,2,1,0:T(8,128)S(1)} collective-permute-done((f32[2,2,64,540]{3,2,1,0:T(8,128)S(1)}, f32[2,2,64,540]{3,2,1,0:T(8,128)S(1)}, u32[]{:S(2)}, u32[]{:S(2)}) %collective-permute-start) | collective-permute-done | bytes 552992 | tf_op jit(solution)/shard_map/ppermute | solution.py:459
  7.5 0.0 copy-done.6
  7.5 3.3 %shard_map.121 = (bf16[2,256,1152]{2,1,0:T(8,128)(2,1)S(1)}, f32[2,64,128]{2,1,0:T(8,128)S(1)}, f32[2,8,540]{2,1,0:T(8,128)S(1)}, f32[2,64,640]{2,1,0:T(8,128)S(1)}, f32[2,64,640]{2,1,0:T(8,128)S(1)}) custom-call(s32[16]{0:T(128)S(1)} %copy-done.6, f32[2,64,2160]{2,1,0:T(8,128)} %bitcast.6, f32[2,2,64,540]{3,2,1,0:T(8,128)S(1)} %copy-done, ...), custom_call_target="tpu_custom_call" | custom-call | flops 1 | bytes 1 | tf_op jit(solution)/shard_map/pallas_call | solution.py:546
  10.8 0.2 collective-permute-start.2
  11.0 7.0 %collective-permute-done.1.refs_0_ = f32[64,2176]{1,0:T(8,128)S(1)} collective-permute-done((f32[64,2176]{1,0:T(8,128)S(1)}, f32[64,2176]{1,0:T(8,128)S(1)}, u32[]{:S(2)}, u32[]{:S(2)}) %collective-permute-start.1) | collective-permute-done | bytes 557088 | tf_op jit(solution)/shard_map/ppermute | solution.py:459
  18.0 0.0 copy-start.7
  18.0 0.0 copy-start.1
  18.0 0.5 shard_map.124
  18.6 0.1 collective-permute-start.3
  18.7 15.0 %all_to_all.15.recv_ref = f32[16,2,8,128]{3,2,1,0:T(8,128)S(1)} all-to-all(f32[16,2,8,128]{3,2,1,0:T(8,128)S(1)} %bitcast.3), channel_id=1, replica_groups=mesh['order'=8,'outer'=2,'inner'=2] {'outer','order'}, dimensions={0} | all-to-all | bytes 262144 | tf_op jit(solution)/shard_map/all_to_all | solution.py:576
  33.6 0.0 collective-permute-done.2.refs_1_
  33.6 0.0 collective-permute-done.3.refs_3_
  33.6 0.4 shard_map.125
  34.0 9.9 %all_to_all.16.recv_ref = f32[32,1,8,128]{3,2,1,0:T(8,128)S(1)} all-to-all(f32[32,1,8,128]{3,2,1,0:T(8,128)S(1)} %shard_map.125), channel_id=1, replica_groups=mesh['order'=8,'outer'=2,'inner'=2] {'inner','outer','order'}, dimensions={0} | all-to-all | bytes 262144 | tf_op jit(solution)/shard_map/all_to_all | solution.py:596
  43.9 0.0 collective-permute-start.4
  43.9 0.0 copy-done.7
  43.9 0.0 copy-done.1
  43.9 0.6 %shard_map.126 = (f32[1,2,64,540]{3,2,1,0:T(8,128)S(1)}, f32[256,128]{1,0:T(8,128)S(1)}) custom-call(f32[2,8,540]{2,1,0:T(8,128)S(1)} %get-tuple-element.22.valid_ref, f32[32,1,8,128]{3,2,1,0:T(8,128)S(1)} %all_to_all.16.recv_ref, f32[2,64,640]{2,1,0:T(8,128)S(1)} %get-tuple-element.33.refs_0_, f32[2,64,640]{2,1,0:T(8,128)S(1)} %collective-permute-done.2.refs_1_, ...), custom_call_target="tpu_custom_call" | custom-call | flops 125829120 | bytes 1105920 | tf_op jit(solution)/shard_map/pallas_call | solution.py:609
  44.6 0.7 %collective-permute-done.4.recv_ref = f32[32,1,8,128]{3,2,1,0:T(8,128)S(1)} collective-permute-done((f32[32,1,8,128]{3,2,1,0:T(8,128)S(1)}, f32[32,1,8,128]{3,2,1,0:T(8,128)S(1)}, u32[]{:S(2)}, u32[]{:S(2)}) %collective-permute-start.4) | collective-permute-done | bytes 131104 | tf_op jit(solution)/shard_map/ppermute | solution.py:459
  45.2 0.0 copy-start.2
  45.3 0.9 %shard_map.127 = (f32[1,2,64,540]{3,2,1,0:T(8,128)S(1)}, f32[32,1,256]{2,1,0:T(1,128)S(1)}) custom-call(f32[2,8,540]{2,1,0:T(8,128)S(1)} %get-tuple-element.22.valid_ref, f32[32,1,8,128]{3,2,1,0:T(8,128)S(1)} %collective-permute-done.4.recv_ref, f32[2,64,640]{2,1,0:T(8,128)S(1)} %get-tuple-element.33.refs_0_, ...), custom_call_target="tpu_custom_call" | custom-call | flops 125829120 | bytes 1105920 | tf_op jit(solution)/shard_map/pallas_call | solution.py:609
  46.2 9.3 %all_to_all.17.sums_ref = f32[32,1,256]{2,1,0:T(1,128)S(1)} all-to-all(f32[32,1,256]{2,1,0:T(1,128)S(1)} %get-tuple-element.38), channel_id=1, replica_groups=mesh['order'=8,'outer'=2,'inner'=2] {'order','outer','inner'}, dimensions={0} | all-to-all | bytes 65536 | tf_op jit(solution)/shard_map/all_to_all | solution.py:626
  55.5 0.0 copy-done.2
  55.5 1.6 %shard_map.128 = (f32[2,2,64,540]{3,2,1,0:T(8,128)}, f32[2,2,64,540]{3,2,1,0:T(8,128)}, f32[2,2,64,540]{3,2,1,0:T(8,128)}) custom-call(f32[2,8,540]{2,1,0:T(8,128)S(1)} %get-tuple-element.22.valid_ref, f32[32,1,256]{2,1,0:T(1,128)S(1)} %all_to_all.17.sums_ref, f32[1,2,64,540]{3,2,1,0:T(8,128)S(1)} %get-tuple-element.39.refs_0_, ...), custom_call_target="tpu_custom_call" | custom-call | flops 1382400 | bytes 3870720 | tf_op jit(solution)/shard_map/pallas_call | solution.py:629
  (1 shorter events, 0.0 us)
Async XLA Ops:
  0.6 4.9 %copy-start.5 = (f32[128,128]{1,0:T(8,128)S(1)}, f32[128,128]{1,0:T(8,128)}, u32[]{:S(2)}) copy-start(f32[128,128]{1,0:T(8,128)} %constant.2.clone.basis_ref) | copy-start | bytes 196612
  0.6 4.8 %copy-start = (f32[2,2,64,540]{3,2,1,0:T(8,128)S(1)}, f32[2,2,64,540]{3,2,1,0:T(8,128)}, u32[]{:S(2)}) copy-start(f32[2,2,64,540]{3,2,1,0:T(8,128)} %refs_3_.1) | copy-start | bytes 1658884
  0.7 4.8 %copy-start.8 = (f32[16,2]{0,1:T(2,128)S(1)}, f32[16,2]{0,1:T(2,128)}, u32[]{:S(2)}) copy-start(f32[16,2]{0,1:T(2,128)} %param.17) | copy-start | bytes 388
  0.7 4.8 %copy-start.3 = (s32[8,4320]{1,0:T(8,128)S(1)}, s32[8,4320]{1,0:T(8,128)}, u32[]{:S(2)}) copy-start(s32[8,4320]{1,0:T(8,128)} %class_ref.1) | copy-start | bytes 414724
  0.7 4.8 %copy-start.4 = (s32[8,4320]{1,0:T(8,128)S(1)}, s32[8,4320]{1,0:T(8,128)}, u32[]{:S(2)}) copy-start(s32[8,4320]{1,0:T(8,128)} %land_ref.1) | copy-start | bytes 414724
  0.7 6.8 %copy-start.6 = (s32[16]{0:T(128)S(1)}, s32[16]{0:T(128)}, u32[]{:S(2)}) copy-start(s32[16]{0:T(128)} %order_ref.1) | copy-start | bytes 196
  2.4 15.7 %collective-permute-start.1 = (f32[64,2176]{1,0:T(8,128)S(1)}, f32[64,2176]{1,0:T(8,128)S(1)}, u32[]{:S(2)}, u32[]{:S(2)}) collective-permute-start(f32[64,2176]{1,0:T(8,128)S(1)} %shard_map.122), channel_id=1, source_target_pairs={{0,2},{2,0},{1,3},{3,1},{4,6},{6,4},{5,7},{7,5},{8,10},{10,8},{9,1... | collective-permute-start | bytes 1671176 | tf_op jit(solution)/shard_map/ppermute | solution.py:459
  5.4 2.1 %collective-permute-start = (f32[2,2,64,540]{3,2,1,0:T(8,128)S(1)}, f32[2,2,64,540]{3,2,1,0:T(8,128)S(1)}, u32[]{:S(2)}, u32[]{:S(2)}) collective-permute-start(f32[2,2,64,540]{3,2,1,0:T(8,128)S(1)} %copy-done), channel_id=1, source_target_pairs={{0,1},{1,0},{2,3},{3,2},{4,5},{5,4},{6,7},{7,6},{8,9},{9,8},{10,11... | collective-permute-start | bytes 1658888 | tf_op jit(solution)/shard_map/ppermute | solution.py:459
  10.8 22.8 %collective-permute-start.2 = (f32[2,64,640]{2,1,0:T(8,128)S(1)}, f32[2,64,640]{2,1,0:T(8,128)S(1)}, u32[]{:S(2)}, u32[]{:S(2)}) collective-permute-start(f32[2,64,640]{2,1,0:T(8,128)S(1)} %get-tuple-element.28), channel_id=1, source_target_pairs={{0,1},{1,0},{2,3},{3,2},{4,5},{5,4},{6,7},{7,6},{8,9},{9,8},{10,11... | collective-permute-start | bytes 983048 | tf_op jit(solution)/shard_map/ppermute | solution.py:459
  18.0 25.9 %copy-start.7 = (f32[540]{0:T(1024)S(1)}, f32[540]{0:T(1024)}, u32[]{:S(2)}) copy-start(f32[540]{0:T(1024)} %param.18) | copy-start | bytes 6484
  18.0 25.9 %copy-start.1 = (f32[2,2,64,540]{3,2,1,0:T(8,128)S(1)}, f32[2,2,64,540]{3,2,1,0:T(8,128)}, u32[]{:S(2)}) copy-start(f32[2,2,64,540]{3,2,1,0:T(8,128)} %refs_4_.5) | copy-start | bytes 1658884
  18.6 15.1 %collective-permute-start.3 = (f32[1,2,64,640]{3,2,1,0:T(8,128)S(1)}, f32[1,2,64,640]{3,2,1,0:T(8,128)S(1)}, u32[]{:S(2)}, u32[]{:S(2)}) collective-permute-start(f32[1,2,64,640]{3,2,1,0:T(8,128)S(1)} %get-tuple-element.30), channel_id=1, source_target_pairs={{0,1},{1,0},{2,3},{3,2},{4,5},{5,4},{6,7},{7,6},{8,9},{9,8},{10,11... | collective-permute-start | bytes 983048 | tf_op jit(solution)/shard_map/ppermute | solution.py:459
  43.9 1.3 %collective-permute-start.4 = (f32[32,1,8,128]{3,2,1,0:T(8,128)S(1)}, f32[32,1,8,128]{3,2,1,0:T(8,128)S(1)}, u32[]{:S(2)}, u32[]{:S(2)}) collective-permute-start(f32[32,1,8,128]{3,2,1,0:T(8,128)S(1)} %all_to_all.16.recv_ref), channel_id=1, source_target_pairs={{0,1},{1,0},{2,3},{3,2},{4,5},{5,4},{6,7},{7,6},{8,9},{9,8},{10,11... | collective-permute-start | bytes 393224 | tf_op jit(solution)/shard_map/ppermute | solution.py:459
  45.2 10.2 %copy-start.2 = (f32[2,2,64,540]{3,2,1,0:T(8,128)S(1)}, f32[2,2,64,540]{3,2,1,0:T(8,128)}, u32[]{:S(2)}) copy-start(f32[2,2,64,540]{3,2,1,0:T(8,128)} %refs_2_.1) | copy-start | bytes 1658884
